TPU v7x, 32 devices: a whole 2x2x4 slice. The times are simulated.
32 devices in a mesh: scale: 4 (over z), img: 8 (over y, x, core).
Axes of the slice: x: 2, y: 2, z: 4, core: 2. Of those that a mesh axis runs over, the one named last changes fastest.
Arguments:
- images: bfloat16 [4, 64, 256, 512], P('scale', 'img'), may hold values from -6 to 6
- valid_mask: int32 [64, 256], P('img'), may hold values from 0 to 1, as said below
- scale_cols: int32 [4], replicated, may hold values from 1 to 256, as said below
- boxes: int32 [128], P('img'), may hold values from -1 to 2047, as said below
- normal_targets: float32 [3, 64, 256], P(None, 'img'), may hold values from -6 to 6
- dense_targets: bfloat16 [64, 256, 1792], P('img', None, 'scale'), may hold values from -6 to 6
- affine_scale: float32 [2, 512], replicated, may hold values from 0.5 to 1.5
- affine_shift: float32 [2, 512], replicated, may hold values from -3 to 3
- conv_bf16: bfloat16 [2, 9, 512, 512], replicated, may hold values from -0.09375 to 0.09375
- head_bf16: bfloat16 [7, 512, 256], replicated, may hold values from -0.25 to 0.25
- vectors: float32 [2304], replicated
- vec_m: float32 [2304], replicated
- vec_v: float32 [2304], replicated
- master: float32 [64, 512, 256], P(('scale', 'img')), may hold values from -0.15625 to 0.15625
- slot_m: float32 [64, 512, 256], P(('scale', 'img'))
- slot_v: float32 [64, 512, 256], P(('scale', 'img'))
- basis_left: float32 [64, 512, 512], P(('scale', 'img'))
- basis_right: float32 [64, 256, 256], P(('scale', 'img'))
- owner_slot: int32 [43], replicated, may hold values from 0 to 63, as said below
Outputs:
- loss: float32 [2], replicated
- grad_norm: float32 [], replicated
- vec_new: float32 [2304], replicated
- vec_m_new: float32 [2304], replicated
- vec_v_new: float32 [2304], replicated
- master_new: float32 [64, 512, 256], P(('scale', 'img'))
- slot_m_new: float32 [64, 512, 256], P(('scale', 'img'))
- slot_v_new: float32 [64, 512, 256], P(('scale', 'img'))
- conv_copy: bfloat16 [2, 9, 512, 512], replicated
- head_copy: bfloat16 [7, 512, 256], replicated
Inputs may be any that keep to these rules, and one draw needn't show every extreme that they name: scale_cols[0] = 256; scale s has between 256 / 2^(s+1) (at least 1) and 256 / 2^s valid columns. `boxes`: in each device's 16 box slots the valid entries come first and at least one is valid; some device has all 16 valid; padding is -1. `owner_slot`: distinct slots. `valid_mask`: at least one pixel is valid.
All inputs are finite; a program needn't handle non-finite values.
Results may differ from a plain program's by a relative error of at most 0.00086.
Values may be sent and summed in bfloat16 or wider, within the bound.
No kernel may reach another device: no remote copies, remote signals or barrier semaphores. Data moves between devices by JAX's collectives and lax.ppermute only.
A program may use at most 192 MiB of HBM per device.

v0:
```python
import jax
import jax.numpy as jnp
from jax import lax
from jax.sharding import PartitionSpec as P

STEP = 5


beta_one = 0.5
beta_two = 0.5
adam_eps = 1e-08
rate_matrix = 0.01
rate_vector = 0.2
weight_decay = 0.01
clip_level = 0.001
box_weight = 2.0
norm_eps = 1e-05
highest = lax.Precision.HIGHEST


def extended(cells, sides, width):
    for axis, dim in sides:
        count = lax.axis_size(axis)
        ends = count - 1
        head = lax.slice_in_dim(cells, 0, width, axis=dim)
        tail = lax.slice_in_dim(cells, cells.shape[dim] - width, cells.shape[dim], axis=dim)
        cells = jnp.concatenate(
            [
                lax.ppermute(tail, axis, [(i, (i + 1) % count) for i in range(ends)]),
                cells,
                lax.ppermute(head, axis, [((i + 1) % count, i) for i in range(ends)]),
            ],
            axis=dim,
        )
    return cells


def for_sending(value):

    def short(part):
        return part.astype(jnp.bfloat16) if part.dtype == jnp.float32 else part

    return jax.tree.map(short, value)


def broadcast(value, axis, source):
    kept = jnp.where(lax.axis_index(axis) == source, value, 0).astype(value.dtype)
    return lax.psum(kept, axis)


def column_table(columns, width):
    fine_idx = jnp.arange(width, dtype=jnp.int32)
    numer = jnp.maximum((2 * fine_idx + 1) * columns - width, 0)
    lower = numer // (2 * width)
    frac = (numer % (2 * width)).astype(jnp.float32) / (2.0 * width)
    upper = jnp.minimum(lower + 1, columns - 1)
    coarse = fine_idx[:, None]
    return (1.0 - frac)[None, :] * (coarse == lower[None, :]).astype(jnp.float32) + frac[
        None, :
    ] * (coarse == upper[None, :]).astype(jnp.float32)


def pad_columns(values):
    return jnp.pad(values, ((0, 0), (1, 1), (0, 0)))


def conv_forward(inputs, weights):
    rows, width = (inputs.shape[0], inputs.shape[1])
    padded = pad_columns(extended(inputs, (("img", 0),), 1))
    total = jnp.zeros((rows, width, weights.shape[2]), jnp.float32)
    for tap_idx in range(weights.shape[0]):
        row_off, col_off = (tap_idx // 3, tap_idx % 3)
        window = padded[row_off : row_off + rows, col_off : col_off + width]
        total = total + jnp.einsum(
            "rwc,cd->rwd", window, weights[tap_idx], preferred_element_type=jnp.float32
        )
    return (padded, total)


def conv_backward(padded, grad_pre, weights, need_input):
    rows, width = (grad_pre.shape[0], grad_pre.shape[1])
    kernel_grads = []
    for tap_idx in range(weights.shape[0]):
        row_off, col_off = (tap_idx // 3, tap_idx % 3)
        window = padded[row_off : row_off + rows, col_off : col_off + width]
        kernel_grads.append(
            jnp.einsum("rwc,rwd->cd", window, grad_pre, preferred_element_type=jnp.float32)
        )
    grad_input = None
    if need_input:
        grad_padded = pad_columns(extended(grad_pre, (("img", 0),), 1))
        grad_input = jnp.zeros((rows, width, weights.shape[1]), jnp.float32)
        for tap_idx in range(weights.shape[0]):
            row_off, col_off = (tap_idx // 3, tap_idx % 3)
            window = grad_padded[
                2 - row_off : 2 - row_off + rows, 2 - col_off : 2 - col_off + width
            ]
            grad_input = grad_input + jnp.einsum(
                "rwd,cd->rwc", window, weights[tap_idx], preferred_element_type=jnp.float32
            )
    return (jnp.stack(kernel_grads), grad_input)


def activate(pre, gain, shift, col_mask):
    return jax.nn.gelu(pre * gain + shift) * col_mask


def tap_norm(result, gamma):
    return gamma * result * lax.rsqrt(jnp.mean(result * result, -1, keepdims=True) + norm_eps)


def cosine_terms(predict, targets, mask_f):
    target_last = jnp.moveaxis(targets, 0, -1)
    inner = jnp.sum(predict * target_last, -1)
    cosine = inner * lax.rsqrt(
        (jnp.sum(predict * predict, -1) + 1.0) * (jnp.sum(target_last * target_last, -1) + 1.0)
    )
    return jnp.sum(mask_f * (1.0 - cosine))


def to_blocks(conv_part, head_part):
    depth, taps, chans = (conv_part.shape[0], conv_part.shape[1], conv_part.shape[2])
    half = head_part.shape[2]
    split = (
        conv_part.reshape(depth, taps, chans, 2, half)
        .transpose(0, 1, 3, 2, 4)
        .reshape(depth * taps * 2, chans, half)
    )
    return jnp.concatenate([split, head_part], 0)


def from_blocks(blocks, depth, taps):
    count_conv = depth * taps * 2
    chans, half = (blocks.shape[1], blocks.shape[2])
    conv_part = (
        blocks[:count_conv]
        .reshape(depth, taps, 2, chans, half)
        .transpose(0, 1, 3, 2, 4)
        .reshape(depth, taps, chans, 2 * half)
    )
    return (conv_part, blocks[count_conv:])


def pick_block(blocks, owner_slot, slot_id):
    match = owner_slot == slot_id
    index = jnp.sum(jnp.where(match, jnp.arange(owner_slot.shape[0], dtype=jnp.int32), 0))
    valid = jnp.any(match).astype(jnp.float32)
    return lax.dynamic_index_in_dim(blocks, index, 0, keepdims=False) * valid


def soap_update(master, moment, second, left, right, grads):
    turned = jnp.einsum("sij,sik->sjk", left, grads, precision=highest)
    turned = jnp.einsum("sjk,skl->sjl", turned, right, precision=highest)
    moment = beta_one * moment + (1.0 - beta_one) * turned
    second = beta_two * second + (1.0 - beta_two) * turned * turned
    ratio = moment / (1.0 - beta_one**STEP) / (jnp.sqrt(second / (1.0 - beta_two**STEP)) + adam_eps)
    back = jnp.einsum("sij,sjk->sik", left, ratio, precision=highest)
    back = jnp.einsum("sik,slk->sil", back, right, precision=highest)
    return (master - rate_matrix * (back + weight_decay * master), moment, second)


def vector_update(params, moment, second, grads):
    moment = beta_one * moment + (1.0 - beta_one) * grads
    second = beta_two * second + (1.0 - beta_two) * grads * grads
    ratio = moment / (1.0 - beta_one**STEP) / (jnp.sqrt(second / (1.0 - beta_two**STEP)) + adam_eps)
    return (params - rate_vector * (ratio + weight_decay * params), moment, second)


def local(
    images,
    valid_mask,
    scale_cols,
    boxes,
    normal_targets,
    dense_targets,
    affine_scale,
    affine_shift,
    conv_bf16,
    head_bf16,
    vectors,
    vec_m,
    vec_v,
    master,
    slot_m,
    slot_v,
    basis_left,
    basis_right,
    owner_slot,
):
    rows, width, chans = (images.shape[1], images.shape[2], images.shape[3])
    heads_count, head_width = (head_bf16.shape[0], head_bf16.shape[2])
    wide = heads_count * head_width
    depth, taps = (conv_bf16.shape[0], conv_bf16.shape[1])
    scale_idx = lax.axis_index("scale")
    columns = lax.dynamic_index_in_dim(scale_cols, scale_idx, 0, keepdims=False)
    col_mask = (jnp.arange(width, dtype=jnp.int32) < columns).astype(jnp.float32)[None, :, None]
    current = images[0] * col_mask.astype(jnp.bfloat16)
    kept = []
    result = None
    for depth_idx in range(depth):
        padded, pre = conv_forward(current, conv_bf16[depth_idx])
        result = activate(pre, affine_scale[depth_idx], affine_shift[depth_idx], col_mask)
        kept.append((padded, pre))
        current = result.astype(jnp.bfloat16)
    gamma = vectors[:chans]
    bias = vectors[chans:]
    tapped, tap_pull = jax.vjp(tap_norm, result, gamma)
    tapped_low = tapped.astype(jnp.bfloat16)
    heads_out = (
        jnp.einsum(
            "rwc,tcd->rwtd", tapped_low, head_bf16, preferred_element_type=jnp.float32
        ).reshape(rows, width, wide)
        + bias
    )
    table = column_table(columns, width)
    raised = jnp.einsum("ij,rik->rjk", table, heads_out, precision=highest)
    joined = lax.psum_scatter(
        raised.astype(jnp.bfloat16), "scale", scatter_dimension=2, tiled=True
    ).astype(jnp.float32)
    mask_f = valid_mask.astype(jnp.float32)
    count = lax.psum(jnp.sum(mask_f), "img")
    pixels = jnp.arange(rows * width, dtype=jnp.int32)
    hits = jnp.sum((boxes[:, None] == pixels[None, :]).astype(jnp.float32), 0).reshape(rows, width)
    weight = mask_f + box_weight * hits
    target = dense_targets.astype(jnp.float32)
    is_first = (scale_idx == 0).astype(jnp.float32)

    def local_loss(joined_part):
        dense = 0.5 * jnp.sum(weight[:, :, None] * (joined_part - target) ** 2)
        normal = is_first * cosine_terms(joined_part[:, :, 0:3], normal_targets, mask_f)
        return ((dense / wide + normal) / count, jnp.stack([dense, normal]))

    loss_local, loss_pull, parts = jax.vjp(local_loss, joined, has_aux=True)
    (grad_joined,) = loss_pull(jnp.ones_like(loss_local))
    grad_full = jax.tree.map(
        lambda part, own: part.astype(own.dtype),
        lax.all_gather(for_sending(grad_joined), "scale", axis=2, tiled=True),
        grad_joined,
    )
    grad_heads = jnp.einsum("ij,rjk->rik", table, grad_full, precision=highest)
    grad_bias = jnp.sum(grad_heads, (0, 1))
    grad_low = grad_heads.astype(jnp.bfloat16).reshape(rows, width, heads_count, head_width)
    grad_head_w = jnp.einsum(
        "rwc,rwtd->tcd", tapped_low, grad_low, preferred_element_type=jnp.float32
    )
    grad_tapped = jnp.einsum(
        "rwtd,tcd->rwc", grad_low, head_bf16, preferred_element_type=jnp.float32
    )
    grad_result, grad_gamma = tap_pull(grad_tapped)
    conv_grads = [None] * depth
    for depth_idx in reversed(range(depth)):
        padded, pre = kept[depth_idx]
        _, act_pull = jax.vjp(
            lambda value: activate(
                value, affine_scale[depth_idx], affine_shift[depth_idx], col_mask
            ),
            pre,
        )
        (grad_pre,) = act_pull(grad_result)
        kernel_grads, grad_result = conv_backward(
            padded, grad_pre.astype(jnp.bfloat16), conv_bf16[depth_idx], depth_idx > 0
        )
        conv_grads[depth_idx] = kernel_grads
    grad_conv = jnp.stack(conv_grads)
    grad_vec = jnp.concatenate([grad_gamma, grad_bias])
    device = lax.axis_index(("scale", "img"))
    per_device = master.shape[0]
    grad_conv, grad_head_w, grad_vec, totals = lax.psum(
        (grad_conv, grad_head_w, grad_vec, parts), ("scale", "img")
    )
    blocks = to_blocks(grad_conv, grad_head_w)
    squares = (
        jnp.sum(grad_conv * grad_conv)
        + jnp.sum(grad_head_w * grad_head_w)
        + jnp.sum(grad_vec * grad_vec)
    )
    owned = jnp.stack(
        [
            pick_block(blocks, owner_slot, device * per_device + slot_idx)
            for slot_idx in range(per_device)
        ]
    )
    grad_norm = jnp.sqrt(squares)
    factor = clip_level / jnp.maximum(grad_norm, clip_level)
    vec_new, vec_m_new, vec_v_new = vector_update(vectors, vec_m, vec_v, grad_vec * factor)
    master_new, slot_m_new, slot_v_new = soap_update(
        master, slot_m, slot_v, basis_left, basis_right, owned * factor
    )
    fresh = master_new.astype(jnp.bfloat16)

    def send_block(block_idx, store):
        slot_id = owner_slot[block_idx]
        piece = lax.dynamic_index_in_dim(fresh, slot_id % per_device, 0, keepdims=False)
        arrived_block = broadcast(piece, ("scale", "img"), slot_id // per_device)
        return lax.dynamic_update_index_in_dim(store, arrived_block, block_idx, 0)

    store = jnp.zeros((owner_slot.shape[0], chans, head_width), jnp.bfloat16)
    store = lax.fori_loop(0, owner_slot.shape[0], send_block, store)
    conv_copy, head_copy = from_blocks(store, depth, taps)
    loss = jnp.stack([totals[0] / wide + totals[1], count])
    return (
        loss,
        grad_norm,
        vec_new,
        vec_m_new,
        vec_v_new,
        master_new,
        slot_m_new,
        slot_v_new,
        conv_copy,
        head_copy,
    )


def solution(mesh):
    in_specs = (
        P("scale", "img", None, None),
        P("img", None),
        P(),
        P("img"),
        P(None, "img", None),
        P("img", None, "scale"),
        P(),
        P(),
        P(),
        P(),
        P(),
        P(),
        P(),
        P(("scale", "img"), None, None),
        P(("scale", "img"), None, None),
        P(("scale", "img"), None, None),
        P(("scale", "img"), None, None),
        P(("scale", "img"), None, None),
        P(),
    )
    out_specs = (
        P(),
        P(),
        P(),
        P(),
        P(),
        P(("scale", "img"), None, None),
        P(("scale", "img"), None, None),
        P(("scale", "img"), None, None),
        P(),
        P(),
    )
    return jax.shard_map(local, mesh=mesh, in_specs=in_specs, out_specs=out_specs, check_vma=False)
```

profile of v0, /device:TPU:0, one launch (start us, length us, event | category | flops | bytes accessed | tf_op | source)
XLA Modules:
  0.0 6736.2 jit_solution(15124246009013567468)
XLA Ops:
  174.2 132.8 %reduce-scatter.2.cloned.1.call-done = bf16[8,256,448]{1,2,0:T(8,128)(2,1)} async-done(((bf16[8,256,1792]{1,2,0:T(8,128)(2,1)}), bf16[8,256,448]{1,2,0:T(8,128)(2,1)}) %reduce-scatter.2.cloned.1.call-update) | async-done | bytes 1835024 | tf_op jit(solution)/shard_map/reduce_scatter | solution.py:217
  332.1 131.3 %all-gather.2.cloned.1.call-done = bf16[8,256,1792]{1,2,0:T(8,128)(2,1)} async-done(((bf16[8,256,448]{1,2,0:T(8,128)(2,1)}), bf16[8,256,1792]{1,2,0:T(8,128)(2,1)}) %all-gather.2.cloned.1.call-update) | async-done | bytes 7340048 | tf_op jit(solution)/shard_map/all_gather | solution.py:237
  584.4 41.2 all-reduce.4
  629.3 308.9 %all-reduce.9.cloned.1.call-done = (f32[2,9,512,512]{3,2,1,0:T(8,128)}, f32[7,512,256]{1,2,0:T(8,128)}) async-done(((f32[2,9,512,512]{3,2,1,0:T(8,128)}, f32[7,512,256]{1,2,0:T(8,128)}), (f32[2,9,512,512]{3,2,1,0:T(8,128)}, f32[7,512,256]{1,2,0:T(8,128)})) %all-reduce.9.cloned.1.call-update) | async-done | bytes 22544400 | tf_op jit(solution)/shard_map/psum | solution.py:268
  985.8 5696.5 %while.15 = (s32[]{:T(128)}, bf16[43,512,256]{2,1,0:T(8,128)(2,1)}, s32[43]{0:T(128)S(1)}, bf16[2,512,256]{2,1,0:T(8,128)(2,1)S(1)}, s32[]{:T(128)}, /*index=5*/...) while((s32[]{:T(128)}, bf16[43,512,256]{2,1,0:T(8,128)(2,1)}, ...), condition=%wide.region_26.27_spmd, body=%wide.region_24.26_spmd.sunk | while | flops 262176 | bytes 2621924 | solution.py:298
  990.1 126.0 %all-reduce.11.cloned.1.call-done = bf16[1,512,256]{2,1,0:T(8,128)(2,1)} async-done(((bf16[1,512,256]{2,1,0:T(8,128)(2,1)}), bf16[1,512,256]{2,1,0:T(8,128)(2,1)}) %all-reduce.11.cloned.1.call-update) | async-done | bytes 262160 | tf_op jit(solution)/shard_map/while/body/eval_jaxpr/psum | solution.py:48
  1121.7 126.7 %all-reduce.11.cloned.1.call-done = bf16[1,512,256]{2,1,0:T(8,128)(2,1)} async-done(((bf16[1,512,256]{2,1,0:T(8,128)(2,1)}), bf16[1,512,256]{2,1,0:T(8,128)(2,1)}) %all-reduce.11.cloned.1.call-update) | async-done | bytes 262160 | tf_op jit(solution)/shard_map/while/body/eval_jaxpr/psum | solution.py:48
  1254.0 126.7 %all-reduce.11.cloned.1.call-done = bf16[1,512,256]{2,1,0:T(8,128)(2,1)} async-done(((bf16[1,512,256]{2,1,0:T(8,128)(2,1)}), bf16[1,512,256]{2,1,0:T(8,128)(2,1)}) %all-reduce.11.cloned.1.call-update) | async-done | bytes 262160 | tf_op jit(solution)/shard_map/while/body/eval_jaxpr/psum | solution.py:48
  1386.4 127.0 %all-reduce.11.cloned.1.call-done = bf16[1,512,256]{2,1,0:T(8,128)(2,1)} async-done(((bf16[1,512,256]{2,1,0:T(8,128)(2,1)}), bf16[1,512,256]{2,1,0:T(8,128)(2,1)}) %all-reduce.11.cloned.1.call-update) | async-done | bytes 262160 | tf_op jit(solution)/shard_map/while/body/eval_jaxpr/psum | solution.py:48
  1519.0 127.0 %all-reduce.11.cloned.1.call-done = bf16[1,512,256]{2,1,0:T(8,128)(2,1)} async-done(((bf16[1,512,256]{2,1,0:T(8,128)(2,1)}), bf16[1,512,256]{2,1,0:T(8,128)(2,1)}) %all-reduce.11.cloned.1.call-update) | async-done | bytes 262160 | tf_op jit(solution)/shard_map/while/body/eval_jaxpr/psum | solution.py:48
  1651.7 127.0 %all-reduce.11.cloned.1.call-done = bf16[1,512,256]{2,1,0:T(8,128)(2,1)} async-done(((bf16[1,512,256]{2,1,0:T(8,128)(2,1)}), bf16[1,512,256]{2,1,0:T(8,128)(2,1)}) %all-reduce.11.cloned.1.call-update) | async-done | bytes 262160 | tf_op jit(solution)/shard_map/while/body/eval_jaxpr/psum | solution.py:48
  1784.3 126.7 %all-reduce.11.cloned.1.call-done = bf16[1,512,256]{2,1,0:T(8,128)(2,1)} async-done(((bf16[1,512,256]{2,1,0:T(8,128)(2,1)}), bf16[1,512,256]{2,1,0:T(8,128)(2,1)}) %all-reduce.11.cloned.1.call-update) | async-done | bytes 262160 | tf_op jit(solution)/shard_map/while/body/eval_jaxpr/psum | solution.py:48
  1916.6 127.0 %all-reduce.11.cloned.1.call-done = bf16[1,512,256]{2,1,0:T(8,128)(2,1)} async-done(((bf16[1,512,256]{2,1,0:T(8,128)(2,1)}), bf16[1,512,256]{2,1,0:T(8,128)(2,1)}) %all-reduce.11.cloned.1.call-update) | async-done | bytes 262160 | tf_op jit(solution)/shard_map/while/body/eval_jaxpr/psum | solution.py:48
  2049.3 126.7 %all-reduce.11.cloned.1.call-done = bf16[1,512,256]{2,1,0:T(8,128)(2,1)} async-done(((bf16[1,512,256]{2,1,0:T(8,128)(2,1)}), bf16[1,512,256]{2,1,0:T(8,128)(2,1)}) %all-reduce.11.cloned.1.call-update) | async-done | bytes 262160 | tf_op jit(solution)/shard_map/while/body/eval_jaxpr/psum | solution.py:48
  2181.6 127.0 %all-reduce.11.cloned.1.call-done = bf16[1,512,256]{2,1,0:T(8,128)(2,1)} async-done(((bf16[1,512,256]{2,1,0:T(8,128)(2,1)}), bf16[1,512,256]{2,1,0:T(8,128)(2,1)}) %all-reduce.11.cloned.1.call-update) | async-done | bytes 262160 | tf_op jit(solution)/shard_map/while/body/eval_jaxpr/psum | solution.py:48
  2314.3 126.7 %all-reduce.11.cloned.1.call-done = bf16[1,512,256]{2,1,0:T(8,128)(2,1)} async-done(((bf16[1,512,256]{2,1,0:T(8,128)(2,1)}), bf16[1,512,256]{2,1,0:T(8,128)(2,1)}) %all-reduce.11.cloned.1.call-update) | async-done | bytes 262160 | tf_op jit(solution)/shard_map/while/body/eval_jaxpr/psum | solution.py:48
  2446.6 126.7 %all-reduce.11.cloned.1.call-done = bf16[1,512,256]{2,1,0:T(8,128)(2,1)} async-done(((bf16[1,512,256]{2,1,0:T(8,128)(2,1)}), bf16[1,512,256]{2,1,0:T(8,128)(2,1)}) %all-reduce.11.cloned.1.call-update) | async-done | bytes 262160 | tf_op jit(solution)/shard_map/while/body/eval_jaxpr/psum | solution.py:48
  2578.9 126.7 %all-reduce.11.cloned.1.call-done = bf16[1,512,256]{2,1,0:T(8,128)(2,1)} async-done(((bf16[1,512,256]{2,1,0:T(8,128)(2,1)}), bf16[1,512,256]{2,1,0:T(8,128)(2,1)}) %all-reduce.11.cloned.1.call-update) | async-done | bytes 262160 | tf_op jit(solution)/shard_map/while/body/eval_jaxpr/psum | solution.py:48
  2711.3 126.7 %all-reduce.11.cloned.1.call-done = bf16[1,512,256]{2,1,0:T(8,128)(2,1)} async-done(((bf16[1,512,256]{2,1,0:T(8,128)(2,1)}), bf16[1,512,256]{2,1,0:T(8,128)(2,1)}) %all-reduce.11.cloned.1.call-update) | async-done | bytes 262160 | tf_op jit(solution)/shard_map/while/body/eval_jaxpr/psum | solution.py:48
  2843.6 126.7 %all-reduce.11.cloned.1.call-done = bf16[1,512,256]{2,1,0:T(8,128)(2,1)} async-done(((bf16[1,512,256]{2,1,0:T(8,128)(2,1)}), bf16[1,512,256]{2,1,0:T(8,128)(2,1)}) %all-reduce.11.cloned.1.call-update) | async-done | bytes 262160 | tf_op jit(solution)/shard_map/while/body/eval_jaxpr/psum | solution.py:48
  2975.9 127.0 %all-reduce.11.cloned.1.call-done = bf16[1,512,256]{2,1,0:T(8,128)(2,1)} async-done(((bf16[1,512,256]{2,1,0:T(8,128)(2,1)}), bf16[1,512,256]{2,1,0:T(8,128)(2,1)}) %all-reduce.11.cloned.1.call-update) | async-done | bytes 262160 | tf_op jit(solution)/shard_map/while/body/eval_jaxpr/psum | solution.py:48
  3108.6 126.7 %all-reduce.11.cloned.1.call-done = bf16[1,512,256]{2,1,0:T(8,128)(2,1)} async-done(((bf16[1,512,256]{2,1,0:T(8,128)(2,1)}), bf16[1,512,256]{2,1,0:T(8,128)(2,1)}) %all-reduce.11.cloned.1.call-update) | async-done | bytes 262160 | tf_op jit(solution)/shard_map/while/body/eval_jaxpr/psum | solution.py:48
  3240.9 127.0 %all-reduce.11.cloned.1.call-done = bf16[1,512,256]{2,1,0:T(8,128)(2,1)} async-done(((bf16[1,512,256]{2,1,0:T(8,128)(2,1)}), bf16[1,512,256]{2,1,0:T(8,128)(2,1)}) %all-reduce.11.cloned.1.call-update) | async-done | bytes 262160 | tf_op jit(solution)/shard_map/while/body/eval_jaxpr/psum | solution.py:48
  3373.5 127.0 %all-reduce.11.cloned.1.call-done = bf16[1,512,256]{2,1,0:T(8,128)(2,1)} async-done(((bf16[1,512,256]{2,1,0:T(8,128)(2,1)}), bf16[1,512,256]{2,1,0:T(8,128)(2,1)}) %all-reduce.11.cloned.1.call-update) | async-done | bytes 262160 | tf_op jit(solution)/shard_map/while/body/eval_jaxpr/psum | solution.py:48
  3506.2 127.0 %all-reduce.11.cloned.1.call-done = bf16[1,512,256]{2,1,0:T(8,128)(2,1)} async-done(((bf16[1,512,256]{2,1,0:T(8,128)(2,1)}), bf16[1,512,256]{2,1,0:T(8,128)(2,1)}) %all-reduce.11.cloned.1.call-update) | async-done | bytes 262160 | tf_op jit(solution)/shard_map/while/body/eval_jaxpr/psum | solution.py:48
  3638.8 126.7 %all-reduce.11.cloned.1.call-done = bf16[1,512,256]{2,1,0:T(8,128)(2,1)} async-done(((bf16[1,512,256]{2,1,0:T(8,128)(2,1)}), bf16[1,512,256]{2,1,0:T(8,128)(2,1)}) %all-reduce.11.cloned.1.call-update) | async-done | bytes 262160 | tf_op jit(solution)/shard_map/while/body/eval_jaxpr/psum | solution.py:48
  3771.2 127.0 %all-reduce.11.cloned.1.call-done = bf16[1,512,256]{2,1,0:T(8,128)(2,1)} async-done(((bf16[1,512,256]{2,1,0:T(8,128)(2,1)}), bf16[1,512,256]{2,1,0:T(8,128)(2,1)}) %all-reduce.11.cloned.1.call-update) | async-done | bytes 262160 | tf_op jit(solution)/shard_map/while/body/eval_jaxpr/psum | solution.py:48
  3903.8 126.7 %all-reduce.11.cloned.1.call-done = bf16[1,512,256]{2,1,0:T(8,128)(2,1)} async-done(((bf16[1,512,256]{2,1,0:T(8,128)(2,1)}), bf16[1,512,256]{2,1,0:T(8,128)(2,1)}) %all-reduce.11.cloned.1.call-update) | async-done | bytes 262160 | tf_op jit(solution)/shard_map/while/body/eval_jaxpr/psum | solution.py:48
  4036.2 126.7 %all-reduce.11.cloned.1.call-done = bf16[1,512,256]{2,1,0:T(8,128)(2,1)} async-done(((bf16[1,512,256]{2,1,0:T(8,128)(2,1)}), bf16[1,512,256]{2,1,0:T(8,128)(2,1)}) %all-reduce.11.cloned.1.call-update) | async-done | bytes 262160 | tf_op jit(solution)/shard_map/while/body/eval_jaxpr/psum | solution.py:48
  4168.5 127.0 %all-reduce.11.cloned.1.call-done = bf16[1,512,256]{2,1,0:T(8,128)(2,1)} async-done(((bf16[1,512,256]{2,1,0:T(8,128)(2,1)}), bf16[1,512,256]{2,1,0:T(8,128)(2,1)}) %all-reduce.11.cloned.1.call-update) | async-done | bytes 262160 | tf_op jit(solution)/shard_map/while/body/eval_jaxpr/psum | solution.py:48
  4301.1 127.0 %all-reduce.11.cloned.1.call-done = bf16[1,512,256]{2,1,0:T(8,128)(2,1)} async-done(((bf16[1,512,256]{2,1,0:T(8,128)(2,1)}), bf16[1,512,256]{2,1,0:T(8,128)(2,1)}) %all-reduce.11.cloned.1.call-update) | async-done | bytes 262160 | tf_op jit(solution)/shard_map/while/body/eval_jaxpr/psum | solution.py:48
  4433.8 126.7 %all-reduce.11.cloned.1.call-done = bf16[1,512,256]{2,1,0:T(8,128)(2,1)} async-done(((bf16[1,512,256]{2,1,0:T(8,128)(2,1)}), bf16[1,512,256]{2,1,0:T(8,128)(2,1)}) %all-reduce.11.cloned.1.call-update) | async-done | bytes 262160 | tf_op jit(solution)/shard_map/while/body/eval_jaxpr/psum | solution.py:48
  4566.1 127.0 %all-reduce.11.cloned.1.call-done = bf16[1,512,256]{2,1,0:T(8,128)(2,1)} async-done(((bf16[1,512,256]{2,1,0:T(8,128)(2,1)}), bf16[1,512,256]{2,1,0:T(8,128)(2,1)}) %all-reduce.11.cloned.1.call-update) | async-done | bytes 262160 | tf_op jit(solution)/shard_map/while/body/eval_jaxpr/psum | solution.py:48
  4698.8 127.0 %all-reduce.11.cloned.1.call-done = bf16[1,512,256]{2,1,0:T(8,128)(2,1)} async-done(((bf16[1,512,256]{2,1,0:T(8,128)(2,1)}), bf16[1,512,256]{2,1,0:T(8,128)(2,1)}) %all-reduce.11.cloned.1.call-update) | async-done | bytes 262160 | tf_op jit(solution)/shard_map/while/body/eval_jaxpr/psum | solution.py:48
  4831.4 126.7 %all-reduce.11.cloned.1.call-done = bf16[1,512,256]{2,1,0:T(8,128)(2,1)} async-done(((bf16[1,512,256]{2,1,0:T(8,128)(2,1)}), bf16[1,512,256]{2,1,0:T(8,128)(2,1)}) %all-reduce.11.cloned.1.call-update) | async-done | bytes 262160 | tf_op jit(solution)/shard_map/while/body/eval_jaxpr/psum | solution.py:48
  4963.7 127.0 %all-reduce.11.cloned.1.call-done = bf16[1,512,256]{2,1,0:T(8,128)(2,1)} async-done(((bf16[1,512,256]{2,1,0:T(8,128)(2,1)}), bf16[1,512,256]{2,1,0:T(8,128)(2,1)}) %all-reduce.11.cloned.1.call-update) | async-done | bytes 262160 | tf_op jit(solution)/shard_map/while/body/eval_jaxpr/psum | solution.py:48
  5096.4 127.0 %all-reduce.11.cloned.1.call-done = bf16[1,512,256]{2,1,0:T(8,128)(2,1)} async-done(((bf16[1,512,256]{2,1,0:T(8,128)(2,1)}), bf16[1,512,256]{2,1,0:T(8,128)(2,1)}) %all-reduce.11.cloned.1.call-update) | async-done | bytes 262160 | tf_op jit(solution)/shard_map/while/body/eval_jaxpr/psum | solution.py:48
  5229.0 126.7 %all-reduce.11.cloned.1.call-done = bf16[1,512,256]{2,1,0:T(8,128)(2,1)} async-done(((bf16[1,512,256]{2,1,0:T(8,128)(2,1)}), bf16[1,512,256]{2,1,0:T(8,128)(2,1)}) %all-reduce.11.cloned.1.call-update) | async-done | bytes 262160 | tf_op jit(solution)/shard_map/while/body/eval_jaxpr/psum | solution.py:48
  5361.3 126.7 %all-reduce.11.cloned.1.call-done = bf16[1,512,256]{2,1,0:T(8,128)(2,1)} async-done(((bf16[1,512,256]{2,1,0:T(8,128)(2,1)}), bf16[1,512,256]{2,1,0:T(8,128)(2,1)}) %all-reduce.11.cloned.1.call-update) | async-done | bytes 262160 | tf_op jit(solution)/shard_map/while/body/eval_jaxpr/psum | solution.py:48
  5493.6 127.0 %all-reduce.11.cloned.1.call-done = bf16[1,512,256]{2,1,0:T(8,128)(2,1)} async-done(((bf16[1,512,256]{2,1,0:T(8,128)(2,1)}), bf16[1,512,256]{2,1,0:T(8,128)(2,1)}) %all-reduce.11.cloned.1.call-update) | async-done | bytes 262160 | tf_op jit(solution)/shard_map/while/body/eval_jaxpr/psum | solution.py:48
  5626.3 126.7 %all-reduce.11.cloned.1.call-done = bf16[1,512,256]{2,1,0:T(8,128)(2,1)} async-done(((bf16[1,512,256]{2,1,0:T(8,128)(2,1)}), bf16[1,512,256]{2,1,0:T(8,128)(2,1)}) %all-reduce.11.cloned.1.call-update) | async-done | bytes 262160 | tf_op jit(solution)/shard_map/while/body/eval_jaxpr/psum | solution.py:48
  5758.6 127.0 %all-reduce.11.cloned.1.call-done = bf16[1,512,256]{2,1,0:T(8,128)(2,1)} async-done(((bf16[1,512,256]{2,1,0:T(8,128)(2,1)}), bf16[1,512,256]{2,1,0:T(8,128)(2,1)}) %all-reduce.11.cloned.1.call-update) | async-done | bytes 262160 | tf_op jit(solution)/shard_map/while/body/eval_jaxpr/psum | solution.py:48
  5891.3 127.0 %all-reduce.11.cloned.1.call-done = bf16[1,512,256]{2,1,0:T(8,128)(2,1)} async-done(((bf16[1,512,256]{2,1,0:T(8,128)(2,1)}), bf16[1,512,256]{2,1,0:T(8,128)(2,1)}) %all-reduce.11.cloned.1.call-update) | async-done | bytes 262160 | tf_op jit(solution)/shard_map/while/body/eval_jaxpr/psum | solution.py:48
  6023.9 127.0 %all-reduce.11.cloned.1.call-done = bf16[1,512,256]{2,1,0:T(8,128)(2,1)} async-done(((bf16[1,512,256]{2,1,0:T(8,128)(2,1)}), bf16[1,512,256]{2,1,0:T(8,128)(2,1)}) %all-reduce.11.cloned.1.call-update) | async-done | bytes 262160 | tf_op jit(solution)/shard_map/while/body/eval_jaxpr/psum | solution.py:48
  6156.6 126.7 %all-reduce.11.cloned.1.call-done = bf16[1,512,256]{2,1,0:T(8,128)(2,1)} async-done(((bf16[1,512,256]{2,1,0:T(8,128)(2,1)}), bf16[1,512,256]{2,1,0:T(8,128)(2,1)}) %all-reduce.11.cloned.1.call-update) | async-done | bytes 262160 | tf_op jit(solution)/shard_map/while/body/eval_jaxpr/psum | solution.py:48
  6288.9 127.0 %all-reduce.11.cloned.1.call-done = bf16[1,512,256]{2,1,0:T(8,128)(2,1)} async-done(((bf16[1,512,256]{2,1,0:T(8,128)(2,1)}), bf16[1,512,256]{2,1,0:T(8,128)(2,1)}) %all-reduce.11.cloned.1.call-update) | async-done | bytes 262160 | tf_op jit(solution)/shard_map/while/body/eval_jaxpr/psum | solution.py:48
  6421.6 126.7 %all-reduce.11.cloned.1.call-done = bf16[1,512,256]{2,1,0:T(8,128)(2,1)} async-done(((bf16[1,512,256]{2,1,0:T(8,128)(2,1)}), bf16[1,512,256]{2,1,0:T(8,128)(2,1)}) %all-reduce.11.cloned.1.call-update) | async-done | bytes 262160 | tf_op jit(solution)/shard_map/while/body/eval_jaxpr/psum | solution.py:48
  6553.9 126.7 %all-reduce.11.cloned.1.call-done = bf16[1,512,256]{2,1,0:T(8,128)(2,1)} async-done(((bf16[1,512,256]{2,1,0:T(8,128)(2,1)}), bf16[1,512,256]{2,1,0:T(8,128)(2,1)}) %all-reduce.11.cloned.1.call-update) | async-done | bytes 262160 | tf_op jit(solution)/shard_map/while/body/eval_jaxpr/psum | solution.py:48
  (414 shorter events, 527.1 us)
Async XLA Ops:
  7.2 299.8 %reduce-scatter.2.cloned.1.call-start = ((), (), s32[]{:S(2)}) async-start(), calls=%async_computation.1 | async-start | bytes 9175040 | tf_op jit(solution)/shard_map/reduce_scatter | solution.py:217
  173.5 289.9 %all-gather.2.cloned.1.call-start = ((), (), s32[]{:S(2)}) async-start(), calls=%async_computation.2 | async-start | bytes 9175040 | tf_op jit(solution)/shard_map/all_gather | solution.py:237
  332.0 606.2 %all-reduce.9.cloned.1.call-start = ((), (), s32[]{:S(2)}) async-start(), calls=%async_computation.3 | async-start | bytes 45088768 | tf_op jit(solution)/shard_map/psum | solution.py:268
  490.9 19.6 collective-permute-start.5
  492.2 18.3 collective-permute-start.4
  986.1 130.0 %all-reduce.11.cloned.1.call-start = ((), (), s32[]{:S(2)}) async-start(), calls=%async_computation.4 | async-start | bytes 524288 | tf_op jit(solution)/shard_map/while/body/eval_jaxpr/psum | solution.py:48
  1117.7 130.6 %all-reduce.11.cloned.1.call-start = ((), (), s32[]{:S(2)}) async-start(), calls=%async_computation.4 | async-start | bytes 524288 | tf_op jit(solution)/shard_map/while/body/eval_jaxpr/psum | solution.py:48
  1250.1 130.7 %all-reduce.11.cloned.1.call-start = ((), (), s32[]{:S(2)}) async-start(), calls=%async_computation.4 | async-start | bytes 524288 | tf_op jit(solution)/shard_map/while/body/eval_jaxpr/psum | solution.py:48
  1382.4 131.0 %all-reduce.11.cloned.1.call-start = ((), (), s32[]{:S(2)}) async-start(), calls=%async_computation.4 | async-start | bytes 524288 | tf_op jit(solution)/shard_map/while/body/eval_jaxpr/psum | solution.py:48
  1515.1 131.0 %all-reduce.11.cloned.1.call-start = ((), (), s32[]{:S(2)}) async-start(), calls=%async_computation.4 | async-start | bytes 524288 | tf_op jit(solution)/shard_map/while/body/eval_jaxpr/psum | solution.py:48
  1647.7 131.0 %all-reduce.11.cloned.1.call-start = ((), (), s32[]{:S(2)}) async-start(), calls=%async_computation.4 | async-start | bytes 524288 | tf_op jit(solution)/shard_map/while/body/eval_jaxpr/psum | solution.py:48
  1780.3 130.6 %all-reduce.11.cloned.1.call-start = ((), (), s32[]{:S(2)}) async-start(), calls=%async_computation.4 | async-start | bytes 524288 | tf_op jit(solution)/shard_map/while/body/eval_jaxpr/psum | solution.py:48
  1912.6 131.0 %all-reduce.11.cloned.1.call-start = ((), (), s32[]{:S(2)}) async-start(), calls=%async_computation.4 | async-start | bytes 524288 | tf_op jit(solution)/shard_map/while/body/eval_jaxpr/psum | solution.py:48
  2045.3 130.7 %all-reduce.11.cloned.1.call-start = ((), (), s32[]{:S(2)}) async-start(), calls=%async_computation.4 | async-start | bytes 524288 | tf_op jit(solution)/shard_map/while/body/eval_jaxpr/psum | solution.py:48
  2177.7 131.0 %all-reduce.11.cloned.1.call-start = ((), (), s32[]{:S(2)}) async-start(), calls=%async_computation.4 | async-start | bytes 524288 | tf_op jit(solution)/shard_map/while/body/eval_jaxpr/psum | solution.py:48
  2310.3 130.7 %all-reduce.11.cloned.1.call-start = ((), (), s32[]{:S(2)}) async-start(), calls=%async_computation.4 | async-start | bytes 524288 | tf_op jit(solution)/shard_map/while/body/eval_jaxpr/psum | solution.py:48
  2442.7 130.6 %all-reduce.11.cloned.1.call-start = ((), (), s32[]{:S(2)}) async-start(), calls=%async_computation.4 | async-start | bytes 524288 | tf_op jit(solution)/shard_map/while/body/eval_jaxpr/psum | solution.py:48
  2575.0 130.7 %all-reduce.11.cloned.1.call-start = ((), (), s32[]{:S(2)}) async-start(), calls=%async_computation.4 | async-start | bytes 524288 | tf_op jit(solution)/shard_map/while/body/eval_jaxpr/psum | solution.py:48
  2707.3 130.6 %all-reduce.11.cloned.1.call-start = ((), (), s32[]{:S(2)}) async-start(), calls=%async_computation.4 | async-start | bytes 524288 | tf_op jit(solution)/shard_map/while/body/eval_jaxpr/psum | solution.py:48
  2839.6 130.7 %all-reduce.11.cloned.1.call-start = ((), (), s32[]{:S(2)}) async-start(), calls=%async_computation.4 | async-start | bytes 524288 | tf_op jit(solution)/shard_map/while/body/eval_jaxpr/psum | solution.py:48
  2971.9 131.0 %all-reduce.11.cloned.1.call-start = ((), (), s32[]{:S(2)}) async-start(), calls=%async_computation.4 | async-start | bytes 524288 | tf_op jit(solution)/shard_map/while/body/eval_jaxpr/psum | solution.py:48
  3104.6 130.6 %all-reduce.11.cloned.1.call-start = ((), (), s32[]{:S(2)}) async-start(), calls=%async_computation.4 | async-start | bytes 524288 | tf_op jit(solution)/shard_map/while/body/eval_jaxpr/psum | solution.py:48
  3236.9 131.0 %all-reduce.11.cloned.1.call-start = ((), (), s32[]{:S(2)}) async-start(), calls=%async_computation.4 | async-start | bytes 524288 | tf_op jit(solution)/shard_map/while/body/eval_jaxpr/psum | solution.py:48
  3369.6 131.0 %all-reduce.11.cloned.1.call-start = ((), (), s32[]{:S(2)}) async-start(), calls=%async_computation.4 | async-start | bytes 524288 | tf_op jit(solution)/shard_map/while/body/eval_jaxpr/psum | solution.py:48
  3502.2 131.0 %all-reduce.11.cloned.1.call-start = ((), (), s32[]{:S(2)}) async-start(), calls=%async_computation.4 | async-start | bytes 524288 | tf_op jit(solution)/shard_map/while/body/eval_jaxpr/psum | solution.py:48
  3634.9 130.7 %all-reduce.11.cloned.1.call-start = ((), (), s32[]{:S(2)}) async-start(), calls=%async_computation.4 | async-start | bytes 524288 | tf_op jit(solution)/shard_map/while/body/eval_jaxpr/psum | solution.py:48
  3767.2 131.0 %all-reduce.11.cloned.1.call-start = ((), (), s32[]{:S(2)}) async-start(), calls=%async_computation.4 | async-start | bytes 524288 | tf_op jit(solution)/shard_map/while/body/eval_jaxpr/psum | solution.py:48
  3899.9 130.7 %all-reduce.11.cloned.1.call-start = ((), (), s32[]{:S(2)}) async-start(), calls=%async_computation.4 | async-start | bytes 524288 | tf_op jit(solution)/shard_map/while/body/eval_jaxpr/psum | solution.py:48
  4032.2 130.6 %all-reduce.11.cloned.1.call-start = ((), (), s32[]{:S(2)}) async-start(), calls=%async_computation.4 | async-start | bytes 524288 | tf_op jit(solution)/shard_map/while/body/eval_jaxpr/psum | solution.py:48
  4164.5 131.0 %all-reduce.11.cloned.1.call-start = ((), (), s32[]{:S(2)}) async-start(), calls=%async_computation.4 | async-start | bytes 524288 | tf_op jit(solution)/shard_map/while/body/eval_jaxpr/psum | solution.py:48
  4297.2 131.0 %all-reduce.11.cloned.1.call-start = ((), (), s32[]{:S(2)}) async-start(), calls=%async_computation.4 | async-start | bytes 524288 | tf_op jit(solution)/shard_map/while/body/eval_jaxpr/psum | solution.py:48
  4429.8 130.6 %all-reduce.11.cloned.1.call-start = ((), (), s32[]{:S(2)}) async-start(), calls=%async_computation.4 | async-start | bytes 524288 | tf_op jit(solution)/shard_map/while/body/eval_jaxpr/psum | solution.py:48
  4562.2 131.0 %all-reduce.11.cloned.1.call-start = ((), (), s32[]{:S(2)}) async-start(), calls=%async_computation.4 | async-start | bytes 524288 | tf_op jit(solution)/shard_map/while/body/eval_jaxpr/psum | solution.py:48
  4694.8 131.0 %all-reduce.11.cloned.1.call-start = ((), (), s32[]{:S(2)}) async-start(), calls=%async_computation.4 | async-start | bytes 524288 | tf_op jit(solution)/shard_map/while/body/eval_jaxpr/psum | solution.py:48
  4827.4 130.6 %all-reduce.11.cloned.1.call-start = ((), (), s32[]{:S(2)}) async-start(), calls=%async_computation.4 | async-start | bytes 524288 | tf_op jit(solution)/shard_map/while/body/eval_jaxpr/psum | solution.py:48
  4959.8 131.0 %all-reduce.11.cloned.1.call-start = ((), (), s32[]{:S(2)}) async-start(), calls=%async_computation.4 | async-start | bytes 524288 | tf_op jit(solution)/shard_map/while/body/eval_jaxpr/psum | solution.py:48
  5092.4 131.0 %all-reduce.11.cloned.1.call-start = ((), (), s32[]{:S(2)}) async-start(), calls=%async_computation.4 | async-start | bytes 524288 | tf_op jit(solution)/shard_map/while/body/eval_jaxpr/psum | solution.py:48
  5225.0 130.6 %all-reduce.11.cloned.1.call-start = ((), (), s32[]{:S(2)}) async-start(), calls=%async_computation.4 | async-start | bytes 524288 | tf_op jit(solution)/shard_map/while/body/eval_jaxpr/psum | solution.py:48
  5357.4 130.7 %all-reduce.11.cloned.1.call-start = ((), (), s32[]{:S(2)}) async-start(), calls=%async_computation.4 | async-start | bytes 524288 | tf_op jit(solution)/shard_map/while/body/eval_jaxpr/psum | solution.py:48
  5489.7 131.0 %all-reduce.11.cloned.1.call-start = ((), (), s32[]{:S(2)}) async-start(), calls=%async_computation.4 | async-start | bytes 524288 | tf_op jit(solution)/shard_map/while/body/eval_jaxpr/psum | solution.py:48
  5622.3 130.7 %all-reduce.11.cloned.1.call-start = ((), (), s32[]{:S(2)}) async-start(), calls=%async_computation.4 | async-start | bytes 524288 | tf_op jit(solution)/shard_map/while/body/eval_jaxpr/psum | solution.py:48
  5754.7 131.0 %all-reduce.11.cloned.1.call-start = ((), (), s32[]{:S(2)}) async-start(), calls=%async_computation.4 | async-start | bytes 524288 | tf_op jit(solution)/shard_map/while/body/eval_jaxpr/psum | solution.py:48
  5887.3 131.0 %all-reduce.11.cloned.1.call-start = ((), (), s32[]{:S(2)}) async-start(), calls=%async_computation.4 | async-start | bytes 524288 | tf_op jit(solution)/shard_map/while/body/eval_jaxpr/psum | solution.py:48
  6020.0 131.0 %all-reduce.11.cloned.1.call-start = ((), (), s32[]{:S(2)}) async-start(), calls=%async_computation.4 | async-start | bytes 524288 | tf_op jit(solution)/shard_map/while/body/eval_jaxpr/psum | solution.py:48
  6152.6 130.6 %all-reduce.11.cloned.1.call-start = ((), (), s32[]{:S(2)}) async-start(), calls=%async_computation.4 | async-start | bytes 524288 | tf_op jit(solution)/shard_map/while/body/eval_jaxpr/psum | solution.py:48
  6284.9 131.0 %all-reduce.11.cloned.1.call-start = ((), (), s32[]{:S(2)}) async-start(), calls=%async_computation.4 | async-start | bytes 524288 | tf_op jit(solution)/shard_map/while/body/eval_jaxpr/psum | solution.py:48
  6417.6 130.7 %all-reduce.11.cloned.1.call-start = ((), (), s32[]{:S(2)}) async-start(), calls=%async_computation.4 | async-start | bytes 524288 | tf_op jit(solution)/shard_map/while/body/eval_jaxpr/psum | solution.py:48
  6550.0 130.6 %all-reduce.11.cloned.1.call-start = ((), (), s32[]{:S(2)}) async-start(), calls=%async_computation.4 | async-start | bytes 524288 | tf_op jit(solution)/shard_map/while/body/eval_jaxpr/psum | solution.py:48
  (43 other events, 1607.1 us)
Sparse Core Ops, SparseCore 0:
  173.6 133.3 reduce-scatter.1
  332.2 131.1 all-gather.1
  576.0 362.1 all-reduce.8
  992.7 123.3 all-reduce.10
  1124.3 124.0 all-reduce.10
  1256.6 124.0 all-reduce.10
  1389.3 124.0 all-reduce.10
  1522.0 124.0 all-reduce.10
  1654.6 124.0 all-reduce.10
  1786.9 124.0 all-reduce.10
  1919.5 124.0 all-reduce.10
  2051.9 124.0 all-reduce.10
  2184.6 124.0 all-reduce.10
  2316.9 124.0 all-reduce.10
  2449.3 124.0 all-reduce.10
  2581.6 124.0 all-reduce.10
  2713.9 124.0 all-reduce.10
  2846.2 124.0 all-reduce.10
  2978.9 124.0 all-reduce.10
  3111.2 124.0 all-reduce.10
  3243.8 124.0 all-reduce.10
  3376.5 124.0 all-reduce.10
  3509.1 124.0 all-reduce.10
  3641.4 124.0 all-reduce.10
  3774.1 124.0 all-reduce.10
  3906.4 124.0 all-reduce.10
  4038.8 124.0 all-reduce.10
  4171.4 124.0 all-reduce.10
  4304.1 124.0 all-reduce.10
  4436.4 124.0 all-reduce.10
  4569.1 124.0 all-reduce.10
  4701.7 124.0 all-reduce.10
  4834.0 124.0 all-reduce.10
  4966.7 124.0 all-reduce.10
  5099.3 124.0 all-reduce.10
  5231.6 124.0 all-reduce.10
  5363.9 124.0 all-reduce.10
  5496.6 124.0 all-reduce.10
  5628.9 124.0 all-reduce.10
  5761.6 124.0 all-reduce.10
  5894.2 124.0 all-reduce.10
  6026.9 124.0 all-reduce.10
  6159.2 124.0 all-reduce.10
  6291.9 124.0 all-reduce.10
  6424.2 124.0 all-reduce.10
  6556.5 124.0 all-reduce.10
where the time goes:
time: 6750 us; the launch traced here: 6740 us
  waiting for transfers between devices  6030 us (89%)
  matrix products  236 us (3%)
  local copies, waits for them, and re-layouts  170 us (3%)
  loops' own time  113 us (2%)
  other arithmetic  92 us (1%)
    psum x43, waiting for transfers between devices, broadcast(): return lax.psum(kept, axis)  5450 us
    psum x1, waiting for transfers between devices, local(): lax.psum((grad_conv, grad_head_w, grad_vec, parts), ('scale', 'img'))  309 us
  transfers between devices with their start and end apart: 52, of which 46 were waited for; matrix products, arithmetic and copies ran while one was open for 0% of the time, Pallas kernels for 0%

commit v1 on v0

v1 whole, which is shorter than its diff:
```python
import jax
import jax.numpy as jnp
from jax import lax
from jax.sharding import PartitionSpec as P

STEP = 5

beta_one = 0.5
beta_two = 0.5
adam_eps = 1e-08
rate_matrix = 0.01
rate_vector = 0.2
weight_decay = 0.01
clip_level = 0.001
box_weight = 2.0
norm_eps = 1e-05
highest = lax.Precision.HIGHEST
bf16 = jnp.bfloat16
f32 = jnp.float32
AXES = ("scale", "img")
GAP = 16
CODE = 32767.0


class Layout:
    def __init__(self, scales, imgs):
        self.scales = scales
        self.imgs = imgs

    def pos(self, group, scale):
        return scale if group % 2 == 0 else self.scales - 1 - scale

    def dev(self, scale, img):
        return scale * self.imgs + img

    def at(self, group, place, core):
        return self.dev(self.pos(group, place), 2 * group + core)

    def all_devices(self):
        return [(s, i) for s in range(self.scales) for i in range(self.imgs)]

    def swap(self, bit):
        return [(self.dev(s, i), self.dev(s, i ^ bit)) for s, i in self.all_devices()]

    def turn(self, step):
        return [
            (self.dev(s, i), self.dev((s + step) % self.scales, i)) for s, i in self.all_devices()
        ]

    def scale_swap(self, bit):
        return [(self.dev(s, i), self.dev(s ^ bit, i)) for s, i in self.all_devices()]

    def rows_round(self, shift, sources):
        pairs = []
        for s in sources:
            for i in range(self.imgs):
                group, core = i // 2, i % 2
                piece = (shift + s) % self.scales
                place = (self.scales // 2) * core + piece // 2
                pairs.append((self.dev(s, i), self.at(group, place, piece % 2)))
        return pairs

    def row_order(self):
        groups = self.imgs // 2
        return [
            self.at(j, place, c) for j in range(groups) for place in range(self.scales) for c in range(2)
        ]

    def down(self):
        order = self.row_order()
        return list(zip(order[:-1], order[1:]))

    def up(self):
        order = self.row_order()
        return list(zip(order[1:], order[:-1]))


def permute(value, pairs):
    return lax.ppermute(value, AXES, pairs)


def after(value, *others):
    return lax.optimization_barrier((value, *others))[0]


def column_table(columns, width, coarse_width):
    fine_idx = jnp.arange(width, dtype=jnp.int32)
    numer = jnp.maximum((2 * fine_idx + 1) * columns - width, 0)
    lower = numer // (2 * width)
    frac = (numer % (2 * width)).astype(f32) / (2.0 * width)
    upper = jnp.minimum(lower + 1, columns - 1)
    coarse = jnp.arange(coarse_width, dtype=jnp.int32)[:, None]
    return (1.0 - frac)[None, :] * (coarse == lower[None, :]).astype(f32) + frac[None, :] * (
        coarse == upper[None, :]
    ).astype(f32)


def halves(value):
    high = value.astype(bf16)
    return high, (value - high.astype(f32)).astype(bf16)


def conv_rows(padded, weights):
    kernel = weights.reshape(3, 3, weights.shape[1], weights.shape[2])
    return lax.conv_general_dilated(
        padded[None],
        kernel,
        (1, 1),
        ((0, 0), (1, 1)),
        dimension_numbers=("NHWC", "HWIO", "NHWC"),
        preferred_element_type=f32,
    )[0]


def conv_rows_back(padded, weights):
    kernel = lax.rev(weights.reshape(3, 3, weights.shape[1], weights.shape[2]), (0, 1))
    return lax.conv_general_dilated(
        padded[None],
        kernel,
        (1, 1),
        ((0, 0), (1, 1)),
        dimension_numbers=("NHWC", "HWOI", "NHWC"),
        preferred_element_type=f32,
    )[0]


def kernel_grad(padded_pair, grad_pair):
    rows, cols = grad_pair.shape[1], grad_pair.shape[2]
    wide = jnp.pad(padded_pair, ((0, 0), (0, 0), (1, 1), (0, 0)))
    grads = []
    for tap in range(9):
        a, b = tap // 3, tap % 3
        window = wide[:, a : a + rows, b : b + cols]
        grads.append(
            jnp.einsum("prwc,prwd->cd", window, grad_pair, preferred_element_type=f32)
        )
    return jnp.stack(grads)


def activate(pre, gain, shift, col_mask):
    return jax.nn.gelu(pre * gain + shift) * col_mask


def tap_norm(result, gamma):
    return gamma * result * lax.rsqrt(jnp.mean(result * result, -1, keepdims=True) + norm_eps)


def cosine_terms(predict, target_last, mask_f):
    inner = jnp.sum(predict * target_last, -1)
    cosine = inner * lax.rsqrt(
        (jnp.sum(predict * predict, -1) + 1.0) * (jnp.sum(target_last * target_last, -1) + 1.0)
    )
    return jnp.sum(mask_f * (1.0 - cosine))


def encode(value):
    n, r, cols = value.shape
    top = jnp.max(jnp.abs(value), 1)
    power = jnp.clip(jnp.ceil(jnp.log2(top)), -100.0, 110.0)
    step = jnp.exp2(-power) * CODE
    codes = jnp.clip(jnp.round(value * step[:, None, :]), -CODE, CODE).astype(jnp.int16)
    pad = -n % 16
    powers = jnp.pad(power.astype(jnp.int16), ((0, pad), (0, 0)))
    return jnp.concatenate([codes.reshape(n * r, cols), powers], 0)


def decode(rows, n):
    pad = -n % 16
    total, cols = rows.shape
    r = (total - n - pad) // n
    power = rows[n * r : n * r + n].astype(f32)
    step = jnp.exp2(power) * (1.0 / CODE)
    return rows[: n * r].reshape(n, r, cols).astype(f32) * step[:, None, :]


def pick(value, index, axis):
    return lax.dynamic_index_in_dim(value, index, axis, keepdims=False)


def reduce_piece(part, split, place, lay):
    x, y, z = place
    n, rows, cols = part.shape
    scales = lay.scales
    eighth = rows // 4
    v = part.reshape(n, 2, 2, eighth, cols)
    va, vb = v[..., :split], v[..., split:]
    wa, wb = split, cols - split
    send_a = encode(pick(va, 1 - x, 1).reshape(n, 2 * eighth, wa))
    send_b = encode(pick(vb, 1 - y, 2).reshape(n, 2 * eighth, wb))
    got_a = permute(send_a, lay.swap(2))
    got_b = permute(send_b, lay.swap(4))
    keep_a = pick(va, x, 1) + decode(got_a, n).reshape(n, 2, eighth, wa)
    keep_b = pick(vb, y, 2) + decode(got_b, n).reshape(n, 2, eighth, wb)
    send_a = encode(pick(keep_a, 1 - y, 1))
    send_b = encode(pick(keep_b, 1 - x, 1))
    got_a = permute(send_a, lay.swap(4))
    got_b = permute(send_b, lay.swap(2))
    keep_a = pick(keep_a, y, 1) + decode(got_a, n)
    keep_b = pick(keep_b, x, 1) + decode(got_b, n)
    keep = jnp.concatenate([keep_a, keep_b], -1).reshape(n, scales, eighth // scales, cols)
    total = pick(keep, z, 1)
    for step in range(1, scales):
        send = encode(pick(keep, (z + step) % scales, 1))
        total = total + decode(permute(send, lay.turn(step)), n)
    return total


def core_trade(total, core, lay):
    n, rows, cols = total.shape
    v = total.reshape(n, 2, rows // 2, cols)
    own = pick(v, core, 1)
    other = permute(pick(v, 1 - core, 1), lay.swap(1))
    first = jnp.where(core == 0, own, other)
    second = jnp.where(core == 0, other, own)
    return jnp.stack([first, second])


def from_blocks(blocks, depth, taps):
    count_conv = depth * taps * 2
    chans, half = (blocks.shape[1], blocks.shape[2])
    conv_part = (
        blocks[:count_conv]
        .reshape(depth, taps, 2, chans, half)
        .transpose(0, 1, 3, 2, 4)
        .reshape(depth, taps, chans, 2 * half)
    )
    return (conv_part, blocks[count_conv:])


def soap_update(master, moment, second, left, right, grads):
    turned = jnp.einsum("sij,sik->sjk", left, grads, precision=highest)
    turned = jnp.einsum("sjk,skl->sjl", turned, right, precision=highest)
    moment = beta_one * moment + (1.0 - beta_one) * turned
    second = beta_two * second + (1.0 - beta_two) * turned * turned
    ratio = moment / (1.0 - beta_one**STEP) / (jnp.sqrt(second / (1.0 - beta_two**STEP)) + adam_eps)
    back = jnp.einsum("sij,sjk->sik", left, ratio, precision=highest)
    back = jnp.einsum("sik,slk->sil", back, right, precision=highest)
    return (master - rate_matrix * (back + weight_decay * master), moment, second)


def vector_update(params, moment, second, grads):
    moment = beta_one * moment + (1.0 - beta_one) * grads
    second = beta_two * second + (1.0 - beta_two) * grads * grads
    ratio = moment / (1.0 - beta_one**STEP) / (jnp.sqrt(second / (1.0 - beta_two**STEP)) + adam_eps)
    return (params - rate_vector * (ratio + weight_decay * params), moment, second)


def butterfly(value, lay):
    bit = 1
    while bit < lay.imgs:
        value = value + permute(value, lay.swap(bit))
        bit *= 2
    bit = 1
    while bit < lay.scales:
        value = value + permute(value, lay.scale_swap(bit))
        bit *= 2
    return value


def local(
    images,
    valid_mask,
    scale_cols,
    boxes,
    normal_targets,
    dense_targets,
    affine_scale,
    affine_shift,
    conv_bf16,
    head_bf16,
    vectors,
    vec_m,
    vec_v,
    master,
    slot_m,
    slot_v,
    basis_left,
    basis_right,
    owner_slot,
):
    held, width, chans = (images.shape[1], images.shape[2], images.shape[3])
    heads_count, head_width = (head_bf16.shape[0], head_bf16.shape[2])
    wide = heads_count * head_width
    depth, taps = (conv_bf16.shape[0], conv_bf16.shape[1])
    scales, imgs = lax.axis_size("scale"), lax.axis_size("img")
    lay = Layout(scales, imgs)
    rows = held // scales
    z = lax.axis_index("scale")
    img = lax.axis_index("img")
    group, core = img // 2, img % 2
    place = jnp.where(group % 2 == 0, z, scales - 1 - z)
    mine = 2 * (place % 2) + core

    widths = [width >> s for s in range(scales)]
    starts = []
    at = 0
    for w in widths:
        starts.append(at)
        at += w + GAP
    cols = at - GAP
    col_iota = jnp.arange(cols, dtype=jnp.int32)
    valid_col = jnp.zeros((cols,), jnp.bool_)
    for s in range(scales):
        valid_col |= (col_iota >= starts[s]) & (col_iota < starts[s] + scale_cols[s])
    col_mask = valid_col.astype(f32)[None, :, None]

    own = images[0]
    fine = [
        permute(own[rows * k : rows * (k + 1)], lay.rows_round(k, [0])) for k in range(scales)
    ]
    coarse = []
    for k in range(scales):
        piece = (k + z) % scales
        send = lax.dynamic_slice_in_dim(own[:, : widths[1]], piece * rows, rows, 0)
        coarse.append(permute(send, lay.rows_round(k, range(1, scales))))
    parts = [(fine[0] + fine[1]) + (fine[2] + fine[3])]
    for s in range(1, scales):
        got = 0.0
        for k in range(scales):
            got = got + jnp.where((mine - k) % scales == s, coarse[k][:, : widths[s]], 0)
        parts.append(got.astype(bf16))
    spread = []
    for s in range(scales):
        spread.append(parts[s])
        if s + 1 < scales:
            spread.append(jnp.zeros((rows, GAP, chans), bf16))
    x_zero = jnp.concatenate(spread, 1) * col_mask.astype(bf16)

    target_base = after(dense_targets, x_zero)
    arrived = []
    for k in range(scales):
        piece = (k + z) % scales
        send = lax.dynamic_slice_in_dim(target_base, piece * rows, rows, 0)
        arrived.append(permute(send, lay.rows_round(k, range(scales))))
    stacked_targets = jnp.stack(arrived)
    target = jnp.concatenate(
        [pick(stacked_targets, (mine - s) % scales, 0) for s in range(scales)], -1
    )

    mask_all = valid_mask.astype(f32)
    pixels = jnp.arange(held * width, dtype=jnp.int32)
    hits = jnp.sum((boxes[:, None] == pixels[None, :]).astype(f32), 0).reshape(held, width)
    packed = jnp.concatenate(
        [mask_all[None], (mask_all + box_weight * hits)[None], normal_targets], 0
    )
    packed_other = permute(packed, lay.swap(1))
    from_own = place // (scales // 2) == core
    packed = jnp.where(from_own, packed, packed_other)
    packed = lax.dynamic_slice_in_dim(packed, mine * rows, rows, 1)
    mask_f, weight = packed[0], packed[1]
    normals = jnp.moveaxis(packed[2:], 0, -1)
    count = jnp.full((8, 128), jnp.sum(mask_all), f32)
    bit = 1
    while bit < imgs:
        count = count + permute(count, lay.swap(bit))
        bit *= 2
    count = count[0, 0]

    current = x_zero
    kept = []
    result = None
    for depth_idx in range(depth):
        above = permute(current[rows - 1 :], lay.down())
        below = permute(current[:1], lay.up())
        padded = jnp.concatenate([above, current, below], 0)
        pre = conv_rows(padded, conv_bf16[depth_idx])
        result = activate(pre, affine_scale[depth_idx], affine_shift[depth_idx], col_mask)
        pair = jnp.stack([padded, permute(padded, lay.swap(1))])
        kept.append((pair, pre))
        current = result.astype(bf16)
    gamma = vectors[:chans]
    bias = vectors[chans:]
    tapped, tap_pull = jax.vjp(tap_norm, result, gamma)
    tapped_low = tapped.astype(bf16)

    tables = []
    for s in range(scales):
        tables.append(column_table(scale_cols[s], width, widths[s]))
        if s + 1 < scales:
            tables.append(jnp.zeros((GAP, width), f32))
    table = jnp.concatenate(tables, 0)
    table_high, table_low = halves(table)
    raised = jnp.einsum("ij,ric->rjc", table_high, tapped_low, preferred_element_type=f32)
    raised += jnp.einsum("ij,ric->rjc", table_low, tapped_low, preferred_element_type=f32)
    raised_high, raised_low = halves(raised)
    heads = head_bf16.transpose(1, 0, 2).reshape(chans, wide)
    joined = (
        jnp.einsum("rjc,ck->rjk", raised_high, heads, preferred_element_type=f32)
        + jnp.einsum("rjc,ck->rjk", raised_low, heads, preferred_element_type=f32)
        + scales * bias
    )

    def local_loss(joined_part):
        dense = 0.5 * jnp.sum(weight[:, :, None] * (joined_part - target.astype(f32)) ** 2)
        normal = cosine_terms(joined_part[:, :, 0:3], normals, mask_f)
        return ((dense / wide + normal) / count, jnp.stack([dense, normal]))

    loss_local, loss_pull, loss_parts = jax.vjp(local_loss, joined, has_aux=True)
    (grad_joined,) = loss_pull(jnp.ones_like(loss_local))
    grad_bias = scales * jnp.sum(grad_joined, (0, 1))
    grad_low = grad_joined.astype(bf16)
    grad_raised = jnp.einsum("rjk,ck->rjc", grad_low, heads, preferred_element_type=f32)
    grad_tapped = jnp.einsum(
        "ij,rjc->ric", table, grad_raised, precision=lax.Precision.HIGH
    )
    half_wide = wide // 2
    raised_pair = jnp.stack([raised_high, permute(raised_high, lay.swap(1))])
    grad_mine = lax.dynamic_slice_in_dim(grad_low, core * half_wide, half_wide, 2)
    grad_give = lax.dynamic_slice_in_dim(grad_low, (1 - core) * half_wide, half_wide, 2)
    grad_pair = jnp.stack([grad_mine, permute(grad_give, lay.swap(1))])
    head_grad = jnp.einsum("prjc,prjk->ck", raised_pair, grad_pair, preferred_element_type=f32)

    grad_result, grad_gamma = tap_pull(grad_tapped)
    half = chans // 2
    conv_grads = [None] * depth
    for depth_idx in reversed(range(depth)):
        pair, pre = kept[depth_idx]
        _, act_pull = jax.vjp(
            lambda value: activate(
                value, affine_scale[depth_idx], affine_shift[depth_idx], col_mask
            ),
            pre,
        )
        (grad_pre,) = act_pull(grad_result)
        grad_pre = grad_pre.astype(bf16)
        if depth_idx > 0:
            above = permute(grad_pre[rows - 1 :], lay.down())
            below = permute(grad_pre[:1], lay.up())
        grad_mine = lax.dynamic_slice_in_dim(grad_pre, core * half, half, 2)
        grad_give = lax.dynamic_slice_in_dim(grad_pre, (1 - core) * half, half, 2)
        grad_pair = jnp.stack([grad_mine, permute(grad_give, lay.swap(1))])
        conv_grads[depth_idx] = kernel_grad(pair, grad_pair)
        if depth_idx > 0:
            grad_padded = jnp.concatenate([above, grad_pre, below], 0)
            grad_result = conv_rows_back(grad_padded, conv_bf16[depth_idx])

    vec_rows = jnp.concatenate(
        [grad_gamma, grad_bias, loss_parts, jnp.zeros((-(chans + wide + 2) % 1024,), f32)]
    ).reshape(-1, 128)
    vec_sum = butterfly(vec_rows, lay).reshape(-1)
    grad_vec = vec_sum[: chans + wide]
    totals = vec_sum[chans + wide : chans + wide + 2]
    vec_squares = jnp.sum(grad_vec * grad_vec)

    blocks_count = owner_slot.shape[0]
    slots_here = master.shape[0]
    slots = slots_here * scales * imgs
    slot_ids = jnp.arange(slots, dtype=jnp.int32)
    match = slot_ids[:, None] == owner_slot[None, :]
    block_of = jnp.sum(
        jnp.where(match, jnp.arange(blocks_count, dtype=jnp.int32)[None, :], 0), 1
    )
    owned_f = jnp.any(match, 1).astype(f32)

    if imgs == 8 and scales == 4:
        x, y = (img // 2) % 2, img // 4
        where = (x, y, z)
        head_final = reduce_piece(head_grad[None], 4 * 128, where, lay)
        finals = [None] * depth
        for depth_idx in reversed(range(depth)):
            finals[depth_idx] = reduce_piece(conv_grads[depth_idx], half // 2, where, lay)
        conv_rows_final = jnp.stack([core_trade(v, core, lay) for v in finals])
        head_rows = core_trade(head_final, core, lay)
        fine_rows = conv_rows_final.shape[3]
        conv_blocks = conv_rows_final.transpose(0, 2, 1, 3, 4).reshape(-1, fine_rows, half)
        head_blocks = (
            head_rows[:, 0]
            .transpose(1, 0, 2)
            .reshape(fine_rows, heads_count, head_width)
            .transpose(1, 0, 2)
        )
        blocks = jnp.concatenate([conv_blocks, head_blocks], 0)
        squares = jnp.sum(blocks * blocks)
        by_slot = blocks[block_of] * owned_f[:, None, None]
        devices = scales * imgs
        top = jnp.max(jnp.abs(by_slot), 1)
        power = jnp.clip(jnp.ceil(jnp.log2(top)), -100.0, 110.0)
        step = jnp.exp2(-power) * CODE
        codes = jnp.clip(jnp.round(by_slot * step[:, None, :]), -CODE, CODE).astype(jnp.int16)
        codes = codes.reshape(devices, slots_here * fine_rows, half)
        powers = power.astype(jnp.int16).reshape(devices, slots_here, half)
        log_sq = jnp.log2(jnp.maximum(squares, 1e-37))
        sq_pow = jnp.floor(log_sq)
        mant = jnp.maximum(squares, 1e-37) * jnp.exp2(-sq_pow) * 8192.0
        mant_high = jnp.floor(mant)
        mant_low = jnp.floor((mant - mant_high) * 16384.0)
        sq_row = jnp.stack([sq_pow, mant_high, mant_low]).astype(jnp.int16)
        sq_row = jnp.broadcast_to(jnp.pad(sq_row, (0, half - 3))[None, None], (devices, 1, half))
        payload = jnp.concatenate([codes, powers, sq_row], 1)
        payload = jnp.pad(payload, ((0, 0), (0, -payload.shape[1] % 16), (0, 0)))
        got = lax.all_to_all(payload, AXES, 0, 0, tiled=True)
        code_rows = slots_here * fine_rows
        got_pow = got[:, code_rows : code_rows + slots_here].astype(f32)
        got_sq = got[:, code_rows + slots_here, 0:3].astype(f32)
        all_squares = (
            (got_sq[:, 1] + got_sq[:, 2] * (1.0 / 16384.0)) * (1.0 / 8192.0) * jnp.exp2(got_sq[:, 0])
        )
        squares_sum = jnp.sum(all_squares) + vec_squares
        values = got[:, :code_rows].reshape(devices, slots_here, fine_rows, half).astype(f32)
        values = values * (jnp.exp2(got_pow) * (1.0 / CODE))[:, :, None, :]
        owned = (
            values.reshape(scales, 2, 2, 2, slots_here, fine_rows, half)
            .transpose(4, 2, 1, 0, 3, 5, 6)
            .reshape(slots_here, chans, half)
        )
    else:
        both = []
        for depth_idx in range(depth):
            own_half = conv_grads[depth_idx]
            none = jnp.zeros_like(own_half)
            both.append(
                jnp.stack(
                    [jnp.where(core == 0, own_half, none), jnp.where(core == 1, own_half, none)], 1
                )
            )
        head_full = jnp.concatenate(
            [
                jnp.where(core == 0, head_grad, 0.0),
                jnp.where(core == 1, head_grad, 0.0),
            ],
            1,
        )
        blocks = jnp.concatenate(
            [v.reshape(-1, chans, half) for v in both]
            + [head_full.reshape(chans, heads_count, head_width).transpose(1, 0, 2)],
            0,
        )
        by_slot = blocks[block_of] * owned_f[:, None, None]
        owned = lax.psum_scatter(by_slot, AXES, scatter_dimension=0, tiled=True)
        squares_sum = lax.psum(jnp.sum(owned * owned), AXES) + vec_squares

    grad_norm = jnp.sqrt(squares_sum)
    factor = clip_level / jnp.maximum(grad_norm, clip_level)
    vec_new, vec_m_new, vec_v_new = vector_update(vectors, vec_m, vec_v, grad_vec * factor)
    master_new, slot_m_new, slot_v_new = soap_update(
        master, slot_m, slot_v, basis_left, basis_right, owned * factor
    )
    fresh = master_new.astype(bf16)
    every = lax.all_gather(fresh, AXES, axis=0, tiled=True)
    store = every[owner_slot]
    conv_copy, head_copy = from_blocks(store, depth, taps)
    loss = jnp.stack([totals[0] / wide + totals[1], count])
    return (
        loss,
        grad_norm,
        vec_new,
        vec_m_new,
        vec_v_new,
        master_new,
        slot_m_new,
        slot_v_new,
        conv_copy,
        head_copy,
    )


def solution(mesh):
    in_specs = (
        P("scale", "img", None, None),
        P("img", None),
        P(),
        P("img"),
        P(None, "img", None),
        P("img", None, "scale"),
        P(),
        P(),
        P(),
        P(),
        P(),
        P(),
        P(),
        P(("scale", "img"), None, None),
        P(("scale", "img"), None, None),
        P(("scale", "img"), None, None),
        P(("scale", "img"), None, None),
        P(("scale", "img"), None, None),
        P(),
    )
    out_specs = (
        P(),
        P(),
        P(),
        P(),
        P(),
        P(("scale", "img"), None, None),
        P(("scale", "img"), None, None),
        P(("scale", "img"), None, None),
        P(),
        P(),
    )
    return jax.shard_map(local, mesh=mesh, in_specs=in_specs, out_specs=out_specs, check_vma=False)
```

time: 6750 us -> 576 us (0.09)
  waiting for transfers between devices: 6030 us -> 212 us
  matrix products: 236 us -> 72.5 us
  loops' own time: 113 us -> 0 us
  starting transfers between devices: 14.7 us -> 105 us
  local copies, waits for them, and re-layouts: 170 us -> 101 us
    psum x44 -> x0, waiting for transfers between devices: 5760 us -> none  [the longest x43 5450 us: broadcast(): return lax.psum(kept, axis)]
    dot_general x50 -> x25, matrix products: 226 us -> 46.8 us  [the longest x18 36.1 us: kernel_grad(): jnp.einsum('prwc,prwd->cd', window, grad_pair, preferred_element_type=f32)]
    reduce_scatter x1 -> x0, waiting for transfers between devices: 133 us -> none  [local(): lax.psum_scatter(raised.astype(jnp.bfloat16), 'scale', scatter_dimension=...]
    another operation x1 -> x0, loops' own time: 113 us -> none  [local(): store = lax.fori_loop(0, owner_slot.shape[0], send_block, store)]
    ppermute x6 -> x57, waiting for transfers between devices: 0.02 us -> 100 us  [permute(): return lax.ppermute(value, AXES, pairs)]
    ppermute x6 -> x57, starting transfers between devices: 14.4 us -> 102 us  [permute(): return lax.ppermute(value, AXES, pairs)]
    dynamic_update_slice x43 -> x0, local copies, waits for them, and re-layouts: 71.8 us -> none  [send_block(): return lax.dynamic_update_index_in_dim(store, arrived_block, block_idx, 0)]
  transfers between devices with their start and end apart: 52 -> 59, of which waited for: 46 -> 22; matrix products, arithmetic and copies ran while one was open for 0% -> 25% of each run, Pallas kernels for 0% -> 0%
where the time goes in v1:
time: 576 us; the launch traced here: 569 us
  waiting for transfers between devices  212 us (37%)
  starting transfers between devices  105 us (18%)
  local copies, waits for them, and re-layouts  101 us (18%)
  matrix products  72.5 us (13%)
  other arithmetic  50.5 us (9%)
  between operations  27.5 us (5%)
    all_gather x1, waiting for transfers between devices, local(): every = lax.all_gather(fresh, AXES, axis=0, tiled=True)  112 us
    ppermute x57, starting transfers between devices, permute(): return lax.ppermute(value, AXES, pairs)  102 us
    ppermute x57, waiting for transfers between devices, permute(): return lax.ppermute(value, AXES, pairs)  100 us
    dot_general x18, matrix products, kernel_grad(): jnp.einsum('prwc,prwd->cd', window, grad_pair, preferred_element_type=f32)  36.1 us
    unnamed x104, local copies, waits for them, and re-layouts  14.3 us
    gather x1, local copies, waits for them, and re-layouts, local(): store = every[owner_slot]  11.8 us
  transfers between devices with their start and end apart: 59, of which 22 were waited for; matrix products, arithmetic and copies ran while one was open for 25% of the time, Pallas kernels for 0%

profile of v1, /device:TPU:0, one launch (start us, length us, event | category | flops | bytes accessed | tf_op | source)
XLA Modules:
  0.0 568.8 jit_solution(3618093097210725959)
XLA Ops:
  10.7 2.9 slice_bitcast_fusion.2
  13.6 2.7 collective-permute-start.1
  16.3 4.0 collective-permute-start.2
  20.3 5.4 collective-permute-start
  40.8 8.3 %fusion.351 = (bf16[1,9,512,512]{3,2,1,0:T(8,128)(2,1)}, bf16[1,9,512,512]{3,2,1,0:T(8,128)(2,1)}) fusion(bf16[2,9,512,512]{3,2,1,0:T(8,128)(2,1)} %param.27), kind=kLoop, calls=%fused_computation.723 | loop fusion | bytes 18874368 | tf_op jit(solution)/shard_map/slice | solution.py:366
  60.3 3.5 copy.333
  73.7 15.5 %collective-permute-done.7 = bf16[2,128,512]{2,1,0:T(8,128)(2,1)S(1)} collective-permute-done((bf16[2,128,512]{2,1,0:T(8,128)(2,1)S(1)}, bf16[2,128,512]{2,1,0:T(8,128)(2,1)S(1)}, u32[]{:S(2)}, u32[]{:S(2)}) %collective-permute-start.7) | collective-permute-done | bytes 262176 | tf_op jit(solution)/shard_map/ppermute | solution.py:79
  99.4 6.4 %collective-permute-start.19 = (bf16[2,256,448]{1,2,0:T(8,128)(2,1)S(1)}, bf16[2,256,448]{1,2,0:T(8,128)(2,1)S(1)}, u32[]{:S(2)}, u32[]{:S(2)}) collective-permute-start(bf16[2,256,448]{1,2,0:T(8,128)(2,1)S(1)} %get-tuple-element.83), channel_id=1, source_target_pairs={{0,9},{1,25},{2,19},{3,3},{4,13},{5,29},{6,23},{7,7},{8,0},{9,16},... | collective-permute-start | bytes 1376264 | tf_op jit(solution)/shard_map/ppermute | solution.py:79
  105.9 4.5 collective-permute-start.17
  110.4 3.7 fusion.343
  118.0 5.3 fusion.95
  127.8 4.1 collective-permute-start.10
  133.2 8.1 %collective-permute-done.18 = bf16[2,256,448]{1,2,0:T(8,128)(2,1)S(1)} collective-permute-done((bf16[2,256,448]{1,2,0:T(8,128)(2,1)S(1)}, bf16[2,256,448]{1,2,0:T(8,128)(2,1)S(1)}, u32[]{:S(2)}, u32[]{:S(2)}) %collective-permute-start.18) | collective-permute-done | bytes 458784 | tf_op jit(solution)/shard_map/ppermute | solution.py:79
  150.9 4.3 concatenate.116
  155.3 3.7 fusion.341
  162.0 5.3 fusion.92
  181.3 2.4 fusion.47
  183.7 2.5 fusion.41
  192.1 10.5 %collective-permute-start.48 = (bf16[2,256,896]{2,1,0:T(8,128)(2,1)S(1)}, bf16[2,256,896]{2,1,0:T(8,128)(2,1)S(1)}, u32[]{:S(2)}, u32[]{:S(2)}) collective-permute-start(bf16[2,256,896]{2,1,0:T(8,128)(2,1)S(1)} %get-tuple-element.77), channel_id=1, source_target_pairs={{0,1},{1,0},{2,3},{3,2},{4,5},{5,4},{6,7},{7,6},{8,9},{9,8},{10,11... | collective-permute-start | bytes 2752520 | tf_op jit(solution)/shard_map/ppermute | solution.py:79
  205.8 5.4 fusion.89
  214.5 2.9 fusion.33
  219.0 6.5 %collective-permute-start.51 = (s16[272,384]{1,0:T(8,128)(2,1)S(1)}, s16[272,384]{1,0:T(8,128)(2,1)S(1)}, u32[]{:S(2)}, u32[]{:S(2)}) collective-permute-start(s16[272,384]{1,0:T(8,128)(2,1)S(1)} %pad_add_fusion.10), channel_id=1, source_target_pairs={{0,4},{1,5},{2,6},{3,7},{4,0},{5,1},{6,2},{7,3},{8,12},{9,13},{10,... | collective-permute-start | bytes 626696 | tf_op jit(solution)/shard_map/ppermute | solution.py:79
  227.5 3.8 collective-permute-done.51
  231.7 3.0 collective-permute-start.52
  237.5 2.7 collective-permute-done.50
  242.8 3.5 collective-permute-done.54
  246.8 6.2 %collective-permute-done.53 = s16[48,896]{1,0:T(8,128)(2,1)S(1)} collective-permute-done((s16[48,896]{1,0:T(8,128)(2,1)S(1)}, s16[48,896]{1,0:T(8,128)(2,1)S(1)}, u32[]{:S(2)}, u32[]{:S(2)}) %collective-permute-start.53) | collective-permute-done | bytes 86048 | tf_op jit(solution)/shard_map/ppermute | solution.py:79
  256.2 2.8 pad_maximum_fusion
  287.2 2.4 fusion.334
  310.3 15.8 %collective-permute-done.30 = s16[1168,128]{1,0:T(8,128)(2,1)S(1)} collective-permute-done((s16[1168,128]{1,0:T(8,128)(2,1)S(1)}, s16[1168,128]{1,0:T(8,128)(2,1)S(1)}, u32[]{:S(2)}, u32[]{:S(2)}) %collective-permute-start.30) | collective-permute-done | bytes 299040 | tf_op jit(solution)/shard_map/ppermute | solution.py:79
  329.2 4.3 collective-permute-done.35
  333.5 6.3 %collective-permute-done.34 = s16[304,256]{1,0:T(8,128)(2,1)S(1)} collective-permute-done((s16[304,256]{1,0:T(8,128)(2,1)S(1)}, s16[304,256]{1,0:T(8,128)(2,1)S(1)}, u32[]{:S(2)}, u32[]{:S(2)}) %collective-permute-start.34) | collective-permute-done | bytes 155680 | tf_op jit(solution)/shard_map/ppermute | solution.py:79
  344.7 5.7 collective-permute-done.40
  353.5 2.3 collective-permute-start.44
  358.3 10.8 %collective-permute-done.44 = s16[304,256]{1,0:T(8,128)(2,1)S(1)} collective-permute-done((s16[304,256]{1,0:T(8,128)(2,1)S(1)}, s16[304,256]{1,0:T(8,128)(2,1)S(1)}, u32[]{:S(2)}, u32[]{:S(2)}) %collective-permute-start.44) | collective-permute-done | bytes 155680 | tf_op jit(solution)/shard_map/ppermute | solution.py:79
  377.0 2.6 all-to-all-start
  384.1 2.6 collective-permute-done.21
  388.0 2.7 collective-permute-done.22
  394.4 3.4 collective-permute-start.24
  397.8 2.8 collective-permute-done.24
  403.8 3.5 fusion.365
  408.7 2.5 fusion.129
  411.4 2.4 fusion.362
  417.6 111.9 %all-gather.2.cloned.1.call-done = bf16[64,512,256]{2,1,0:T(8,128)(2,1)} async-done(((bf16[2,512,256]{2,1,0:T(8,128)(2,1)}), bf16[64,512,256]{2,1,0:T(8,128)(2,1)}) %all-gather.2.cloned.1.call-update) | async-done | bytes 16777232 | tf_op jit(solution)/shard_map/all_gather | solution.py:539
  529.4 11.8 %gather_fusion.1 = bf16[43,512,256]{2,1,0:T(8,128)(2,1)} fusion(bf16[64,512,256]{2,1,0:T(8,128)(2,1)} %all-gather.2.cloned.1.call-done, s32[1024]{0:T(1024)S(1)} %pad_clamp_fusion), kind=kCustom, calls=%fused_computation.1 | custom fusion | bytes 22544556 | tf_op jit(solution)/shard_map/gather | solution.py:540
  541.2 2.8 slice.580
  544.1 8.3 %slice.579 = bf16[36,512,256]{2,1,0:T(8,128)(2,1)} slice(bf16[43,512,256]{2,1,0:T(8,128)(2,1)} %gather_fusion.1), slice={[0:36], [0:512], [0:256]} | slice | bytes 18874368 | tf_op jit(solution)/shard_map/slice | solution.py:222
  552.4 8.2 %copy.403 = bf16[2,9,2,64,8,256]{5,4,2,3,1,0:T(8,128)(2,1)} copy(bf16[2,9,2,64,8,256]{5,4,3,2,1,0:T(8,128)(2,1)} %bitcast.642) | data formatting | bytes 18874368 | tf_op jit(solution)/shard_map/reshape | solution.py:225
  (496 shorter events, 188.2 us)
Async XLA Ops:
  10.2 41.2 %collective-permute-start.13 = (f32[8,128]{1,0:T(8,128)S(1)}, f32[8,128]{1,0:T(8,128)S(1)}, u32[]{:S(2)}, u32[]{:S(2)}) collective-permute-start(f32[8,128]{1,0:T(8,128)S(1)} %broadcast_in_dim.68), channel_id=1, source_target_pairs={{0,1},{1,0},{2,3},{3,2},{4,5},{5,4},{6,7},{7,6},{8,9},{9,8},{10,11... | collective-permute-start | bytes 12296 | tf_op jit(solution)/shard_map/ppermute | solution.py:79
  13.6 53.6 %collective-permute-start.1 = (bf16[2,256,512]{2,1,0:T(8,128)(2,1)}, bf16[2,256,512]{2,1,0:T(8,128)(2,1)}, u32[]{:S(2)}, u32[]{:S(2)}) collective-permute-start(bf16[2,256,512]{2,1,0:T(8,128)(2,1)} %get-tuple-element.72), channel_id=1, source_target_pairs={{0,1},{1,17},{2,27},{3,11},{4,5},{5,21},{6,31},{7,15}} | collective-permute-start | bytes 1572872 | tf_op jit(solution)/shard_map/ppermute | solution.py:79
  16.3 51.6 %collective-permute-start.2 = (bf16[2,256,512]{2,1,0:T(8,128)(2,1)}, bf16[2,256,512]{2,1,0:T(8,128)(2,1)}, u32[]{:S(2)}, u32[]{:S(2)}) collective-permute-start(bf16[2,256,512]{2,1,0:T(8,128)(2,1)} %get-tuple-element.73), channel_id=1, source_target_pairs={{0,8},{1,24},{2,18},{3,2},{4,12},{5,28},{6,22},{7,6}} | collective-permute-start | bytes 1572872 | tf_op jit(solution)/shard_map/ppermute | solution.py:79
  20.3 48.9 %collective-permute-start = (bf16[2,256,512]{2,1,0:T(8,128)(2,1)}, bf16[2,256,512]{2,1,0:T(8,128)(2,1)}, u32[]{:S(2)}, u32[]{:S(2)}) collective-permute-start(bf16[2,256,512]{2,1,0:T(8,128)(2,1)} %get-tuple-element.74), channel_id=1, source_target_pairs={{0,0},{1,16},{2,26},{3,10},{4,4},{5,20},{6,30},{7,14}} | collective-permute-start | bytes 1572872 | tf_op jit(solution)/shard_map/ppermute | solution.py:79
  25.7 44.9 %collective-permute-start.3 = (bf16[2,256,512]{2,1,0:T(8,128)(2,1)}, bf16[2,256,512]{2,1,0:T(8,128)(2,1)}, u32[]{:S(2)}, u32[]{:S(2)}) collective-permute-start(bf16[2,256,512]{2,1,0:T(8,128)(2,1)} %get-tuple-element.75), channel_id=1, source_target_pairs={{0,9},{1,25},{2,19},{3,3},{4,13},{5,29},{6,23},{7,7}} | collective-permute-start | bytes 1572872 | tf_op jit(solution)/shard_map/ppermute | solution.py:79
  56.4 7.4 %collective-permute-start.15 = (f32[8,128]{1,0:T(8,128)S(1)}, f32[8,128]{1,0:T(8,128)S(1)}, u32[]{:S(2)}, u32[]{:S(2)}) collective-permute-start(f32[8,128]{1,0:T(8,128)S(1)} %fusion.383), channel_id=1, source_target_pairs={{0,4},{1,5},{2,6},{3,7},{4,0},{5,1},{6,2},{7,3},{8,12},{9,13},{10,... | collective-permute-start | bytes 12296 | tf_op jit(solution)/shard_map/ppermute | solution.py:79
  63.8 30.3 %collective-permute-start.12 = (f32[5,8,256]{2,1,0:T(8,128)S(1)}, f32[5,8,256]{2,1,0:T(8,128)}, u32[]{:S(2)}, u32[]{:S(2)}) collective-permute-start(f32[5,8,256]{2,1,0:T(8,128)S(1)} %pad_maximum_fusion.9), channel_id=1, source_target_pairs={{0,1},{1,0},{2,3},{3,2},{4,5},{5,4},{6,7},{7,6},{8,9},{9,8},{10,11... | collective-permute-start | bytes 122888 | tf_op jit(solution)/shard_map/ppermute | solution.py:79
  67.3 6.4 %collective-permute-start.4 = (bf16[2,128,512]{2,1,0:T(8,128)(2,1)S(1)}, bf16[2,128,512]{2,1,0:T(8,128)(2,1)S(1)}, u32[]{:S(2)}, u32[]{:S(2)}) collective-permute-start(bf16[2,128,512]{2,1,0:T(8,128)(2,1)S(1)} %copy-done.15), channel_id=1, source_target_pairs={{8,1},{9,17},{10,27},{11,11},{12,5},{13,21},{14,31},{15,15},{16,8}... | collective-permute-start | bytes 786440 | tf_op jit(solution)/shard_map/ppermute | solution.py:79
  68.0 21.2 %collective-permute-start.7 = (bf16[2,128,512]{2,1,0:T(8,128)(2,1)S(1)}, bf16[2,128,512]{2,1,0:T(8,128)(2,1)S(1)}, u32[]{:S(2)}, u32[]{:S(2)}) collective-permute-start(bf16[2,128,512]{2,1,0:T(8,128)(2,1)S(1)} %copy-done.14), channel_id=1, source_target_pairs={{8,0},{9,16},{10,26},{11,10},{12,4},{13,20},{14,30},{15,14},{16,1}... | collective-permute-start | bytes 786440 | tf_op jit(solution)/shard_map/ppermute | solution.py:79
  69.3 19.9 %collective-permute-start.6 = (bf16[2,128,512]{2,1,0:T(8,128)(2,1)S(1)}, bf16[2,128,512]{2,1,0:T(8,128)(2,1)S(1)}, u32[]{:S(2)}, u32[]{:S(2)}) collective-permute-start(bf16[2,128,512]{2,1,0:T(8,128)(2,1)S(1)} %copy-done.13), channel_id=1, source_target_pairs={{8,9},{9,25},{10,19},{11,3},{12,13},{13,29},{14,23},{15,7},{16,0},... | collective-permute-start | bytes 786440 | tf_op jit(solution)/shard_map/ppermute | solution.py:79
  70.6 18.6 %collective-permute-start.5 = (bf16[2,128,512]{2,1,0:T(8,128)(2,1)S(1)}, bf16[2,128,512]{2,1,0:T(8,128)(2,1)S(1)}, u32[]{:S(2)}, u32[]{:S(2)}) collective-permute-start(bf16[2,128,512]{2,1,0:T(8,128)(2,1)S(1)} %get-tuple-element.115), channel_id=1, source_target_pairs={{8,8},{9,24},{10,18},{11,2},{12,12},{13,28},{14,22},{15,6},{16,9},... | collective-permute-start | bytes 786440 | tf_op jit(solution)/shard_map/ppermute | solution.py:79
  90.8 15.1 %collective-permute-start.8 = (bf16[1,528,512]{2,1,0:T(8,128)(2,1)}, bf16[1,528,512]{2,1,0:T(8,128)(2,1)}, u32[]{:S(2)}, u32[]{:S(2)}) collective-permute-start(bf16[1,528,512]{2,1,0:T(8,128)(2,1)} %get-tuple-element.108), channel_id=1, source_target_pairs={{0,1},{1,8},{8,9},{9,16},{16,17},{17,24},{24,25},{25,26},{26,27},{... | collective-permute-start | bytes 1622024 | tf_op jit(solution)/shard_map/ppermute | solution.py:79
  92.9 17.5 %collective-permute-start.9 = (bf16[1,528,512]{2,1,0:T(8,128)(2,1)}, bf16[1,528,512]{2,1,0:T(8,128)(2,1)}, u32[]{:S(2)}, u32[]{:S(2)}) collective-permute-start(bf16[1,528,512]{2,1,0:T(8,128)(2,1)} %get-tuple-element.109), channel_id=1, source_target_pairs={{1,0},{8,1},{9,8},{16,9},{17,16},{24,17},{25,24},{26,25},{27,26},{... | collective-permute-start | bytes 1622024 | tf_op jit(solution)/shard_map/ppermute | solution.py:79
  98.7 33.1 %collective-permute-start.16 = (bf16[2,256,448]{1,2,0:T(8,128)(2,1)S(1)}, bf16[2,256,448]{1,2,0:T(8,128)(2,1)S(1)}, u32[]{:S(2)}, u32[]{:S(2)}) collective-permute-start(bf16[2,256,448]{1,2,0:T(8,128)(2,1)S(1)} %get-tuple-element.82), channel_id=1, source_target_pairs={{0,0},{1,16},{2,26},{3,10},{4,4},{5,20},{6,30},{7,14},{8,1},{9,17}... | collective-permute-start | bytes 1376264 | tf_op jit(solution)/shard_map/ppermute | solution.py:79
  99.4 33.7 %collective-permute-start.19 = (bf16[2,256,448]{1,2,0:T(8,128)(2,1)S(1)}, bf16[2,256,448]{1,2,0:T(8,128)(2,1)S(1)}, u32[]{:S(2)}, u32[]{:S(2)}) collective-permute-start(bf16[2,256,448]{1,2,0:T(8,128)(2,1)S(1)} %get-tuple-element.83), channel_id=1, source_target_pairs={{0,9},{1,25},{2,19},{3,3},{4,13},{5,29},{6,23},{7,7},{8,0},{9,16},... | collective-permute-start | bytes 1376264 | tf_op jit(solution)/shard_map/ppermute | solution.py:79
  105.8 35.5 %collective-permute-start.18 = (bf16[2,256,448]{1,2,0:T(8,128)(2,1)S(1)}, bf16[2,256,448]{1,2,0:T(8,128)(2,1)S(1)}, u32[]{:S(2)}, u32[]{:S(2)}) collective-permute-start(bf16[2,256,448]{1,2,0:T(8,128)(2,1)S(1)} %get-tuple-element.84), channel_id=1, source_target_pairs={{0,8},{1,24},{2,18},{3,2},{4,12},{5,28},{6,22},{7,6},{8,9},{9,25},... | collective-permute-start | bytes 1376264 | tf_op jit(solution)/shard_map/ppermute | solution.py:79
  105.9 35.4 %collective-permute-start.17 = (bf16[2,256,448]{1,2,0:T(8,128)(2,1)S(1)}, bf16[2,256,448]{1,2,0:T(8,128)(2,1)S(1)}, u32[]{:S(2)}, u32[]{:S(2)}) collective-permute-start(bf16[2,256,448]{1,2,0:T(8,128)(2,1)S(1)} %get-tuple-element.85), channel_id=1, source_target_pairs={{0,1},{1,17},{2,27},{3,11},{4,5},{5,21},{6,31},{7,15},{8,8},{9,24}... | collective-permute-start | bytes 1376264 | tf_op jit(solution)/shard_map/ppermute | solution.py:79
  127.8 27.5 %collective-permute-start.10 = (bf16[1,528,512]{2,1,0:T(8,128)(2,1)}, bf16[1,528,512]{2,1,0:T(8,128)(2,1)}, u32[]{:S(2)}, u32[]{:S(2)}) collective-permute-start(bf16[1,528,512]{2,1,0:T(8,128)(2,1)} %get-tuple-element.106), channel_id=1, source_target_pairs={{0,1},{1,8},{8,9},{9,16},{16,17},{17,24},{24,25},{25,26},{26,27},{... | collective-permute-start | bytes 1622024 | tf_op jit(solution)/shard_map/ppermute | solution.py:79
  131.9 23.4 %collective-permute-start.11 = (bf16[1,528,512]{2,1,0:T(8,128)(2,1)}, bf16[1,528,512]{2,1,0:T(8,128)(2,1)}, u32[]{:S(2)}, u32[]{:S(2)}) collective-permute-start(bf16[1,528,512]{2,1,0:T(8,128)(2,1)} %get-tuple-element.107), channel_id=1, source_target_pairs={{1,0},{8,1},{9,8},{16,9},{17,16},{24,17},{25,24},{26,25},{27,26},{... | collective-permute-start | bytes 1622024 | tf_op jit(solution)/shard_map/ppermute | solution.py:79
  186.3 5.6 collective-permute-start.26
  189.2 67.0 %collective-permute-start.25 = (bf16[4,528,512]{2,1,0:T(8,128)(2,1)}, bf16[4,528,512]{2,1,0:T(8,128)(2,1)}, u32[]{:S(2)}, u32[]{:S(2)}) collective-permute-start(bf16[4,528,512]{2,1,0:T(8,128)(2,1)} %get-tuple-element.68), channel_id=1, source_target_pairs={{0,1},{1,0},{2,3},{3,2},{4,5},{5,4},{6,7},{7,6},{8,9},{9,8},{10,11... | collective-permute-start | bytes 6488072 | tf_op jit(solution)/shard_map/ppermute | solution.py:79
  190.4 27.0 %collective-permute-start.47 = (bf16[2,256,512]{1,2,0:T(8,128)(2,1)S(1)}, bf16[2,256,512]{1,2,0:T(8,128)(2,1)S(1)}, u32[]{:S(2)}, u32[]{:S(2)}) collective-permute-start(bf16[2,256,512]{1,2,0:T(8,128)(2,1)S(1)} %get-tuple-element.186), channel_id=1, source_target_pairs={{0,1},{1,0},{2,3},{3,2},{4,5},{5,4},{6,7},{7,6},{8,9},{9,8},{10,11... | collective-permute-start | bytes 1572872 | tf_op jit(solution)/shard_map/ppermute | solution.py:79
  190.4 92.3 %collective-permute-start.37 = (bf16[4,528,512]{2,1,0:T(8,128)(2,1)}, bf16[4,528,512]{2,1,0:T(8,128)(2,1)}, u32[]{:S(2)}, u32[]{:S(2)}) collective-permute-start(bf16[4,528,512]{2,1,0:T(8,128)(2,1)} %get-tuple-element.71), channel_id=1, source_target_pairs={{0,1},{1,0},{2,3},{3,2},{4,5},{5,4},{6,7},{7,6},{8,9},{9,8},{10,11... | collective-permute-start | bytes 6488072 | tf_op jit(solution)/shard_map/ppermute | solution.py:79
  192.0 90.8 %collective-permute-start.38 = (bf16[2,528,256]{2,1,0:T(8,128)(2,1)}, bf16[2,528,256]{2,1,0:T(8,128)(2,1)}, u32[]{:S(2)}, u32[]{:S(2)}) collective-permute-start(bf16[2,528,256]{2,1,0:T(8,128)(2,1)} %get-tuple-element.105), channel_id=1, source_target_pairs={{0,1},{1,0},{2,3},{3,2},{4,5},{5,4},{6,7},{7,6},{8,9},{9,8},{10,11... | collective-permute-start | bytes 1622024 | tf_op jit(solution)/shard_map/ppermute | solution.py:79
  192.1 25.3 %collective-permute-start.48 = (bf16[2,256,896]{2,1,0:T(8,128)(2,1)S(1)}, bf16[2,256,896]{2,1,0:T(8,128)(2,1)S(1)}, u32[]{:S(2)}, u32[]{:S(2)}) collective-permute-start(bf16[2,256,896]{2,1,0:T(8,128)(2,1)S(1)} %get-tuple-element.77), channel_id=1, source_target_pairs={{0,1},{1,0},{2,3},{3,2},{4,5},{5,4},{6,7},{7,6},{8,9},{9,8},{10,11... | collective-permute-start | bytes 2752520 | tf_op jit(solution)/shard_map/ppermute | solution.py:79
  219.0 12.3 %collective-permute-start.51 = (s16[272,384]{1,0:T(8,128)(2,1)S(1)}, s16[272,384]{1,0:T(8,128)(2,1)S(1)}, u32[]{:S(2)}, u32[]{:S(2)}) collective-permute-start(s16[272,384]{1,0:T(8,128)(2,1)S(1)} %pad_add_fusion.10), channel_id=1, source_target_pairs={{0,4},{1,5},{2,6},{3,7},{4,0},{5,1},{6,2},{7,3},{8,12},{9,13},{10,... | collective-permute-start | bytes 626696 | tf_op jit(solution)/shard_map/ppermute | solution.py:79
  225.7 9.0 %collective-permute-start.49 = (s16[272,512]{1,0:T(8,128)(2,1)S(1)}, s16[272,512]{1,0:T(8,128)(2,1)S(1)}, u32[]{:S(2)}, u32[]{:S(2)}) collective-permute-start(s16[272,512]{1,0:T(8,128)(2,1)S(1)} %pad_add_fusion.9), channel_id=1, source_target_pairs={{0,2},{1,3},{2,0},{3,1},{4,6},{5,7},{6,4},{7,5},{8,10},{9,11},{10,... | collective-permute-start | bytes 835592 | tf_op jit(solution)/shard_map/ppermute | solution.py:79
  231.7 5.8 %collective-permute-start.52 = (s16[144,384]{1,0:T(8,128)(2,1)S(1)}, s16[144,384]{1,0:T(8,128)(2,1)S(1)}, u32[]{:S(2)}, u32[]{:S(2)}) collective-permute-start(s16[144,384]{1,0:T(8,128)(2,1)S(1)} %pad_add_fusion.18), channel_id=1, source_target_pairs={{0,2},{1,3},{2,0},{3,1},{4,6},{5,7},{6,4},{7,5},{8,10},{9,11},{10,... | collective-permute-start | bytes 331784 | tf_op jit(solution)/shard_map/ppermute | solution.py:79
  240.6 5.7 %collective-permute-start.54 = (s16[48,896]{1,0:T(8,128)(2,1)S(1)}, s16[48,896]{1,0:T(8,128)(2,1)S(1)}, u32[]{:S(2)}, u32[]{:S(2)}) collective-permute-start(s16[48,896]{1,0:T(8,128)(2,1)S(1)} %pad_add_fusion.20), channel_id=1, source_target_pairs={{0,16},{1,17},{2,18},{3,19},{4,20},{5,21},{6,22},{7,23},{8,24},{9,... | collective-permute-start | bytes 258056 | tf_op jit(solution)/shard_map/ppermute | solution.py:79
  240.7 6.0 %collective-permute-start.55 = (s16[48,896]{1,0:T(8,128)(2,1)S(1)}, s16[48,896]{1,0:T(8,128)(2,1)S(1)}, u32[]{:S(2)}, u32[]{:S(2)}) collective-permute-start(s16[48,896]{1,0:T(8,128)(2,1)S(1)} %pad_add_fusion.19), channel_id=1, source_target_pairs={{0,24},{1,25},{2,26},{3,27},{4,28},{5,29},{6,30},{7,31},{8,0},{9,1... | collective-permute-start | bytes 258056 | tf_op jit(solution)/shard_map/ppermute | solution.py:79
  246.3 6.7 %collective-permute-start.53 = (s16[48,896]{1,0:T(8,128)(2,1)S(1)}, s16[48,896]{1,0:T(8,128)(2,1)S(1)}, u32[]{:S(2)}, u32[]{:S(2)}) collective-permute-start(s16[48,896]{1,0:T(8,128)(2,1)S(1)} %pad_add_fusion.21), channel_id=1, source_target_pairs={{0,8},{1,9},{2,10},{3,11},{4,12},{5,13},{6,14},{7,15},{8,16},{9,17... | collective-permute-start | bytes 258056 | tf_op jit(solution)/shard_map/ppermute | solution.py:79
  278.5 27.6 %collective-permute-start.29 = (s16[2320,128]{1,0:T(8,128)(2,1)S(1)}, s16[2320,128]{1,0:T(8,128)(2,1)S(1)}, u32[]{:S(2)}, u32[]{:S(2)}) collective-permute-start(s16[2320,128]{1,0:T(8,128)(2,1)S(1)} %pad_add_fusion.4), channel_id=1, source_target_pairs={{0,2},{1,3},{2,0},{3,1},{4,6},{5,7},{6,4},{7,5},{8,10},{9,11},{10,... | collective-permute-start | bytes 1781768 | tf_op jit(solution)/shard_map/ppermute | solution.py:79
  280.7 27.0 %collective-permute-start.31 = (s16[2320,128]{1,0:T(8,128)(2,1)S(1)}, s16[2320,128]{1,0:T(8,128)(2,1)S(1)}, u32[]{:S(2)}, u32[]{:S(2)}) collective-permute-start(s16[2320,128]{1,0:T(8,128)(2,1)S(1)} %pad_add_fusion.3), channel_id=1, source_target_pairs={{0,4},{1,5},{2,6},{3,7},{4,0},{5,1},{6,2},{7,3},{8,12},{9,13},{10,... | collective-permute-start | bytes 1781768 | tf_op jit(solution)/shard_map/ppermute | solution.py:79
  304.4 35.8 %collective-permute-start.39 = (s16[2320,128]{1,0:T(8,128)(2,1)S(1)}, s16[2320,128]{1,0:T(8,128)(2,1)S(1)}, u32[]{:S(2)}, u32[]{:S(2)}) collective-permute-start(s16[2320,128]{1,0:T(8,128)(2,1)S(1)} %pad_add_fusion.2), channel_id=1, source_target_pairs={{0,2},{1,3},{2,0},{3,1},{4,6},{5,7},{6,4},{7,5},{8,10},{9,11},{10,... | collective-permute-start | bytes 1781768 | tf_op jit(solution)/shard_map/ppermute | solution.py:79
  305.0 37.3 %collective-permute-start.41 = (s16[2320,128]{1,0:T(8,128)(2,1)S(1)}, s16[2320,128]{1,0:T(8,128)(2,1)S(1)}, u32[]{:S(2)}, u32[]{:S(2)}) collective-permute-start(s16[2320,128]{1,0:T(8,128)(2,1)S(1)} %pad_add_fusion.1), channel_id=1, source_target_pairs={{0,4},{1,5},{2,6},{3,7},{4,0},{5,1},{6,2},{7,3},{8,12},{9,13},{10,... | collective-permute-start | bytes 1781768 | tf_op jit(solution)/shard_map/ppermute | solution.py:79
  306.8 19.3 %collective-permute-start.30 = (s16[1168,128]{1,0:T(8,128)(2,1)S(1)}, s16[1168,128]{1,0:T(8,128)(2,1)S(1)}, u32[]{:S(2)}, u32[]{:S(2)}) collective-permute-start(s16[1168,128]{1,0:T(8,128)(2,1)S(1)} %pad_add_fusion.8), channel_id=1, source_target_pairs={{0,4},{1,5},{2,6},{3,7},{4,0},{5,1},{6,2},{7,3},{8,12},{9,13},{10,... | collective-permute-start | bytes 897032 | tf_op jit(solution)/shard_map/ppermute | solution.py:79
  308.3 18.0 %collective-permute-start.32 = (s16[1168,128]{1,0:T(8,128)(2,1)S(1)}, s16[1168,128]{1,0:T(8,128)(2,1)S(1)}, u32[]{:S(2)}, u32[]{:S(2)}) collective-permute-start(s16[1168,128]{1,0:T(8,128)(2,1)S(1)} %pad_add_fusion.7), channel_id=1, source_target_pairs={{0,2},{1,3},{2,0},{3,1},{4,6},{5,7},{6,4},{7,5},{8,10},{9,11},{10,... | collective-permute-start | bytes 897032 | tf_op jit(solution)/shard_map/ppermute | solution.py:79
  326.8 6.6 %collective-permute-start.35 = (s16[304,256]{1,0:T(8,128)(2,1)S(1)}, s16[304,256]{1,0:T(8,128)(2,1)S(1)}, u32[]{:S(2)}, u32[]{:S(2)}) collective-permute-start(s16[304,256]{1,0:T(8,128)(2,1)S(1)} %pad_add_fusion.14), channel_id=1, source_target_pairs={{0,24},{1,25},{2,26},{3,27},{4,28},{5,29},{6,30},{7,31},{8,0},{9,1... | collective-permute-start | bytes 466952 | tf_op jit(solution)/shard_map/ppermute | solution.py:79
  327.0 12.8 %collective-permute-start.34 = (s16[304,256]{1,0:T(8,128)(2,1)S(1)}, s16[304,256]{1,0:T(8,128)(2,1)S(1)}, u32[]{:S(2)}, u32[]{:S(2)}) collective-permute-start(s16[304,256]{1,0:T(8,128)(2,1)S(1)} %pad_add_fusion.15), channel_id=1, source_target_pairs={{0,16},{1,17},{2,18},{3,19},{4,20},{5,21},{6,22},{7,23},{8,24},{9,... | collective-permute-start | bytes 466952 | tf_op jit(solution)/shard_map/ppermute | solution.py:79
  327.1 12.8 %collective-permute-start.33 = (s16[304,256]{1,0:T(8,128)(2,1)S(1)}, s16[304,256]{1,0:T(8,128)(2,1)S(1)}, u32[]{:S(2)}, u32[]{:S(2)}) collective-permute-start(s16[304,256]{1,0:T(8,128)(2,1)S(1)} %pad_add_fusion.16), channel_id=1, source_target_pairs={{0,8},{1,9},{2,10},{3,11},{4,12},{5,13},{6,14},{7,15},{8,16},{9,17... | collective-permute-start | bytes 466952 | tf_op jit(solution)/shard_map/ppermute | solution.py:79
  340.1 29.4 %collective-permute-start.36 = (f32[9,16,256]{2,1,0:T(8,128)S(1)}, f32[9,16,256]{2,1,0:T(8,128)S(1)}, u32[]{:S(2)}, u32[]{:S(2)}) collective-permute-start(f32[9,16,256]{2,1,0:T(8,128)S(1)} %dynamic-slice_bitcast_fusion.4), channel_id=1, source_target_pairs={{0,1},{1,0},{2,3},{3,2},{4,5},{5,4},{6,7},{7,6},{8,9},{9,8},{10,11... | collective-permute-start | bytes 442376 | tf_op jit(solution)/shard_map/ppermute | solution.py:79
  340.8 9.6 %collective-permute-start.40 = (s16[1168,128]{1,0:T(8,128)(2,1)S(1)}, s16[1168,128]{1,0:T(8,128)(2,1)S(1)}, u32[]{:S(2)}, u32[]{:S(2)}) collective-permute-start(s16[1168,128]{1,0:T(8,128)(2,1)S(1)} %pad_add_fusion.6), channel_id=1, source_target_pairs={{0,4},{1,5},{2,6},{3,7},{4,0},{5,1},{6,2},{7,3},{8,12},{9,13},{10,... | collective-permute-start | bytes 897032 | tf_op jit(solution)/shard_map/ppermute | solution.py:79
  342.9 9.3 %collective-permute-start.42 = (s16[1168,128]{1,0:T(8,128)(2,1)S(1)}, s16[1168,128]{1,0:T(8,128)(2,1)S(1)}, u32[]{:S(2)}, u32[]{:S(2)}) collective-permute-start(s16[1168,128]{1,0:T(8,128)(2,1)S(1)} %pad_add_fusion.5), channel_id=1, source_target_pairs={{0,2},{1,3},{2,0},{3,1},{4,6},{5,7},{6,4},{7,5},{8,10},{9,11},{10,... | collective-permute-start | bytes 897032 | tf_op jit(solution)/shard_map/ppermute | solution.py:79
  353.5 15.7 %collective-permute-start.44 = (s16[304,256]{1,0:T(8,128)(2,1)S(1)}, s16[304,256]{1,0:T(8,128)(2,1)S(1)}, u32[]{:S(2)}, u32[]{:S(2)}) collective-permute-start(s16[304,256]{1,0:T(8,128)(2,1)S(1)} %pad_add_fusion.12), channel_id=1, source_target_pairs={{0,16},{1,17},{2,18},{3,19},{4,20},{5,21},{6,22},{7,23},{8,24},{9,... | collective-permute-start | bytes 466952 | tf_op jit(solution)/shard_map/ppermute | solution.py:79
  355.8 13.4 %collective-permute-start.43 = (s16[304,256]{1,0:T(8,128)(2,1)S(1)}, s16[304,256]{1,0:T(8,128)(2,1)S(1)}, u32[]{:S(2)}, u32[]{:S(2)}) collective-permute-start(s16[304,256]{1,0:T(8,128)(2,1)S(1)} %pad_add_fusion.13), channel_id=1, source_target_pairs={{0,8},{1,9},{2,10},{3,11},{4,12},{5,13},{6,14},{7,15},{8,16},{9,17... | collective-permute-start | bytes 466952 | tf_op jit(solution)/shard_map/ppermute | solution.py:79
  377.0 24.2 %all-to-all-start = ((s16[32,48,256]{2,1,0:T(8,128)(2,1)}), s16[32,48,256]{2,1,0:T(8,128)(2,1)S(1)}, u32[]{:S(2)}, u32[]{:S(2)}) async-start(s16[32,48,256]{2,1,0:T(8,128)(2,1)} %pad.111), calls=%async_computation | async-start | bytes 1572864 | tf_op jit(solution)/shard_map/all_to_all | solution.py:491
  379.6 149.8 %all-gather.2.cloned.1.call-start = ((), (), s32[]{:S(2)}) async-start(), calls=%async_computation.1 | async-start | bytes 17301504 | tf_op jit(solution)/shard_map/all_gather | solution.py:539
  394.4 6.2 %collective-permute-start.24 = (f32[24,128]{1,0:T(8,128)S(1)}, f32[24,128]{1,0:T(8,128)S(1)}, u32[]{:S(2)}, u32[]{:S(2)}) collective-permute-start(f32[24,128]{1,0:T(8,128)S(1)} %add.889), channel_id=1, source_target_pairs={{0,16},{1,17},{2,18},{3,19},{4,20},{5,21},{6,22},{7,23},{8,24},{9,... | collective-permute-start | bytes 36872 | tf_op jit(solution)/shard_map/ppermute | solution.py:79
  (48 other events, 703.2 us)
Sparse Core Ops, SparseCore 0:
  413.9 115.4 all-gather.1

commit v2 on v1

v2 whole, which is shorter than its diff:
```python
import jax
import jax.numpy as jnp
from jax import lax
from jax.experimental import pallas as pl
from jax.experimental.pallas import tpu as pltpu
from jax.sharding import PartitionSpec as P

STEP = 5

beta_one = 0.5
beta_two = 0.5
adam_eps = 1e-08
rate_matrix = 0.01
rate_vector = 0.2
weight_decay = 0.01
clip_level = 0.001
box_weight = 2.0
norm_eps = 1e-05
highest = lax.Precision.HIGHEST
bf16 = jnp.bfloat16
f32 = jnp.float32
AXES = ("scale", "img")
GAP = 16
CODE = 32767.0
VMEM_BYTES = 56 * 2**20


class Layout:
    def __init__(self, scales, imgs):
        self.scales = scales
        self.imgs = imgs

    def pos(self, group, scale):
        return scale if group % 2 == 0 else self.scales - 1 - scale

    def dev(self, scale, img):
        return scale * self.imgs + img

    def at(self, group, place, core):
        return self.dev(self.pos(group, place), 2 * group + core)

    def all_devices(self):
        return [(s, i) for s in range(self.scales) for i in range(self.imgs)]

    def swap(self, bit):
        return [(self.dev(s, i), self.dev(s, i ^ bit)) for s, i in self.all_devices()]

    def turn(self, step):
        return [
            (self.dev(s, i), self.dev((s + step) % self.scales, i)) for s, i in self.all_devices()
        ]

    def scale_swap(self, bit):
        return [(self.dev(s, i), self.dev(s ^ bit, i)) for s, i in self.all_devices()]

    def rows_round(self, shift, sources):
        pairs = []
        for s in sources:
            for i in range(self.imgs):
                group, core = i // 2, i % 2
                piece = (shift + s) % self.scales
                place = (self.scales // 2) * core + piece // 2
                pairs.append((self.dev(s, i), self.at(group, place, piece % 2)))
        return pairs

    def row_order(self):
        groups = self.imgs // 2
        return [
            self.at(j, place, c) for j in range(groups) for place in range(self.scales) for c in range(2)
        ]

    def outward(self):
        order = self.row_order()
        pairs = []
        for at in range(1, len(order) - 1, 2):
            pairs += [(order[at], order[at + 1]), (order[at + 1], order[at])]
        return pairs


def permute(value, pairs):
    return lax.ppermute(value, AXES, pairs)


def after(value, *others):
    return lax.optimization_barrier((value, *others))[0]


def table_kernel(starts, widths, width, cols_ref, up_high, up_low, down_high, down_low):
    def table(shape, coarse_axis):
        place = lax.broadcasted_iota(jnp.int32, shape, coarse_axis)
        fine = lax.broadcasted_iota(jnp.int32, shape, 1 - coarse_axis)
        total = jnp.zeros(shape, f32)
        bits = (2 * width).bit_length() - 1
        for s, (start, span) in enumerate(zip(starts, widths)):
            columns = cols_ref[s]
            numer = jnp.maximum((2 * fine + 1) * columns - width, 0)
            lower = lax.shift_right_logical(numer, bits)
            frac = (numer - lax.shift_left(lower, bits)).astype(f32) * (0.5 / width)
            upper = jnp.minimum(lower + 1, columns - 1)
            coarse = place - start
            inside = (coarse >= 0) & (coarse < span)
            part = jnp.where(coarse == lower, 1.0 - frac, 0.0) + jnp.where(coarse == upper, frac, 0.0)
            total += jnp.where(inside, part, 0.0)
        return halves(total)

    up_high[...], up_low[...] = table(up_high.shape, 1)
    down_high[...], down_low[...] = table(down_high.shape, 0)


def table_call(scale_cols, starts, widths, width, cols):
    vmem = pl.BlockSpec(memory_space=pltpu.VMEM)
    return pl.pallas_call(
        lambda *refs: table_kernel(starts, widths, width, *refs),
        in_specs=[pl.BlockSpec(memory_space=pltpu.SMEM)],
        out_specs=[vmem] * 4,
        out_shape=[jax.ShapeDtypeStruct((width, cols), bf16)] * 2
        + [jax.ShapeDtypeStruct((cols, width), bf16)] * 2,
        name="tables",
    )(scale_cols)


def halves(value):
    high = value.astype(bf16)
    return high, (value - high.astype(f32)).astype(bf16)


def whole(shape):
    return pl.BlockSpec(shape, lambda *_: (0,) * len(shape))


def spread_taps(store, at, row, cols, chans):
    base = pl.multiple_of(at * cols, 16)
    value = row.astype(f32)
    store[pl.ds(base, cols), pl.ds(0, chans)] = pltpu.roll(value, 1, 0).astype(bf16)
    store[pl.ds(base, cols), pl.ds(chans, chans)] = row
    store[pl.ds(base, cols), pl.ds(2 * chans, chans)] = pltpu.roll(value, cols - 1, 0).astype(bf16)


def load_taps(rows, cols, chans, core, cur, partner, outer, taps):
    for r in range(rows):
        spread_taps(taps, r + 1, cur[pl.ds(r * cols, cols), :], cols, chans)
    outside = (rows + 1) * core
    spread_taps(taps, outside, outer[...], cols, chans)
    inside = pl.multiple_of((rows - 1) * core * cols, 16)
    spread_taps(taps, rows + 1 - outside, partner[pl.ds(inside, cols), :], cols, chans)


def fetch(source, layer, target, sems):
    copies = [pltpu.make_async_copy(source.at[layer, a], target.at[a], sems.at[a]) for a in range(3)]
    for copy in copies:
        copy.start()
    return copies


def conv_into(pre, taps, weights, copies, cols):
    size = pre.shape[0]
    for a in range(3):
        copies[a].wait()
        value = jnp.dot(taps[pl.ds(a * cols, size), :], weights[a], preferred_element_type=f32)
        if a == 0:
            pre[...] = value
        else:
            pre[...] += value


def gelu_slope(u):
    root = 0.7978845608028654
    bend = 0.044715
    th = jnp.tanh(root * (u + bend * u * u * u))
    return 0.5 * (1.0 + th) + 0.5 * u * (1.0 - th * th) * root * (1.0 + 3.0 * bend * u * u)


def first_conv_kernel(
    rows, cols, chans, layer, core_ref, cur, partner, outer, gain, shift, mask, w_hbm, pre, out, taps, w, sems
):
    copies = fetch(w_hbm, layer, w, sems)
    load_taps(rows, cols, chans, core_ref[0], cur, partner, outer, taps)
    out[pl.ds(0, cols), :] = outer[...]
    conv_into(pre, taps, w, copies, cols)

    def body(i, carry):
        at = pl.ds(pl.multiple_of(i * 32, 32), 32)
        u = pre[at, :] * gain[...] + shift[...]
        to = pl.ds(pl.multiple_of(cols + i * 32, 32), 32)
        out[to, :] = (jax.nn.gelu(u) * mask[at, :]).astype(bf16)
        return carry

    lax.fori_loop(0, rows * cols // 32, body, 0)


def back_conv_kernel(
    rows, cols, chans, layer, core_ref, cur, partner, outer, gain, shift, mask, pre_in, w_hbm, out, taps, w, sems, acc
):
    copies = fetch(w_hbm, layer, w, sems)
    size = rows * cols
    cur = cur.at[pl.ds(cols, size)]
    partner = partner.at[pl.ds(cols, size)]
    load_taps(rows, cols, chans, core_ref[0], cur, partner, outer, taps)
    for a in range(3):
        copies[2 - a].wait()
        value = 0.0
        for b in range(3):
            value += lax.dot_general(
                taps[pl.ds(a * cols, size), b * chans : (b + 1) * chans],
                w[2 - a, (2 - b) * chans : (3 - b) * chans, :],
                (((1,), (1,)), ((), ())),
                preferred_element_type=f32,
            )
        if a == 0:
            acc[...] = value
        else:
            acc[...] += value

    def body(i, carry):
        at = pl.ds(pl.multiple_of(i * 32, 32), 32)
        u = pre_in[at, :] * gain[...] + shift[...]
        out[at, :] = (acc[at, :] * mask[at, :] * gelu_slope(u) * gain[...]).astype(bf16)
        return carry

    lax.fori_loop(0, size // 32, body, 0)


def conv_call(kernel, core, cur, partner, outer, gain, shift, mask, more, weights, layer, shapes, acc, name):
    cols, chans = outer.shape
    rows = 2
    size = rows * cols
    scratch = [
        pltpu.VMEM(((rows + 2) * cols, 3 * chans), bf16),
        pltpu.VMEM((3, 3 * chans, chans), bf16),
        pltpu.SemaphoreType.DMA((3,)),
    ]
    if acc:
        scratch.append(pltpu.VMEM((size, chans), f32))
    vmem = pl.BlockSpec(memory_space=pltpu.VMEM)
    return pl.pallas_call(
        lambda *refs: kernel(rows, cols, chans, layer, *refs),
        in_specs=[pl.BlockSpec(memory_space=pltpu.SMEM)]
        + [vmem] * (6 + len(more))
        + [pl.BlockSpec(memory_space=pl.ANY)],
        out_specs=[vmem for _ in shapes],
        out_shape=shapes,
        scratch_shapes=scratch,
        compiler_params=pltpu.CompilerParams(vmem_limit_bytes=VMEM_BYTES),
        cost_estimate=pl.CostEstimate(flops=1, bytes_accessed=1, transcendentals=0),
        name=name,
    )(core, cur, partner, outer, gain, shift, mask, *more, weights)


def head_kernel(
    rows,
    cols,
    width,
    scales,
    layer,
    core_ref,
    mine_ref,
    cur,
    partner,
    outer,
    gain,
    shift,
    mask,
    gamma,
    bias,
    weight,
    valid,
    normals,
    heads_hbm,
    first_hbm,
    second_hbm,
    third_hbm,
    fourth_hbm,
    up_high_hbm,
    up_low_hbm,
    down_high_hbm,
    down_low_hbm,
    w_hbm,
    out,
    mine,
    pack,
    dgamma,
    dbias,
    sums,
    taps,
    w,
    sems,
    pre,
    y_ref,
    tapped,
    raised_high,
    raised_low,
    dj_low,
    back,
    target,
    heads,
    target_in,
    up_high,
    up_low,
    down_high,
    down_low,
    more_sems,
    target_sems,
):
    chans = outer.shape[1]
    size = rows * cols
    core = core_ref[0]
    copies = fetch(w_hbm, layer, w, sems)
    pairs = (
        (up_high_hbm, up_high),
        (up_low_hbm, up_low),
        (heads_hbm, heads),
        (down_high_hbm, down_high),
        (down_low_hbm, down_low),
    )
    loads = [pltpu.make_async_copy(a, b, more_sems.at[i]) for i, (a, b) in enumerate(pairs)]
    for load in loads:
        load.start()
    arrived = (first_hbm, second_hbm, third_hbm, fourth_hbm)
    for s in range(scales):
        for k in range(scales):

            @pl.when(lax.rem(mine_ref[0] - s - k + 2 * scales, scales) == 0)
            def _(s=s, k=k):
                pltpu.make_async_copy(arrived[k], target_in.at[s], target_sems.at[s]).start()

    cur = cur.at[pl.ds(cols, size)]
    partner = partner.at[pl.ds(cols, size)]
    load_taps(rows, cols, chans, core, cur, partner, outer, taps)
    out[pl.ds(0, cols), :] = outer[...]
    conv_into(pre, taps, w, copies, cols)

    def forward(i, carry):
        at = pl.ds(pl.multiple_of(i * 32, 32), 32)
        u = pre[at, :] * gain[...] + shift[...]
        y = jax.nn.gelu(u) * mask[at, :]
        y_ref[at, :] = y
        scale = lax.rsqrt(jnp.mean(y * y, -1, keepdims=True) + norm_eps)
        tapped[at, :] = (gamma[...] * y * scale).astype(bf16)
        return carry

    lax.fori_loop(0, size // 32, forward, 0)
    for load in loads:
        load.wait()
    for s in range(scales):
        pltpu.make_async_copy(arrived[s], target_in.at[s], target_sems.at[s]).wait()
    part = target_in.shape[2]
    for s in range(scales):
        target[:, s * part : (s + 1) * part] = target_in[s]

    half_wide = mine.shape[1]
    for r in range(rows):
        line = tapped[pl.ds(r * cols, cols), :]
        value = jnp.dot(up_high[...], line, preferred_element_type=f32)
        value += jnp.dot(up_low[...], line, preferred_element_type=f32)
        high = value.astype(bf16)
        raised_high[pl.ds(r * width, width), :] = high
        pack[pl.ds(r * width, width), pl.ds(half_wide, chans)] = high
        raised_low[pl.ds(r * width, width), :] = (value - high.astype(f32)).astype(bf16)

    step = heads.shape[2]
    wide = heads.shape[0] * step
    dense = jnp.zeros((1, step), f32)
    normal = jnp.zeros((1, 1), f32)
    for t in range(wide // step):
        joined = jnp.dot(raised_high[...], heads[t], preferred_element_type=f32)
        joined += jnp.dot(raised_low[...], heads[t], preferred_element_type=f32)
        joined += float(scales) * bias[:, t * step : (t + 1) * step]
        diff = joined - target[:, t * step : (t + 1) * step].astype(f32)
        pulled = weight[...] * diff
        dense += jnp.sum(pulled * diff, 0, keepdims=True)
        grad = pulled * (1.0 / wide)
        if t == 0:
            lane = lax.broadcasted_iota(jnp.int32, (joined.shape[0], 128), 1)
            n = jnp.where(lane < 3, joined[:, :128], 0.0)
            other = normals[...]
            inner = jnp.sum(n * other, -1, keepdims=True)
            own_sq = jnp.sum(n * n, -1, keepdims=True) + 1.0
            other_sq = jnp.sum(other * other, -1, keepdims=True) + 1.0
            root = lax.rsqrt(own_sq * other_sq)
            normal += jnp.sum(valid[...] * (1.0 - inner * root), 0, keepdims=True)
            turn = valid[...] * root * (inner / own_sq * n - other)
            grad = jnp.concatenate([grad[:, :128] + turn, grad[:, 128:]], 1)
        dbias[:, t * step : (t + 1) * step] = float(scales) * jnp.sum(grad, 0, keepdims=True)
        dj_low[:, t * step : (t + 1) * step] = grad.astype(bf16)
        half = step // 2
        first, second = grad[:, :half], grad[:, half:]
        mine[:, t * half : (t + 1) * half] = jnp.where(core == 0, first, second).astype(bf16)
        pack[:, t * half : (t + 1) * half] = jnp.where(core == 0, second, first).astype(bf16)
    lane = lax.broadcasted_iota(jnp.int32, (1, 128), 1)
    total = 0.5 * jnp.sum(dense, 1, keepdims=True)
    sums[...] = jnp.where(lane == 0, total, jnp.where(lane == 1, normal, 0.0))

    draised = 0.0
    for t in range(heads.shape[0]):
        draised += lax.dot_general(
            dj_low[:, t * step : (t + 1) * step],
            heads[t],
            (((1,), (1,)), ((), ())),
            preferred_element_type=f32,
        )
    for r in range(rows):
        part = draised[r * width : (r + 1) * width]
        high = part.astype(bf16)
        low = (part - high.astype(f32)).astype(bf16)
        value = jnp.dot(down_high[...], high, preferred_element_type=f32)
        value += jnp.dot(down_low[...], high, preferred_element_type=f32)
        value += jnp.dot(down_high[...], low, preferred_element_type=f32)
        back[pl.ds(r * cols, cols), :] = value

    def backward(i, carry):
        at = pl.ds(pl.multiple_of(i * 32, 32), 32)
        y = y_ref[at, :]
        dt = back[at, :]
        scale = lax.rsqrt(jnp.mean(y * y, -1, keepdims=True) + norm_eps)
        dty = dt * y
        pull = jnp.mean(gamma[...] * dty, -1, keepdims=True)
        dy = gamma[...] * dt * scale - y * (scale * scale * scale * pull)
        u = pre[at, :] * gain[...] + shift[...]
        to = pl.ds(pl.multiple_of(cols + i * 32, 32), 32)
        out[to, :] = (dy * mask[at, :] * gelu_slope(u) * gain[...]).astype(bf16)
        return carry + jnp.sum(dty * scale, 0, keepdims=True)

    dgamma[...] = lax.fori_loop(0, size // 32, backward, jnp.zeros((1, chans), f32))


def head_call(core, mine, cur, partner, outer, vectors, pixel, heads, target, tables, weights, layer):
    cols, chans = outer.shape
    rows = 2
    size = rows * cols
    width = tables[0].shape[0]
    wide = heads.shape[0] * heads.shape[2]
    pixels = rows * width
    scales = len(target)
    vmem = pl.BlockSpec(memory_space=pltpu.VMEM)
    anywhere = pl.BlockSpec(memory_space=pl.ANY)
    shapes = [
        jax.ShapeDtypeStruct((size + cols, chans), bf16),
        jax.ShapeDtypeStruct((pixels, wide // 2), bf16),
        jax.ShapeDtypeStruct((pixels, wide // 2 + chans), bf16),
        jax.ShapeDtypeStruct((1, chans), f32),
        jax.ShapeDtypeStruct((1, wide), f32),
        jax.ShapeDtypeStruct((1, 128), f32),
    ]
    return pl.pallas_call(
        lambda *refs: head_kernel(rows, cols, width, scales, layer, *refs),
        in_specs=[pl.BlockSpec(memory_space=pltpu.SMEM)] * 2 + [vmem] * 11 + [anywhere] * (6 + scales),
        out_specs=[vmem for _ in shapes],
        out_shape=shapes,
        scratch_shapes=[
            pltpu.VMEM(((rows + 2) * cols, 3 * chans), bf16),
            pltpu.VMEM((3, 3 * chans, chans), bf16),
            pltpu.SemaphoreType.DMA((3,)),
            pltpu.VMEM((size, chans), f32),
            pltpu.VMEM((size, chans), f32),
            pltpu.VMEM((size, chans), bf16),
            pltpu.VMEM((pixels, chans), bf16),
            pltpu.VMEM((pixels, chans), bf16),
            pltpu.VMEM((pixels, wide), bf16),
            pltpu.VMEM((size, chans), f32),
            pltpu.VMEM((pixels, wide), bf16),
            pltpu.VMEM(heads.shape, bf16),
            pltpu.VMEM((scales, *target[0].shape), bf16),
        ]
        + [pltpu.VMEM(table.shape, bf16) for table in tables]
        + [pltpu.SemaphoreType.DMA((5,)), pltpu.SemaphoreType.DMA((scales,))],
        compiler_params=pltpu.CompilerParams(vmem_limit_bytes=VMEM_BYTES),
        cost_estimate=pl.CostEstimate(flops=1, bytes_accessed=1, transcendentals=0),
        name="head_rows",
    )(core, mine, cur, partner, outer, *vectors, *pixel, heads, *target, *tables, weights)


def kernel_grad_kernel(
    rows, cols, chans, part, x_at, g_at, core_ref, cur, partner, outer, far, g_own, g_far, out, taps, grads
):
    step = pl.program_id(0)
    core = core_ref[0]
    size = rows * cols

    @pl.when(step == 0)
    def _():
        own_at = 1 + rows * core
        far_at = 1 + rows * (1 - core)
        for r in range(rows):
            at = pl.ds(x_at + r * cols, cols)
            spread_taps(taps, own_at + r, cur[at, :], cols, chans)
            spread_taps(taps, far_at + r, partner[at, :], cols, chans)
        spread_taps(taps, (2 * rows + 1) * core, outer[...], cols, chans)
        spread_taps(taps, (2 * rows + 1) * (1 - core), far[...], cols, chans)
        for h in range(grads.shape[1] // part):
            lanes = pl.ds(pl.multiple_of((2 * h + core) * part, part), part)
            own_rows = pl.ds(pl.multiple_of(core * size, 16), size)
            far_rows = pl.ds(pl.multiple_of((1 - core) * size, 16), size)
            grads[own_rows, h * part : (h + 1) * part] = g_own[pl.ds(g_at, size), lanes]
            grads[far_rows, h * part : (h + 1) * part] = g_far[pl.ds(g_at, size), lanes]

    window = taps[pl.ds(pl.multiple_of(step * cols, 16), 2 * size), :]
    value = lax.dot_general(
        grads[...], window, (((0,), (0,)), ((), ())), preferred_element_type=f32
    )
    for b in range(3):
        out[b] = value[:, b * chans : (b + 1) * chans]


def kernel_grad(core, cur, partner, outer, far, g_own, g_far, part):
    cols, chans = outer.shape
    rows = 2
    size = rows * cols
    outs = g_own.shape[1] // 2
    x_at, g_at = cur.shape[0] - size, g_own.shape[0] - size
    return pl.pallas_call(
        lambda *refs: kernel_grad_kernel(rows, cols, chans, part, x_at, g_at, *refs),
        grid=(3,),
        in_specs=[
            pl.BlockSpec(memory_space=pltpu.SMEM),
            whole(cur.shape),
            whole(cur.shape),
            whole((cols, chans)),
            pl.BlockSpec((cols, chans), lambda i: (0, 0)),
            whole(g_own.shape),
            whole(g_own.shape),
        ],
        out_specs=pl.BlockSpec((3, outs, chans), lambda i: (i, 0, 0)),
        out_shape=jax.ShapeDtypeStruct((9, outs, chans), f32),
        scratch_shapes=[
            pltpu.VMEM(((2 * rows + 2) * cols, 3 * chans), bf16),
            pltpu.VMEM((2 * size, outs), bf16),
        ],
        compiler_params=pltpu.CompilerParams(vmem_limit_bytes=VMEM_BYTES),
        cost_estimate=pl.CostEstimate(flops=1, bytes_accessed=1, transcendentals=0),
        name="kernel_grad",
    )(core, cur, partner, outer, far, g_own, g_far)


def head_grad_kernel(mine, own, got, out):
    half = mine.shape[1]
    dims = (((0,), (0,)), ((), ()))
    value = lax.dot_general(mine[...], own[:, half:], dims, preferred_element_type=f32)
    out[...] = value + lax.dot_general(
        got[:, :half], got[:, half:], dims, preferred_element_type=f32
    )


def head_grad_call(mine, own, got):
    vmem = pl.BlockSpec(memory_space=pltpu.VMEM)
    half = mine.shape[1]
    chans = own.shape[1] - half
    return pl.pallas_call(
        head_grad_kernel,
        in_specs=[vmem] * 3,
        out_specs=vmem,
        out_shape=jax.ShapeDtypeStruct((half, chans), f32),
        compiler_params=pltpu.CompilerParams(vmem_limit_bytes=VMEM_BYTES),
        cost_estimate=pl.CostEstimate(flops=1, bytes_accessed=1, transcendentals=0),
        name="head_grad",
    )(mine, own, got)


def coded(value):
    top = jnp.max(jnp.abs(value), 0, keepdims=True)
    power = jnp.clip(jnp.ceil(jnp.log2(top)), -100.0, 110.0)
    codes = jnp.clip(jnp.round(value * (jnp.exp2(-power) * CODE)), -CODE, CODE)
    return codes.astype(jnp.int32), power.astype(jnp.int32)


def route_kernel(devices, here, block_of, blocks, out):
    lanes = 128
    groups = blocks.shape[2] // lanes
    unit = groups * blocks.shape[1]
    total = jnp.zeros(blocks.shape[1:], f32)
    for b in range(blocks.shape[0]):
        total += blocks[b] * blocks[b]
    squares = jnp.maximum(jnp.sum(jnp.sum(total, 0, keepdims=True), 1, keepdims=True), 1e-37)
    sq_pow = jnp.floor(jnp.log2(squares))
    mant = squares * jnp.exp2(-sq_pow) * 8192.0
    mant_high = jnp.floor(mant)
    mant_low = jnp.floor((mant - mant_high) * 16384.0)
    row = lax.broadcasted_iota(jnp.int32, (16, lanes), 0)
    lane = lax.broadcasted_iota(jnp.int32, (16, lanes), 1)
    base = jnp.where(lane == 0, sq_pow, jnp.where(lane == 1, mant_high, mant_low)).astype(jnp.int32)
    base = jnp.where(row == here, base, 0)

    def body(d, carry):
        tail = base
        for k in range(here):
            b = block_of[here * d + k]
            value = blocks[jnp.maximum(b, 0)] * (b >= 0).astype(f32)
            value = jnp.concatenate(
                [value[:, g * lanes : (g + 1) * lanes] for g in range(groups)], 0
            )
            codes, power = coded(value)
            out[d, pl.ds(k * unit, unit), :] = codes.astype(jnp.int16)
            tail = jnp.where(row == k, power, tail)
        out[d, pl.ds(here * unit, 16), :] = tail.astype(jnp.int16)
        return carry

    lax.fori_loop(0, devices, body, 0, unroll=4)


def route_call(blocks, block_of, devices):
    here = block_of.shape[0] // devices
    rows = here * blocks.shape[1] * blocks.shape[2] // 128 + 16
    vmem = pl.BlockSpec(memory_space=pltpu.VMEM)
    return pl.pallas_call(
        lambda *refs: route_kernel(devices, here, *refs),
        in_specs=[pl.BlockSpec(memory_space=pltpu.SMEM), vmem],
        out_specs=vmem,
        out_shape=jax.ShapeDtypeStruct((devices, rows, 128), jnp.int16),
        compiler_params=pltpu.CompilerParams(vmem_limit_bytes=VMEM_BYTES),
        name="route",
    )(block_of, blocks)


def dot_split(a, b, dims):
    dims = (dims, ((), ()))
    value = lax.dot_general(a[0], b[0], dims, preferred_element_type=f32)
    value += lax.dot_general(a[1], b[0], dims, preferred_element_type=f32)
    return value + lax.dot_general(a[0], b[1], dims, preferred_element_type=f32)


def update_kernel(
    starts, scalars, got, master, moment, second, left, right, master_new, moment_new, second_new, fresh, norm, grads, sums
):
    here, chans, half = master.shape
    lanes = 128
    groups = chans // lanes
    unit = (got.shape[1] - 16) // here
    fine = unit // groups
    for d, start in enumerate(starts):
        tail = got[d, pl.ds(here * unit, 16), :].astype(jnp.int32).astype(f32)
        sums[pl.ds(d, 1), :] = tail[here : here + 1]
        for k in range(here):
            value = got[d, pl.ds(k * unit, unit), :].astype(jnp.int32).astype(f32)
            value = value * (jnp.exp2(tail[k : k + 1]) * (1.0 / CODE))
            for g in range(groups):
                grads[k, pl.ds(start, fine), g * lanes : (g + 1) * lanes] = value[g * fine : (g + 1) * fine]
    rows = sums[...]
    lane = lax.broadcasted_iota(jnp.int32, rows.shape, 1)

    def column(index):
        return jnp.sum(jnp.where(lane == index, rows, 0.0), 1, keepdims=True)

    squares = (column(1) + column(2) * (1.0 / 16384.0)) * (1.0 / 8192.0) * jnp.exp2(column(0))
    squares = jnp.sum(squares, 0, keepdims=True) + scalars[0]
    grad_norm = jnp.sqrt(squares) / scalars[1]
    factor = clip_level / jnp.maximum(grad_norm, clip_level) / scalars[1]
    place = lax.broadcasted_iota(jnp.int32, (1, lanes), 1)
    norm[...] = jnp.where(place == 0, grad_norm, factor)
    for k in range(here):
        side = halves(left[k])
        other = halves(right[k])
        turned = dot_split(side, halves(grads[k]), ((0,), (1,)))
        turned = dot_split(halves(turned), other, ((1,), (0,))) * factor
        first = beta_one * moment[k] + (1.0 - beta_one) * turned
        spread = beta_two * second[k] + (1.0 - beta_two) * turned * turned
        moment_new[k] = first
        second_new[k] = spread
        ratio = (first / (1.0 - beta_one**STEP)) / (jnp.sqrt(spread / (1.0 - beta_two**STEP)) + adam_eps)
        back = dot_split(side, halves(ratio), ((1,), (0,)))
        back = dot_split(halves(back), other, ((1,), (1,)))
        value = master[k] - rate_matrix * (back + weight_decay * master[k])
        master_new[k] = value
        fresh[k] = value.astype(bf16)


def update_call(scalars, got, starts, master, moment, second, left, right):
    vmem = pl.BlockSpec(memory_space=pltpu.VMEM)
    here, chans, half = master.shape
    like = jax.ShapeDtypeStruct(master.shape, f32)
    return pl.pallas_call(
        lambda *refs: update_kernel(starts, *refs),
        in_specs=[pl.BlockSpec(memory_space=pltpu.SMEM)] + [vmem] * 6,
        out_specs=[vmem] * 5,
        out_shape=[
            like,
            like,
            like,
            jax.ShapeDtypeStruct(master.shape, bf16),
            jax.ShapeDtypeStruct((1, 128), f32),
        ],
        scratch_shapes=[
            pltpu.VMEM((here, half, chans), f32),
            pltpu.VMEM((len(starts), 128), f32),
        ],
        compiler_params=pltpu.CompilerParams(vmem_limit_bytes=VMEM_BYTES),
        name="update",
    )(scalars, got, master, moment, second, left, right)


def place_kernel(depth, taps, half, arrays, array, item, *refs):
    sources = refs[:arrays]
    conv, head, conv_store, head_store, in_sems, out_sems = refs[arrays:]
    blocks = array.shape[0]
    count = 2 * depth * taps

    def load(b, source):
        if b < count:
            target = conv_store.at[b // 2, :, pl.ds((b % 2) * half, half)]
        else:
            target = head_store.at[b - count]
        return pltpu.make_async_copy(source, target, in_sems.at[b])

    for b in range(blocks):
        for g in range(arrays):

            @pl.when(array[b] == g)
            def _(b=b, g=g):
                load(b, sources[g].at[item[b]]).start()

    stores = []
    for b in range(blocks):
        load(b, sources[0].at[0]).wait()
        if b >= count:
            stores.append(
                pltpu.make_async_copy(
                    head_store.at[b - count], head.at[b - count], out_sems.at[len(stores)]
                )
            )
            stores[-1].start()
        elif b % 2 == 1:
            tap = b // 2
            stores.append(
                pltpu.make_async_copy(
                    conv_store.at[tap], conv.at[tap // taps, tap % taps], out_sems.at[len(stores)]
                )
            )
            stores[-1].start()
    for store in stores:
        store.wait()


def place_blocks(sources, array, item, depth, taps):
    blocks = array.shape[0]
    chans, half = sources[0].shape[1:]
    heads = blocks - 2 * depth * taps
    anywhere = pl.BlockSpec(memory_space=pl.ANY)
    smem = pl.BlockSpec(memory_space=pltpu.SMEM)
    return pl.pallas_call(
        lambda *refs: place_kernel(depth, taps, half, len(sources), *refs),
        in_specs=[smem, smem] + [anywhere] * len(sources),
        out_specs=[anywhere, anywhere],
        out_shape=[
            jax.ShapeDtypeStruct((depth, taps, chans, 2 * half), bf16),
            jax.ShapeDtypeStruct((heads, chans, half), bf16),
        ],
        scratch_shapes=[
            pltpu.VMEM((depth * taps, chans, 2 * half), bf16),
            pltpu.VMEM((heads, chans, half), bf16),
            pltpu.SemaphoreType.DMA((blocks,)),
            pltpu.SemaphoreType.DMA((depth * taps + heads,)),
        ],
        compiler_params=pltpu.CompilerParams(vmem_limit_bytes=VMEM_BYTES),
        name="place_blocks",
    )(array, item, *sources)


def spread_slots(own, lay, z, beside):
    def line(value, pairs):
        return permute(
            value, [(lay.dev(a, i), lay.dev(b, i)) for a, b in pairs for i in range(lay.imgs)]
        )

    def over_x(value):
        return permute(value, lay.swap(2))

    def over_y(value):
        return permute(value, lay.swap(4))

    inner = (z == 1) | (z == 2)
    z_one = line(own, [(0, 1), (1, 0), (2, 3), (3, 2)])
    x_own = over_x(own)
    y_own = over_y(own)
    middle_own = line(own, [(1, 2), (2, 1)])
    middle_one = line(z_one, [(1, 2), (2, 1)])
    xy_own = over_x(y_own)
    y_one = over_y(z_one)
    outer_own = line(middle_own, [(1, 0), (2, 3)])
    outer_one = line(middle_one, [(1, 0), (2, 3)])
    z_two = jnp.where(inner, middle_one, outer_own)
    x_one = over_x(z_one)
    y_two = over_y(after(z_two, *beside))
    x_two = over_x(z_two)
    z_three = jnp.where(inner, middle_own, outer_one)
    xy_one = over_y(x_one)
    y_three = over_y(z_three)
    x_three = over_x(z_three)
    xy_three = over_y(x_three)
    xy_two = over_x(y_two)
    bundles = [
        jnp.concatenate(v, 0)
        for v in (
            (own, z_one, x_own, y_own),
            (z_two, z_three, xy_own, x_one),
            (y_one, x_two, y_two, xy_one),
            (x_three, y_three, xy_two, xy_three),
        )
    ]
    return bundles + [permute(v, lay.swap(1)) for v in bundles]


PLACES = (0, 1, 4, 5, 3, 8, 10, 13, 2, 7, 9, 12, 6, 11, 14, 15)


def encode(value):
    n, r, cols = value.shape
    top = jnp.max(jnp.abs(value), 1)
    power = jnp.clip(jnp.ceil(jnp.log2(top)), -100.0, 110.0)
    step = jnp.exp2(-power) * CODE
    codes = jnp.clip(jnp.round(value * step[:, None, :]), -CODE, CODE).astype(jnp.int16)
    pad = -n % 16
    powers = jnp.pad(power.astype(jnp.int16), ((0, pad), (0, 0)))
    return jnp.concatenate([codes.reshape(n * r, cols), powers], 0)


def decode(rows, n):
    pad = -n % 16
    total, cols = rows.shape
    r = (total - n - pad) // n
    power = rows[n * r : n * r + n].astype(f32)
    step = jnp.exp2(power) * (1.0 / CODE)
    return rows[: n * r].reshape(n, r, cols).astype(f32) * step[:, None, :]


def pick(value, index, axis):
    return lax.dynamic_index_in_dim(value, index, axis, keepdims=False)


class Sum:
    def __init__(self, parts, place, lay):
        self.x, self.y, self.z = place
        self.lay = lay
        self.counts = [part.shape[0] for part in parts]
        self.rows, cols = parts[0].shape[1:]
        self.w = cols // 2
        quarter = self.rows // 4
        self.va, self.vb = [], []
        sends = ([], [])
        for part in parts:
            n = part.shape[0]
            v = part.reshape(n, 2, 2, quarter, cols)
            va, vb = v[..., : self.w], v[..., self.w :]
            shape = (n, 2 * quarter, self.w)
            sends[0].append(encode(pick(va, 1 - self.x, 1).reshape(shape)))
            sends[1].append(encode(pick(vb, 1 - self.y, 2).reshape(shape)))
            self.va.append(va)
            self.vb.append(vb)
        self.send = [jnp.concatenate(send, 0) if len(send) > 1 else send[0] for send in sends]

    def split(self, rows_sent, r):
        at = 0
        out = []
        for n in self.counts:
            size = n * r + n + (-n % 16)
            out.append(decode(rows_sent[at : at + size], n))
            at += size
        return out

    def first(self):
        self.got = [permute(self.send[0], self.lay.swap(2)), permute(self.send[1], self.lay.swap(4))]

    def second(self, *wait):
        got = lax.optimization_barrier((*self.got, *wait))
        quarter = self.rows // 4
        got_a, got_b = self.split(got[0], 2 * quarter), self.split(got[1], 2 * quarter)
        send_a, send_b, self.keep = [], [], []
        for n, va, vb, ga, gb in zip(self.counts, self.va, self.vb, got_a, got_b):
            keep_a = pick(va, self.x, 1) + ga.reshape(n, 2, quarter, self.w)
            keep_b = pick(vb, self.y, 2) + gb.reshape(n, 2, quarter, self.w)
            send_a.append(encode(pick(keep_a, 1 - self.y, 1)))
            send_b.append(encode(pick(keep_b, 1 - self.x, 1)))
            self.keep.append((pick(keep_a, self.y, 1), pick(keep_b, self.x, 1)))
        self.send = [jnp.concatenate(v, 0) if len(v) > 1 else v[0] for v in (send_a, send_b)]
        self.got = [permute(self.send[0], self.lay.swap(4)), permute(self.send[1], self.lay.swap(2))]

    def third(self, *wait):
        got = lax.optimization_barrier((*self.got, *wait))
        quarter = self.rows // 4
        got_a, got_b = self.split(got[0], quarter), self.split(got[1], quarter)
        return [
            jnp.concatenate([keep_a + ga, keep_b + gb], -1)
            for (keep_a, keep_b), ga, gb in zip(self.keep, got_a, got_b)
        ]


def line_sum(keeps, scales):
    keep = jnp.concatenate(keeps, 0) if len(keeps) > 1 else keeps[0]
    n, rows, cols = keep.shape
    r = rows // scales
    keep = keep.reshape(n, scales, r, cols)
    top = jnp.max(jnp.abs(keep), 2)
    power = jnp.clip(jnp.ceil(jnp.log2(top)), -100.0, 110.0)
    step = jnp.exp2(-power) * CODE
    codes = jnp.clip(jnp.round(keep * step[:, :, None, :]), -CODE, CODE).astype(jnp.int16)
    codes = codes.transpose(1, 0, 2, 3).reshape(scales, n * r, cols)
    powers = jnp.pad(power.astype(jnp.int16).transpose(1, 0, 2), ((0, 0), (0, -n % 16), (0, 0)))
    got = lax.all_to_all(jnp.concatenate([codes, powers], 1), "scale", 0, 0, tiled=True)
    values = got[:, : n * r].reshape(scales, n, r, cols).astype(f32)
    step = jnp.exp2(got[:, n * r : n * r + n].astype(f32)) * (1.0 / CODE)
    return jnp.sum(values * step[:, :, None, :], 0)


def soap_update(master, moment, second, left, right, grads):
    turned = jnp.einsum("sij,ski->sjk", left, grads, precision=highest)
    turned = jnp.einsum("sjk,skl->sjl", turned, right, precision=highest)
    moment = beta_one * moment + (1.0 - beta_one) * turned
    second = beta_two * second + (1.0 - beta_two) * turned * turned
    ratio = moment / (1.0 - beta_one**STEP) / (jnp.sqrt(second / (1.0 - beta_two**STEP)) + adam_eps)
    back = jnp.einsum("sij,sjk->sik", left, ratio, precision=highest)
    back = jnp.einsum("sik,slk->sil", back, right, precision=highest)
    return (master - rate_matrix * (back + weight_decay * master), moment, second)


def vector_update(params, moment, second, grads):
    moment = beta_one * moment + (1.0 - beta_one) * grads
    second = beta_two * second + (1.0 - beta_two) * grads * grads
    ratio = moment / (1.0 - beta_one**STEP) / (jnp.sqrt(second / (1.0 - beta_two**STEP)) + adam_eps)
    return (params - rate_vector * (ratio + weight_decay * params), moment, second)


def butterfly(value, lay):
    bit = 1
    while bit < lay.imgs:
        value = value + permute(value, lay.swap(bit))
        bit *= 2
    bit = 1
    while bit < lay.scales:
        value = value + permute(value, lay.scale_swap(bit))
        bit *= 2
    return value


def local(
    images,
    valid_mask,
    scale_cols,
    boxes,
    normal_targets,
    dense_targets,
    affine_scale,
    affine_shift,
    conv_bf16,
    head_bf16,
    vectors,
    vec_m,
    vec_v,
    master,
    slot_m,
    slot_v,
    basis_left,
    basis_right,
    owner_slot,
):
    held, width, chans = (images.shape[1], images.shape[2], images.shape[3])
    heads_count, head_width = (head_bf16.shape[0], head_bf16.shape[2])
    wide = heads_count * head_width
    depth, taps = (conv_bf16.shape[0], conv_bf16.shape[1])
    scales, imgs = lax.axis_size("scale"), lax.axis_size("img")
    lay = Layout(scales, imgs)
    rows = held // scales
    z = lax.axis_index("scale")
    img = lax.axis_index("img")
    group, core = img // 2, img % 2
    place = jnp.where(group % 2 == 0, z, scales - 1 - z)
    mine = 2 * (place % 2) + core

    widths = [width >> s for s in range(scales)]
    starts = []
    at = 0
    for w in widths:
        starts.append(at)
        at += w + GAP
    cols = at
    col_iota = jnp.arange(cols, dtype=jnp.int32)
    valid_col = jnp.zeros((cols,), jnp.bool_)
    for s in range(scales):
        valid_col |= (col_iota >= starts[s]) & (col_iota < starts[s] + scale_cols[s])
    col_mask = valid_col.astype(f32)[None, :, None]

    own = images[0]
    fine = [
        permute(own[rows * k : rows * (k + 1)], lay.rows_round(k, [0])) for k in range(scales)
    ]
    coarse = []
    for k in range(scales):
        piece = (k + z) % scales
        send = lax.dynamic_slice_in_dim(own[:, : widths[1]], piece * rows, rows, 0)
        coarse.append(permute(send, lay.rows_round(k, range(1, scales))))
    parts = [(fine[0] + fine[1]) + (fine[2] + fine[3])]
    for s in range(1, scales):
        got = 0.0
        for k in range(scales):
            got = got + jnp.where((mine - k) % scales == s, coarse[k][:, : widths[s]], 0)
        parts.append(got.astype(bf16))
    spread = []
    for s in range(scales):
        spread.append(parts[s])
        spread.append(jnp.zeros((rows, GAP, chans), bf16))
    x_zero = (jnp.concatenate(spread, 1) * col_mask.astype(bf16)).reshape(rows * cols, chans)

    arrived = []
    for k in range(scales):
        piece = (k + z) % scales
        send = lax.dynamic_slice_in_dim(dense_targets, piece * rows, rows, 0)
        send = after(send, fine[1])
        got = permute(send, lay.rows_round(k, range(scales)))
        arrived.append(got.reshape(rows * width, dense_targets.shape[2]))
    hold = arrived[:2]

    valid_mask, boxes, normal_targets, scale_cols, *_ = lax.optimization_barrier(
        (valid_mask, boxes, normal_targets, scale_cols, *fine, *coarse)
    )

    mask_all = valid_mask.astype(f32)
    pixels = jnp.arange(held * width, dtype=jnp.int32)
    hits = jnp.sum((boxes[:, None] == pixels[None, :]).astype(f32), 0).reshape(held, width)
    packed = jnp.concatenate(
        [mask_all[None], (mask_all + box_weight * hits)[None], normal_targets], 0
    )
    packed_other = permute(packed, lay.swap(1))
    from_own = place // (scales // 2) == core
    packed = jnp.where(from_own, packed, packed_other)
    packed = lax.dynamic_slice_in_dim(packed, mine * rows, rows, 1).reshape(5, rows * width)
    valid, weight = packed[0][:, None], packed[1][:, None]
    normals = jnp.pad(packed[2:].T, ((0, 0), (0, 128 - 3)))
    tables = table_call(scale_cols, starts, widths, width, cols)
    gamma = vectors[:chans]
    bias = vectors[chans:]
    core_here = core.reshape(1)
    flat_mask = jnp.broadcast_to(col_mask, (rows, cols, 1)).reshape(rows * cols, 1)

    all_taps = conv_bf16.reshape(depth, 3, 3 * chans, chans)

    size = rows * cols

    def neighbours(value):
        partner = permute(value, lay.swap(1))
        at = value.shape[0] - size + core * (rows - 1) * cols
        return partner, permute(lax.dynamic_slice_in_dim(value, at, cols, 0), lay.outward())

    def gain_of(depth_idx):
        return affine_scale[depth_idx].reshape(1, chans), affine_shift[depth_idx].reshape(1, chans)

    pre_shape = jax.ShapeDtypeStruct((size, chans), f32)
    buffer_shape = jax.ShapeDtypeStruct((size + cols, chans), bf16)
    grad_shape = jax.ShapeDtypeStruct((size, chans), bf16)
    partner_zero, outer_zero = neighbours(x_zero)
    outer_zero = after(outer_zero, *hold)
    pre_zero, x_one = conv_call(
        first_conv_kernel,
        core_here,
        x_zero,
        partner_zero,
        outer_zero,
        *gain_of(0),
        flat_mask,
        [],
        all_taps,
        0,
        [pre_shape, buffer_shape],
        False,
        "conv_rows",
    )
    partner_one, outer_one = neighbours(x_one)
    grad_one, grad_mine, grad_pack, grad_gamma, grad_bias, loss_parts = head_call(
        core_here,
        mine.reshape(1),
        x_one,
        partner_one,
        outer_one,
        (*gain_of(1), flat_mask, gamma.reshape(1, chans), bias.reshape(1, wide)),
        (weight, valid, normals),
        head_bf16,
        arrived,
        tables,
        all_taps,
        1,
    )
    part = head_width // 2
    half = chans // 2
    staged = imgs == 8 and scales == 4
    x, y = (img // 2) % 2, img // 4
    where = (x, y, z)
    grad_partner, grad_outer = neighbours(grad_one)
    pack_got = permute(grad_pack, lay.swap(1))
    conv_grad_one = kernel_grad(
        core_here, x_one, partner_one, outer_one, grad_partner, grad_one, grad_partner, part
    )
    if staged:
        early = Sum([conv_grad_one.reshape(2 * taps, part, chans)], where, lay)
        early.first()
        grad_outer = after(grad_outer, *early.send)
    (grad_zero,) = conv_call(
        back_conv_kernel,
        core_here,
        grad_one,
        grad_partner,
        grad_outer,
        *gain_of(0),
        flat_mask,
        [pre_zero],
        all_taps,
        1,
        [grad_shape],
        True,
        "conv_back",
    )
    grad_zero_partner = permute(grad_zero, lay.swap(1))
    head_grad = head_grad_call(grad_mine, grad_pack, after(pack_got, grad_zero))
    if staged:
        middle = Sum([head_grad.reshape(heads_count, part, chans)], where, lay)
        middle.first()
        early.second(*middle.send)
        grad_zero_partner = after(grad_zero_partner, *early.send)
    conv_grad_zero = kernel_grad(
        core_here,
        x_zero,
        partner_zero,
        outer_zero,
        partner_one,
        grad_zero,
        grad_zero_partner,
        part,
    )
    if staged:
        late = Sum([conv_grad_zero.reshape(2 * taps, part, chans)], where, lay)
        late.first()
    grad_gamma, grad_bias = grad_gamma.reshape(chans), grad_bias.reshape(wide)
    own_count = jnp.where(z == 0, jnp.sum(mask_all), 0.0).reshape(1)
    loss_parts = jnp.concatenate([loss_parts[0, :2], own_count])

    vec_rows = jnp.concatenate(
        [grad_gamma, grad_bias, loss_parts, jnp.zeros((-(chans + wide + 3) % 1024,), f32)]
    ).reshape(-1, 128)
    vec_sum = butterfly(vec_rows, lay).reshape(-1)
    totals = vec_sum[chans + wide : chans + wide + 2]
    count = vec_sum[chans + wide + 2]
    grad_vec = vec_sum[: chans + wide]
    vec_squares = jnp.sum(grad_vec * grad_vec)

    blocks_count = owner_slot.shape[0]
    slots_here = master.shape[0]
    slots = slots_here * scales * imgs
    slot_ids = jnp.arange(slots, dtype=jnp.int32)
    match = slot_ids[:, None] == owner_slot[None, :]
    block_of = jnp.sum(
        jnp.where(match, jnp.arange(blocks_count, dtype=jnp.int32)[None, :], 0), 1
    )
    owned_f = jnp.any(match, 1).astype(f32)

    if staged:
        early_total = line_sum(early.third(*late.send), scales)
        middle.second(*late.send)
        late.second()
        late_total = line_sum(late.third() + middle.third(), scales)
        blocks = jnp.concatenate([late_total[: 2 * taps], early_total, late_total[2 * taps :]], 0)
        payload = route_call(blocks, jnp.where(owned_f > 0, block_of, -1), scales * imgs)
        got = lax.all_to_all(payload, AXES, 0, 0, tiled=True)
        starts_here = [
            (i % 2) * (half // 2) + (i // 2 % 2) * (half // 4) + (i // 4) * (half // 8) + s * (half // 32)
            for s, i in lay.all_devices()
        ]
        master_new, slot_m_new, slot_v_new, fresh, norm = update_call(
            jnp.stack([vec_squares, count]),
            got,
            starts_here,
            master,
            slot_m,
            slot_v,
            basis_left,
            basis_right,
        )
        grad_norm, factor = norm[0, 0], norm[0, 1]
        vec_out = vector_update(vectors, vec_m, vec_v, grad_vec * factor)
        sources = spread_slots(fresh, lay, z, vec_out)
        owner = owner_slot // slots_here
        other_img = owner % imgs
        turn = other_img ^ img
        step = ((turn >> 1) & 1) * 8 + (turn >> 2) * 4 + ((owner // imgs) ^ z)
        place = jnp.sum(
            jnp.where(
                step[:, None] == jnp.arange(16, dtype=jnp.int32)[None, :],
                jnp.asarray(PLACES, jnp.int32)[None, :],
                0,
            ),
            1,
        )
        array = place // 4 + 4 * (turn & 1)
        item = (place % 4) * slots_here + owner_slot % slots_here
    else:
        parts = jnp.concatenate(
            [v.reshape(2 * taps, part, chans) for v in (conv_grad_zero, conv_grad_one)]
            + [head_grad.reshape(heads_count, part, chans)],
            0,
        )
        none = jnp.zeros_like(parts)
        blocks = jnp.concatenate(
            [jnp.where(core == 0, parts, none), jnp.where(core == 1, parts, none)], 1
        )
        by_slot = blocks[block_of] * owned_f[:, None, None]
        owned = lax.psum_scatter(by_slot, AXES, scatter_dimension=0, tiled=True)
        squares_sum = lax.psum(jnp.sum(owned * owned), AXES) + vec_squares

        grad_norm = jnp.sqrt(squares_sum) / count
        factor = clip_level / jnp.maximum(grad_norm, clip_level) / count
        master_new, slot_m_new, slot_v_new = soap_update(
            master, slot_m, slot_v, basis_left, basis_right, owned * factor
        )
        sources = [lax.all_gather(master_new.astype(bf16), AXES, axis=0, tiled=True)]
        array, item = jnp.zeros_like(owner_slot), owner_slot
        vec_out = vector_update(vectors, vec_m, vec_v, grad_vec * factor)
    vec_new, vec_m_new, vec_v_new = vec_out
    conv_copy, head_copy = place_blocks(sources, array, item, depth, taps)
    loss = jnp.stack([totals[0] / wide + totals[1], count])
    return (
        loss,
        grad_norm,
        vec_new,
        vec_m_new,
        vec_v_new,
        master_new,
        slot_m_new,
        slot_v_new,
        conv_copy,
        head_copy,
    )


def solution(mesh):
    in_specs = (
        P("scale", "img", None, None),
        P("img", None),
        P(),
        P("img"),
        P(None, "img", None),
        P("img", None, "scale"),
        P(),
        P(),
        P(),
        P(),
        P(),
        P(),
        P(),
        P(("scale", "img"), None, None),
        P(("scale", "img"), None, None),
        P(("scale", "img"), None, None),
        P(("scale", "img"), None, None),
        P(("scale", "img"), None, None),
        P(),
    )
    out_specs = (
        P(),
        P(),
        P(),
        P(),
        P(),
        P(("scale", "img"), None, None),
        P(("scale", "img"), None, None),
        P(("scale", "img"), None, None),
        P(),
        P(),
    )
    return jax.shard_map(local, mesh=mesh, in_specs=in_specs, out_specs=out_specs, check_vma=False)
```

time: 576 us -> 460 us (0.80)
  Pallas kernels: 0 us -> 109 us
  waiting for transfers between devices: 212 us -> 135 us
  matrix products: 72.5 us -> 0 us
  local copies, waits for them, and re-layouts: 101 us -> 57.6 us
  between operations: 27.5 us -> 6.57 us
  other arithmetic: 50.5 us -> 34.4 us
    all_gather x1 -> x0, waiting for transfers between devices: 112 us -> none  [local(): every = lax.all_gather(fresh, AXES, axis=0, tiled=True)]
    pallas_call x0 -> x10, Pallas kernels: none -> 109 us  [the longest x1 29 us: head_call(): pl.pallas_call(lambda *refs: head_kernel(rows, cols, width, scales, layer...]
    dot_general x29 -> x0, matrix products: 56.6 us -> none  [the longest x18 36.1 us: kernel_grad(): jnp.einsum('prwc,prwd->cd', window, grad_pair, preferred_element_type=f32)]
    all_to_all x0 -> x2, waiting for transfers between devices: none -> 20 us  [line_sum(): lax.all_to_all(jnp.concatenate([codes, powers], 1), 'scale', 0, 0, tiled=...]
    conv_general_dilated x3 -> x0, matrix products: 15.9 us -> none  [the longest x2 10.6 us: conv_rows(): lax.conv_general_dilated(padded[None], kernel, (1, 1), ((0, 0), (1, 1)),...]
    ppermute x57 -> x59, waiting for transfers between devices: 100 us -> 115 us  [permute(): return lax.ppermute(value, AXES, pairs)]
    slice x17 -> x11, local copies, waits for them, and re-layouts: 24.6 us -> 10.4 us  [the longest x3 7.66 us: __init__(): va, vb = (v[..., :self.w], v[..., self.w:])]
    gather x2 -> x0, local copies, waits for them, and re-layouts: 13.5 us -> none  [the longest x1 11.8 us: local(): store = every[owner_slot]]
  transfers between devices with their start and end apart: 59 -> 62, of which waited for: 22 -> 24; matrix products, arithmetic and copies ran while one was open for 25% -> 16% of each run, Pallas kernels for 0% -> 10%
where the time goes in v2:
time: 460 us; the launch traced here: 451 us
  waiting for transfers between devices  135 us (29%)
  Pallas kernels  109 us (24%)
  starting transfers between devices  108 us (23%)
  local copies, waits for them, and re-layouts  57.6 us (13%)
  other arithmetic  34.4 us (7%)
  between operations  6.57 us (1%)
    ppermute x59, waiting for transfers between devices, permute(): return lax.ppermute(value, AXES, pairs)  115 us
    ppermute x59, starting transfers between devices, permute(): return lax.ppermute(value, AXES, pairs)  95.4 us
    pallas_call x1, Pallas kernels, head_call(): pl.pallas_call(lambda *refs: head_kernel(rows, cols, width, scales, layer...  29 us
    pallas_call x2, Pallas kernels, conv_call(): pl.pallas_call(lambda *refs: kernel(rows, cols, chans, layer, *refs), in_...  28.1 us
    pallas_call x2, Pallas kernels, kernel_grad(): pl.pallas_call(lambda *refs: kernel_grad_kernel(rows, cols, chans, part,...  24 us
    all_to_all x2, waiting for transfers between devices, line_sum(): lax.all_to_all(jnp.concatenate([codes, powers], 1), 'scale', 0, 0, tiled=...  20 us
    unnamed x97, local copies, waits for them, and re-layouts  15.9 us
    slice x12, local copies, waits for them, and re-layouts, decode(): return rows[:n * r].reshape(n, r, cols).astype(f32) * step[:, None, :]  10.3 us
  transfers between devices with their start and end apart: 62, of which 24 were waited for; matrix products, arithmetic and copies ran while one was open for 16% of the time, Pallas kernels for 10%

profile of v2, /device:TPU:0, one launch (start us, length us, event | category | flops | bytes accessed | tf_op | source)
XLA Modules:
  0.0 451.1 jit_solution(10024994036756504499)
XLA Ops:
  0.7 3.0 slice_bitcast_fusion.2
  3.7 3.2 collective-permute-start.1
  6.8 4.0 collective-permute-start.2
  10.9 5.4 %collective-permute-start = (bf16[2,256,512]{2,1,0:T(8,128)(2,1)}, bf16[2,256,512]{2,1,0:T(8,128)(2,1)}, u32[]{:S(2)}, u32[]{:S(2)}) collective-permute-start(bf16[2,256,512]{2,1,0:T(8,128)(2,1)} %get-tuple-element.134), channel_id=1, source_target_pairs={{0,0},{1,16},{2,26},{3,10},{4,4},{5,20},{6,30},{7,14}} | collective-permute-start | bytes 1572872 | tf_op jit(solution)/shard_map/ppermute | solution.py:81
  16.2 2.1 collective-permute-start.3
  26.6 7.4 %collective-permute-done.3 = bf16[2,256,512]{2,1,0:T(8,128)(2,1)} collective-permute-done((bf16[2,256,512]{2,1,0:T(8,128)(2,1)}, bf16[2,256,512]{2,1,0:T(8,128)(2,1)}, u32[]{:S(2)}, u32[]{:S(2)}) %collective-permute-start.3) | collective-permute-done | bytes 524320 | tf_op jit(solution)/shard_map/ppermute | solution.py:81
  36.6 6.9 %collective-permute-done.5 = bf16[2,128,512]{2,1,0:T(8,128)(2,1)S(1)} collective-permute-done((bf16[2,128,512]{2,1,0:T(8,128)(2,1)S(1)}, bf16[2,128,512]{2,1,0:T(8,128)(2,1)S(1)}, u32[]{:S(2)}, u32[]{:S(2)}) %collective-permute-start.5) | collective-permute-done | bytes 262176 | tf_op jit(solution)/shard_map/ppermute | solution.py:81
  44.1 2.2 collective-permute-start.8
  47.0 2.7 constant_dynamic-slice_fusion.14
  49.7 5.1 %collective-permute-start.10 = (bf16[2,256,448]{1,2,0:T(8,128)(2,1)}, bf16[2,256,448]{1,2,0:T(8,128)(2,1)}, u32[]{:S(2)}, u32[]{:S(2)}) collective-permute-start(bf16[2,256,448]{1,2,0:T(8,128)(2,1)} %get-tuple-element.54), channel_id=1, source_target_pairs={{0,0},{1,16},{2,26},{3,10},{4,4},{5,20},{6,30},{7,14},{8,1},{9,17}... | collective-permute-start | bytes 1376264 | tf_op jit(solution)/shard_map/ppermute | solution.py:81
  54.8 3.7 collective-permute-start.11
  62.4 13.5 %collective-permute-done.11 = bf16[2,256,448]{1,2,0:T(8,128)(2,1)} collective-permute-done((bf16[2,256,448]{1,2,0:T(8,128)(2,1)}, bf16[2,256,448]{1,2,0:T(8,128)(2,1)}, u32[]{:S(2)}, u32[]{:S(2)}) %collective-permute-start.11) | collective-permute-done | bytes 458784 | tf_op jit(solution)/shard_map/ppermute | solution.py:81
  79.1 13.3 %conv_rows.1 = (f32[1088,512]{1,0:T(8,128)}, bf16[1632,512]{1,0:T(8,128)(2,1)}) custom-call(s32[1]{0:T(128)} %bitcast.refs_0_, bf16[1088,512]{1,0:T(8,128)(2,1)} %copy-done.2, bf16[1088,512]{1,0:T(8,128)(2,1)} %copy-done.7, bf16[544,512]{1,0:T(8,128)(2,1)} %copy-done.14, f32[1,512]{1,0:T(1,128)} %get-tuple-element.195.refs_4_, ...), custom_call_target="tpu_custom_call" | custom-call | flops 1 | bytes 1 | tf_op jit(solution)/shard_map/conv_rows/pallas_call | solution.py:235
  92.5 3.6 collective-permute-start.15
  96.2 4.3 collective-permute-start.16
  105.7 2.3 tables.1
  112.6 3.0 collective-permute-done.16
  119.1 29.0 %head_rows.1 = (bf16[1632,512]{1,0:T(8,128)(2,1)}, bf16[512,896]{1,0:T(8,128)(2,1)}, bf16[512,1408]{1,0:T(8,128)(2,1)}, f32[1,512]{1,0:T(1,128)}, f32[1,1792]{1,0:T(1,128)}, /*index=5*/f32[1,128]{1,0:T(1,128)}) custom-call(s32[1]{0:T(128)} %bitcast.refs_0_, s32[1]{0:T(128)} %bitcast.1.refs_1_, bf16[1632,512]{1,0:T(8,128)(2,1)} %get-tuple-element.57.refs_2_.refs_1_, ...), custom_call_target="tpu_custom_call" | custom-call | flops 1 | bytes 1 | tf_op jit(solution)/shard_map/head_rows/pallas_call | solution.py:444
  148.1 5.6 %collective-permute-start.22 = (bf16[1632,512]{1,0:T(8,128)(2,1)}, bf16[1632,512]{1,0:T(8,128)(2,1)S(1)}, u32[]{:S(2)}, u32[]{:S(2)}) collective-permute-start(bf16[1632,512]{1,0:T(8,128)(2,1)} %get-tuple-element.71.refs_5_.refs_1_), channel_id=1, source_target_pairs={{0,1},{1,0},{2,3},{3,2},{4,5},{5,4},{6,7},{7,6},{8,9},{9,8},{10,11... | collective-permute-start | bytes 5013512 | tf_op jit(solution)/shard_map/ppermute | solution.py:81
  156.5 3.8 collective-permute-start.27
  161.5 12.2 %kernel_grad.2 = f32[9,256,512]{2,1,0:T(8,128)} custom-call(s32[1]{0:T(128)} %bitcast.refs_0_, bf16[1632,512]{1,0:T(8,128)(2,1)} %get-tuple-element.57.refs_2_.refs_1_, bf16[1632,512]{1,0:T(8,128)(2,1)} %copy-done, bf16[544,512]{1,0:T(8,128)(2,1)} %copy-done.15, bf16[1632,512]{1,0:T(8,128)(2,1)} %copy-done.1, ...), custom_call_target="tpu_custom_call" | custom-call | flops 1 | bytes 1 | tf_op jit(solution)/shard_map/kernel_grad/pallas_call | solution.py:510
  173.7 3.1 fusion.91
  180.2 3.8 collective-permute-start.25
  184.8 14.8 %conv_back.1.refs_5_ = bf16[1088,512]{1,0:T(8,128)(2,1)} custom-call(s32[1]{0:T(128)} %bitcast.refs_0_, bf16[1632,512]{1,0:T(8,128)(2,1)} %get-tuple-element.71.refs_5_.refs_1_, bf16[1632,512]{1,0:T(8,128)(2,1)} %copy-done.1, bf16[544,512]{1,0:T(8,128)(2,1)} %copy-done.22, f32[1,512]{1,0:T(1,128)} %get-tuple-element.195.refs_4_, ...), custom_call_target="tpu_custom_call" | custom-call | flops 1 | bytes 1 | tf_op jit(solution)/shard_map/conv_back/pallas_call | solution.py:235
  200.8 4.4 head_grad.1
  218.3 11.7 %kernel_grad.3 = f32[9,256,512]{2,1,0:T(8,128)} custom-call(s32[1]{0:T(128)} %bitcast.refs_0_, bf16[1088,512]{1,0:T(8,128)(2,1)} %copy-done.2, bf16[1088,512]{1,0:T(8,128)(2,1)} %copy-done.7, bf16[544,512]{1,0:T(8,128)(2,1)} %copy-done.14, bf16[1632,512]{1,0:T(8,128)(2,1)} %copy-done, bf16[1088,512]{1,0:T(8,128)(2,1)} %conv_back.1.refs_5_, ...), custom_call_target="tpu_custom_call" | custom-call | flops 1 | bytes 1 | tf_op jit(solution)/shard_map/kernel_grad/pallas_call | solution.py:510
  230.1 2.9 fusion.90
  252.8 4.5 all-to-all-start.1
  257.3 4.3 collective-permute-done.35
  272.7 3.4 collective-permute-done.31
  279.3 4.8 %all-to-all-start = ((s16[4,232,512]{2,1,0:T(8,128)(2,1)}), s16[4,232,512]{2,1,0:T(8,128)(2,1)S(1)}, u32[]{:S(2)}, u32[]{:S(2)}) async-start(s16[4,232,512]{2,1,0:T(8,128)(2,1)} %pad_add_fusion), calls=%async_computation | async-start | bytes 1900544 | tf_op jit(solution)/shard_map/all_to_all | solution.py:895
  285.1 20.0 %all-to-all-done = s16[4,232,512]{2,1,0:T(8,128)(2,1)S(1)} async-done(((s16[4,232,512]{2,1,0:T(8,128)(2,1)}), s16[4,232,512]{2,1,0:T(8,128)(2,1)S(1)}, u32[]{:S(2)}, u32[]{:S(2)}) %all-to-all-start) | async-done | bytes 950304 | tf_op jit(solution)/shard_map/all_to_all | solution.py:895
  306.5 2.7 route.1
  309.1 3.7 all-to-all-start.2
  326.1 3.3 collective-permute-start.21
  335.1 9.1 %update.1 = (f32[2,512,256]{2,1,0:T(8,128)}, f32[2,512,256]{2,1,0:T(8,128)}, f32[2,512,256]{2,1,0:T(8,128)}, bf16[2,512,256]{2,1,0:T(8,128)(2,1)}, f32[1,128]{1,0:T(1,128)}) custom-call(f32[2]{0:T(128)} %pad_maximum_fusion.5.refs_0_, s16[32,80,128]{2,1,0:T(8,128)(2,1)} %copy-done.13, f32[2,512,256]{2,1,0:T(8,128)} %refs_2_.1, f32[2,512,256]{2,1,0:T(8,128)} %refs_3_.1, ...), custom_call_target="tpu_custom_call" | custom-call | tf_op jit(solution)/shard_map/update/pallas_call | solution.py:669
  344.2 2.1 collective-permute-start.38
  347.0 10.7 %collective-permute-done.38 = bf16[2,512,256]{2,1,0:T(8,128)(2,1)S(1)} collective-permute-done((bf16[2,512,256]{2,1,0:T(8,128)(2,1)}, bf16[2,512,256]{2,1,0:T(8,128)(2,1)S(1)}, u32[]{:S(2)}, u32[]{:S(2)}) %collective-permute-start.38) | collective-permute-done | bytes 524320 | tf_op jit(solution)/shard_map/ppermute | solution.py:81
  368.3 2.7 collective-permute-done.40
  372.3 4.2 collective-permute-done.43
  376.6 2.1 collective-permute-start.48
  378.7 7.6 %collective-permute-done.46 = bf16[2,512,256]{2,1,0:T(8,128)(2,1)S(1)} collective-permute-done((bf16[2,512,256]{2,1,0:T(8,128)(2,1)S(1)}, bf16[2,512,256]{2,1,0:T(8,128)(2,1)S(1)}, u32[]{:S(2)}, u32[]{:S(2)}) %collective-permute-start.46) | collective-permute-done | bytes 524320 | tf_op jit(solution)/shard_map/ppermute | solution.py:81
  389.7 19.0 %collective-permute-done.48 = bf16[2,512,256]{2,1,0:T(8,128)(2,1)S(1)} collective-permute-done((bf16[2,512,256]{2,1,0:T(8,128)(2,1)S(1)}, bf16[2,512,256]{2,1,0:T(8,128)(2,1)S(1)}, u32[]{:S(2)}, u32[]{:S(2)}) %collective-permute-start.48) | collective-permute-done | bytes 524320 | tf_op jit(solution)/shard_map/ppermute | solution.py:81
  410.9 9.1 %collective-permute-done.51 = bf16[2,512,256]{2,1,0:T(8,128)(2,1)S(1)} collective-permute-done((bf16[2,512,256]{2,1,0:T(8,128)(2,1)S(1)}, bf16[2,512,256]{2,1,0:T(8,128)(2,1)S(1)}, u32[]{:S(2)}, u32[]{:S(2)}) %collective-permute-start.51) | collective-permute-done | bytes 524320 | tf_op jit(solution)/shard_map/ppermute | solution.py:81
  420.9 2.7 collective-permute-done.52
  423.7 4.2 collective-permute-done.53
  427.9 6.6 %collective-permute-done.54 = bf16[2,512,256]{2,1,0:T(8,128)(2,1)S(1)} collective-permute-done((bf16[2,512,256]{2,1,0:T(8,128)(2,1)S(1)}, bf16[2,512,256]{2,1,0:T(8,128)(2,1)S(1)}, u32[]{:S(2)}, u32[]{:S(2)}) %collective-permute-start.54) | collective-permute-done | bytes 524320 | tf_op jit(solution)/shard_map/ppermute | solution.py:81
  441.3 9.3 %place_blocks.1 = (bf16[2,9,512,512]{3,2,1,0:T(8,128)(2,1)}, bf16[7,512,256]{2,1,0:T(8,128)(2,1)}) custom-call(s32[43]{0:T(128)} %get-tuple-element.186.refs_0_, s32[43]{0:T(128)} %get-tuple-element.185.refs_1_, bf16[8,512,256]{2,1,0:T(8,128)(2,1)} %copy-done.12, bf16[8,512,256]{2,1,0:T(8,128)(2,1)} %copy-done.5, bf16[8,512,256]{2,1,0:T(8,128)(2,1)} %copy-done.10, ...), custom_call_target="tpu_custom_call" | custom-call | tf_op jit(solution)/shard_map/place_blocks/pallas_call | solution.py:737
  (349 shorter events, 131.5 us)
Async XLA Ops:
  3.7 19.0 %collective-permute-start.1 = (bf16[2,256,512]{2,1,0:T(8,128)(2,1)}, bf16[2,256,512]{2,1,0:T(8,128)(2,1)}, u32[]{:S(2)}, u32[]{:S(2)}) collective-permute-start(bf16[2,256,512]{2,1,0:T(8,128)(2,1)} %get-tuple-element.132), channel_id=1, source_target_pairs={{0,1},{1,17},{2,27},{3,11},{4,5},{5,21},{6,31},{7,15}} | collective-permute-start | bytes 1572872 | tf_op jit(solution)/shard_map/ppermute | solution.py:81
  6.8 17.1 %collective-permute-start.2 = (bf16[2,256,512]{2,1,0:T(8,128)(2,1)}, bf16[2,256,512]{2,1,0:T(8,128)(2,1)}, u32[]{:S(2)}, u32[]{:S(2)}) collective-permute-start(bf16[2,256,512]{2,1,0:T(8,128)(2,1)} %get-tuple-element.133), channel_id=1, source_target_pairs={{0,8},{1,24},{2,18},{3,2},{4,12},{5,28},{6,22},{7,6}} | collective-permute-start | bytes 1572872 | tf_op jit(solution)/shard_map/ppermute | solution.py:81
  10.9 14.4 %collective-permute-start = (bf16[2,256,512]{2,1,0:T(8,128)(2,1)}, bf16[2,256,512]{2,1,0:T(8,128)(2,1)}, u32[]{:S(2)}, u32[]{:S(2)}) collective-permute-start(bf16[2,256,512]{2,1,0:T(8,128)(2,1)} %get-tuple-element.134), channel_id=1, source_target_pairs={{0,0},{1,16},{2,26},{3,10},{4,4},{5,20},{6,30},{7,14}} | collective-permute-start | bytes 1572872 | tf_op jit(solution)/shard_map/ppermute | solution.py:81
  16.2 17.7 %collective-permute-start.3 = (bf16[2,256,512]{2,1,0:T(8,128)(2,1)}, bf16[2,256,512]{2,1,0:T(8,128)(2,1)}, u32[]{:S(2)}, u32[]{:S(2)}) collective-permute-start(bf16[2,256,512]{2,1,0:T(8,128)(2,1)} %get-tuple-element.135), channel_id=1, source_target_pairs={{0,9},{1,25},{2,19},{3,3},{4,13},{5,29},{6,23},{7,7}} | collective-permute-start | bytes 1572872 | tf_op jit(solution)/shard_map/ppermute | solution.py:81
  18.5 17.2 %collective-permute-start.4 = (bf16[2,128,512]{2,1,0:T(8,128)(2,1)S(1)}, bf16[2,128,512]{2,1,0:T(8,128)(2,1)S(1)}, u32[]{:S(2)}, u32[]{:S(2)}) collective-permute-start(bf16[2,128,512]{2,1,0:T(8,128)(2,1)S(1)} %get-tuple-element.142), channel_id=1, source_target_pairs={{8,1},{9,17},{10,27},{11,11},{12,5},{13,21},{14,31},{15,15},{16,8}... | collective-permute-start | bytes 786440 | tf_op jit(solution)/shard_map/ppermute | solution.py:81
  22.7 13.1 %collective-permute-start.7 = (bf16[2,128,512]{2,1,0:T(8,128)(2,1)S(1)}, bf16[2,128,512]{2,1,0:T(8,128)(2,1)S(1)}, u32[]{:S(2)}, u32[]{:S(2)}) collective-permute-start(bf16[2,128,512]{2,1,0:T(8,128)(2,1)S(1)} %get-tuple-element.143), channel_id=1, source_target_pairs={{8,0},{9,16},{10,26},{11,10},{12,4},{13,20},{14,30},{15,14},{16,1}... | collective-permute-start | bytes 786440 | tf_op jit(solution)/shard_map/ppermute | solution.py:81
  24.0 12.6 %collective-permute-start.6 = (bf16[2,128,512]{2,1,0:T(8,128)(2,1)S(1)}, bf16[2,128,512]{2,1,0:T(8,128)(2,1)S(1)}, u32[]{:S(2)}, u32[]{:S(2)}) collective-permute-start(bf16[2,128,512]{2,1,0:T(8,128)(2,1)S(1)} %get-tuple-element.144), channel_id=1, source_target_pairs={{8,9},{9,25},{10,19},{11,3},{12,13},{13,29},{14,23},{15,7},{16,0},... | collective-permute-start | bytes 786440 | tf_op jit(solution)/shard_map/ppermute | solution.py:81
  25.3 18.1 %collective-permute-start.5 = (bf16[2,128,512]{2,1,0:T(8,128)(2,1)S(1)}, bf16[2,128,512]{2,1,0:T(8,128)(2,1)S(1)}, u32[]{:S(2)}, u32[]{:S(2)}) collective-permute-start(bf16[2,128,512]{2,1,0:T(8,128)(2,1)S(1)} %get-tuple-element.145), channel_id=1, source_target_pairs={{8,8},{9,24},{10,18},{11,2},{12,12},{13,28},{14,22},{15,6},{16,9},... | collective-permute-start | bytes 786440 | tf_op jit(solution)/shard_map/ppermute | solution.py:81
  44.1 33.8 %collective-permute-start.8 = (bf16[1088,512]{1,0:T(8,128)(2,1)S(1)}, bf16[1088,512]{1,0:T(8,128)(2,1)S(1)}, u32[]{:S(2)}, u32[]{:S(2)}) collective-permute-start(bf16[1088,512]{1,0:T(8,128)(2,1)S(1)} %bitcast_multiply_fusion.6.refs_1_), channel_id=1, source_target_pairs={{0,1},{1,0},{2,3},{3,2},{4,5},{5,4},{6,7},{7,6},{8,9},{9,8},{10,11... | collective-permute-start | bytes 3342344 | tf_op jit(solution)/shard_map/ppermute | solution.py:81
  46.3 31.6 %collective-permute-start.9 = (bf16[544,512]{1,0:T(8,128)(2,1)S(1)}, bf16[544,512]{1,0:T(8,128)(2,1)S(1)}, u32[]{:S(2)}, u32[]{:S(2)}) collective-permute-start(bf16[544,512]{1,0:T(8,128)(2,1)S(1)} %constant_dynamic-slice_fusion.19), channel_id=1, source_target_pairs={{1,8},{8,1},{9,16},{16,9},{17,24},{24,17},{25,26},{26,25},{27,18},... | collective-permute-start | bytes 1671176 | tf_op jit(solution)/shard_map/ppermute | solution.py:81
  54.8 21.1 %collective-permute-start.11 = (bf16[2,256,448]{1,2,0:T(8,128)(2,1)}, bf16[2,256,448]{1,2,0:T(8,128)(2,1)}, u32[]{:S(2)}, u32[]{:S(2)}) collective-permute-start(bf16[2,256,448]{1,2,0:T(8,128)(2,1)} %get-tuple-element.55), channel_id=1, source_target_pairs={{0,1},{1,17},{2,27},{3,11},{4,5},{5,21},{6,31},{7,15},{8,8},{9,24}... | collective-permute-start | bytes 1376264 | tf_op jit(solution)/shard_map/ppermute | solution.py:81
  92.5 25.2 %collective-permute-start.12 = (bf16[1632,512]{1,0:T(8,128)(2,1)}, bf16[1632,512]{1,0:T(8,128)(2,1)S(1)}, u32[]{:S(2)}, u32[]{:S(2)}) collective-permute-start(bf16[1632,512]{1,0:T(8,128)(2,1)} %get-tuple-element.57.refs_2_.refs_1_), channel_id=1, source_target_pairs={{0,1},{1,0},{2,3},{3,2},{4,5},{5,4},{6,7},{7,6},{8,9},{9,8},{10,11... | collective-permute-start | bytes 5013512 | tf_op jit(solution)/shard_map/ppermute | solution.py:81
  92.5 18.1 %collective-permute-start.15 = (bf16[2,256,448]{1,2,0:T(8,128)(2,1)}, bf16[2,256,448]{1,2,0:T(8,128)(2,1)}, u32[]{:S(2)}, u32[]{:S(2)}) collective-permute-start(bf16[2,256,448]{1,2,0:T(8,128)(2,1)} %get-tuple-element.61), channel_id=1, source_target_pairs={{0,8},{1,24},{2,18},{3,2},{4,12},{5,28},{6,22},{7,6},{8,9},{9,25},... | collective-permute-start | bytes 1376264 | tf_op jit(solution)/shard_map/ppermute | solution.py:81
  96.2 19.4 %collective-permute-start.16 = (bf16[2,256,448]{1,2,0:T(8,128)(2,1)S(1)}, bf16[2,256,448]{1,2,0:T(8,128)(2,1)}, u32[]{:S(2)}, u32[]{:S(2)}) collective-permute-start(bf16[2,256,448]{1,2,0:T(8,128)(2,1)S(1)} %copy-done.23), channel_id=1, source_target_pairs={{0,9},{1,25},{2,19},{3,3},{4,13},{5,29},{6,23},{7,7},{8,0},{9,16},... | collective-permute-start | bytes 1376264 | tf_op jit(solution)/shard_map/ppermute | solution.py:81
  101.7 16.0 %collective-permute-start.13 = (bf16[544,512]{1,0:T(8,128)(2,1)S(1)}, bf16[544,512]{1,0:T(8,128)(2,1)S(1)}, u32[]{:S(2)}, u32[]{:S(2)}) collective-permute-start(bf16[544,512]{1,0:T(8,128)(2,1)S(1)} %constant_dynamic-slice_fusion.16), channel_id=1, source_target_pairs={{1,8},{8,1},{9,16},{16,9},{17,24},{24,17},{25,26},{26,25},{27,18},... | collective-permute-start | bytes 1671176 | tf_op jit(solution)/shard_map/ppermute | solution.py:81
  155.6 28.4 %collective-permute-start.23 = (bf16[544,512]{1,0:T(8,128)(2,1)}, bf16[544,512]{1,0:T(8,128)(2,1)S(1)}, u32[]{:S(2)}, u32[]{:S(2)}) collective-permute-start(bf16[544,512]{1,0:T(8,128)(2,1)} %constant_dynamic-slice_fusion.13), channel_id=1, source_target_pairs={{1,8},{8,1},{9,16},{16,9},{17,24},{24,17},{25,26},{26,25},{27,18},... | collective-permute-start | bytes 1671176 | tf_op jit(solution)/shard_map/ppermute | solution.py:81
  156.5 43.3 %collective-permute-start.27 = (bf16[512,1408]{1,0:T(8,128)(2,1)}, bf16[512,1408]{1,0:T(8,128)(2,1)S(1)}, u32[]{:S(2)}, u32[]{:S(2)}) collective-permute-start(bf16[512,1408]{1,0:T(8,128)(2,1)} %get-tuple-element.75.own), channel_id=1, source_target_pairs={{0,1},{1,0},{2,3},{3,2},{4,5},{5,4},{6,7},{7,6},{8,9},{9,8},{10,11... | collective-permute-start | bytes 4325384 | tf_op jit(solution)/shard_map/ppermute | solution.py:81
  177.4 32.1 %collective-permute-start.26 = (s16[1184,256]{1,0:T(8,128)(2,1)S(1)}, s16[1184,256]{1,0:T(8,128)(2,1)}, u32[]{:S(2)}, u32[]{:S(2)}) collective-permute-start(s16[1184,256]{1,0:T(8,128)(2,1)S(1)} %pad_add_fusion.4), channel_id=1, source_target_pairs={{0,4},{1,5},{2,6},{3,7},{4,0},{5,1},{6,2},{7,3},{8,12},{9,13},{10,... | collective-permute-start | bytes 1818632 | tf_op jit(solution)/shard_map/ppermute | solution.py:81
  180.2 29.3 %collective-permute-start.25 = (s16[1184,256]{1,0:T(8,128)(2,1)}, s16[1184,256]{1,0:T(8,128)(2,1)}, u32[]{:S(2)}, u32[]{:S(2)}) collective-permute-start(s16[1184,256]{1,0:T(8,128)(2,1)} %pad_add_fusion.5), channel_id=1, source_target_pairs={{0,2},{1,3},{2,0},{3,1},{4,6},{5,7},{6,4},{7,5},{8,10},{9,11},{10,... | collective-permute-start | bytes 1818632 | tf_op jit(solution)/shard_map/ppermute | solution.py:81
  199.6 18.7 %collective-permute-start.24 = (bf16[1088,512]{1,0:T(8,128)(2,1)}, bf16[1088,512]{1,0:T(8,128)(2,1)}, u32[]{:S(2)}, u32[]{:S(2)}) collective-permute-start(bf16[1088,512]{1,0:T(8,128)(2,1)} %conv_back.1.refs_5_), channel_id=1, source_target_pairs={{0,1},{1,0},{2,3},{3,2},{4,5},{5,4},{6,7},{7,6},{8,9},{9,8},{10,11... | collective-permute-start | bytes 3342344 | tf_op jit(solution)/shard_map/ppermute | solution.py:81
  208.0 29.2 %collective-permute-start.33 = (s16[464,256]{1,0:T(8,128)(2,1)}, s16[464,256]{1,0:T(8,128)(2,1)}, u32[]{:S(2)}, u32[]{:S(2)}) collective-permute-start(s16[464,256]{1,0:T(8,128)(2,1)} %pad_add_fusion.10), channel_id=1, source_target_pairs={{0,4},{1,5},{2,6},{3,7},{4,0},{5,1},{6,2},{7,3},{8,12},{9,13},{10,... | collective-permute-start | bytes 712712 | tf_op jit(solution)/shard_map/ppermute | solution.py:81
  209.3 27.9 %collective-permute-start.32 = (s16[464,256]{1,0:T(8,128)(2,1)}, s16[464,256]{1,0:T(8,128)(2,1)}, u32[]{:S(2)}, u32[]{:S(2)}) collective-permute-start(s16[464,256]{1,0:T(8,128)(2,1)} %pad_add_fusion.11), channel_id=1, source_target_pairs={{0,2},{1,3},{2,0},{3,1},{4,6},{5,7},{6,4},{7,5},{8,10},{9,11},{10,... | collective-permute-start | bytes 712712 | tf_op jit(solution)/shard_map/ppermute | solution.py:81
  213.7 26.8 %collective-permute-start.37 = (s16[608,256]{1,0:T(8,128)(2,1)}, s16[608,256]{1,0:T(8,128)(2,1)}, u32[]{:S(2)}, u32[]{:S(2)}) collective-permute-start(s16[608,256]{1,0:T(8,128)(2,1)} %pad_add_fusion.8), channel_id=1, source_target_pairs={{0,2},{1,3},{2,0},{3,1},{4,6},{5,7},{6,4},{7,5},{8,10},{9,11},{10,... | collective-permute-start | bytes 933896 | tf_op jit(solution)/shard_map/ppermute | solution.py:81
  216.8 23.7 %collective-permute-start.36 = (s16[608,256]{1,0:T(8,128)(2,1)S(1)}, s16[608,256]{1,0:T(8,128)(2,1)S(1)}, u32[]{:S(2)}, u32[]{:S(2)}) collective-permute-start(s16[608,256]{1,0:T(8,128)(2,1)S(1)} %pad_add_fusion.9), channel_id=1, source_target_pairs={{0,4},{1,5},{2,6},{3,7},{4,0},{5,1},{6,2},{7,3},{8,12},{9,13},{10,... | collective-permute-start | bytes 933896 | tf_op jit(solution)/shard_map/ppermute | solution.py:81
  235.5 28.7 %collective-permute-start.29 = (s16[1184,256]{1,0:T(8,128)(2,1)}, s16[1184,256]{1,0:T(8,128)(2,1)}, u32[]{:S(2)}, u32[]{:S(2)}) collective-permute-start(s16[1184,256]{1,0:T(8,128)(2,1)} %pad_add_fusion.2), channel_id=1, source_target_pairs={{0,4},{1,5},{2,6},{3,7},{4,0},{5,1},{6,2},{7,3},{8,12},{9,13},{10,... | collective-permute-start | bytes 1818632 | tf_op jit(solution)/shard_map/ppermute | solution.py:81
  243.9 20.3 %collective-permute-start.28 = (s16[1184,256]{1,0:T(8,128)(2,1)}, s16[1184,256]{1,0:T(8,128)(2,1)}, u32[]{:S(2)}, u32[]{:S(2)}) collective-permute-start(s16[1184,256]{1,0:T(8,128)(2,1)} %pad_add_fusion.3), channel_id=1, source_target_pairs={{0,2},{1,3},{2,0},{3,1},{4,6},{5,7},{6,4},{7,5},{8,10},{9,11},{10,... | collective-permute-start | bytes 1818632 | tf_op jit(solution)/shard_map/ppermute | solution.py:81
  246.9 14.7 %collective-permute-start.35 = (s16[240,256]{1,0:T(8,128)(2,1)}, s16[240,256]{1,0:T(8,128)(2,1)}, u32[]{:S(2)}, u32[]{:S(2)}) collective-permute-start(s16[240,256]{1,0:T(8,128)(2,1)} %pad_add_fusion.12), channel_id=1, source_target_pairs={{0,2},{1,3},{2,0},{3,1},{4,6},{5,7},{6,4},{7,5},{8,10},{9,11},{10,... | collective-permute-start | bytes 368648 | tf_op jit(solution)/shard_map/ppermute | solution.py:81
  252.8 26.5 %all-to-all-start.1 = ((s16[4,176,512]{2,1,0:T(8,128)(2,1)}), s16[4,176,512]{2,1,0:T(8,128)(2,1)S(1)}, u32[]{:S(2)}, u32[]{:S(2)}) async-start(s16[4,176,512]{2,1,0:T(8,128)(2,1)} %pad_add_fusion.1), calls=%async_computation.1 | async-start | bytes 1441792 | tf_op jit(solution)/shard_map/all_to_all | solution.py:895
  279.3 25.8 %all-to-all-start = ((s16[4,232,512]{2,1,0:T(8,128)(2,1)}), s16[4,232,512]{2,1,0:T(8,128)(2,1)S(1)}, u32[]{:S(2)}, u32[]{:S(2)}) async-start(s16[4,232,512]{2,1,0:T(8,128)(2,1)} %pad_add_fusion), calls=%async_computation | async-start | bytes 1900544 | tf_op jit(solution)/shard_map/all_to_all | solution.py:895
  309.1 25.1 %all-to-all-start.2 = ((s16[32,80,128]{2,1,0:T(8,128)(2,1)}), s16[32,80,128]{2,1,0:T(8,128)(2,1)S(1)}, u32[]{:S(2)}, u32[]{:S(2)}) async-start(s16[32,80,128]{2,1,0:T(8,128)(2,1)} %route.1), calls=%async_computation.2 | async-start | bytes 1310720 | tf_op jit(solution)/shard_map/all_to_all | solution.py:1156
  344.2 13.6 %collective-permute-start.38 = (bf16[2,512,256]{2,1,0:T(8,128)(2,1)}, bf16[2,512,256]{2,1,0:T(8,128)(2,1)S(1)}, u32[]{:S(2)}, u32[]{:S(2)}) collective-permute-start(bf16[2,512,256]{2,1,0:T(8,128)(2,1)} %get-tuple-element.94), channel_id=1, source_target_pairs={{0,8},{1,9},{2,10},{3,11},{4,12},{5,13},{6,14},{7,15},{8,0},{9,1},... | collective-permute-start | bytes 1572872 | tf_op jit(solution)/shard_map/ppermute | solution.py:81
  346.3 14.9 %collective-permute-start.42 = (bf16[2,512,256]{2,1,0:T(8,128)(2,1)}, bf16[2,512,256]{2,1,0:T(8,128)(2,1)S(1)}, u32[]{:S(2)}, u32[]{:S(2)}) collective-permute-start(bf16[2,512,256]{2,1,0:T(8,128)(2,1)} %get-tuple-element.94), channel_id=1, source_target_pairs={{8,16},{9,17},{10,18},{11,19},{12,20},{13,21},{14,22},{15,23},{16,... | collective-permute-start | bytes 1572872 | tf_op jit(solution)/shard_map/ppermute | solution.py:81
  360.0 16.6 %collective-permute-start.39 = (bf16[2,512,256]{2,1,0:T(8,128)(2,1)}, bf16[2,512,256]{2,1,0:T(8,128)(2,1)S(1)}, u32[]{:S(2)}, u32[]{:S(2)}) collective-permute-start(bf16[2,512,256]{2,1,0:T(8,128)(2,1)} %get-tuple-element.94), channel_id=1, source_target_pairs={{0,2},{1,3},{2,0},{3,1},{4,6},{5,7},{6,4},{7,5},{8,10},{9,11},{10,... | collective-permute-start | bytes 1572872 | tf_op jit(solution)/shard_map/ppermute | solution.py:81
  361.2 15.3 %collective-permute-start.43 = (bf16[2,512,256]{2,1,0:T(8,128)(2,1)S(1)}, bf16[2,512,256]{2,1,0:T(8,128)(2,1)S(1)}, u32[]{:S(2)}, u32[]{:S(2)}) collective-permute-start(bf16[2,512,256]{2,1,0:T(8,128)(2,1)S(1)} %collective-permute-done.42), channel_id=1, source_target_pairs={{8,0},{9,1},{10,2},{11,3},{12,4},{13,5},{14,6},{15,7},{16,24},{17,... | collective-permute-start | bytes 1572872 | tf_op jit(solution)/shard_map/ppermute | solution.py:81
  365.1 21.2 %collective-permute-start.46 = (bf16[2,512,256]{2,1,0:T(8,128)(2,1)S(1)}, bf16[2,512,256]{2,1,0:T(8,128)(2,1)S(1)}, u32[]{:S(2)}, u32[]{:S(2)}) collective-permute-start(bf16[2,512,256]{2,1,0:T(8,128)(2,1)S(1)} %collective-permute-done.38), channel_id=1, source_target_pairs={{0,2},{1,3},{2,0},{3,1},{4,6},{5,7},{6,4},{7,5},{8,10},{9,11},{10,... | collective-permute-start | bytes 1572872 | tf_op jit(solution)/shard_map/ppermute | solution.py:81
  365.9 20.9 %collective-permute-start.44 = (bf16[2,512,256]{2,1,0:T(8,128)(2,1)S(1)}, bf16[2,512,256]{2,1,0:T(8,128)(2,1)S(1)}, u32[]{:S(2)}, u32[]{:S(2)}) collective-permute-start(bf16[2,512,256]{2,1,0:T(8,128)(2,1)S(1)} %collective-permute-done.41), channel_id=1, source_target_pairs={{8,0},{9,1},{10,2},{11,3},{12,4},{13,5},{14,6},{15,7},{16,24},{17,... | collective-permute-start | bytes 1572872 | tf_op jit(solution)/shard_map/ppermute | solution.py:81
  371.0 17.3 %collective-permute-start.47 = (bf16[2,512,256]{2,1,0:T(8,128)(2,1)S(1)}, bf16[2,512,256]{2,1,0:T(8,128)(2,1)S(1)}, u32[]{:S(2)}, u32[]{:S(2)}) collective-permute-start(bf16[2,512,256]{2,1,0:T(8,128)(2,1)S(1)} %collective-permute-done.38), channel_id=1, source_target_pairs={{0,4},{1,5},{2,6},{3,7},{4,0},{5,1},{6,2},{7,3},{8,12},{9,13},{10,... | collective-permute-start | bytes 1572872 | tf_op jit(solution)/shard_map/ppermute | solution.py:81
  376.5 34.3 %collective-permute-start.45 = (bf16[2,512,256]{2,1,0:T(8,128)(2,1)S(1)}, bf16[2,512,256]{2,1,0:T(8,128)(2,1)S(1)}, u32[]{:S(2)}, u32[]{:S(2)}) collective-permute-start(bf16[2,512,256]{2,1,0:T(8,128)(2,1)S(1)} %collective-permute-done.40), channel_id=1, source_target_pairs={{0,2},{1,3},{2,0},{3,1},{4,6},{5,7},{6,4},{7,5},{8,10},{9,11},{10,... | collective-permute-start | bytes 1572872 | tf_op jit(solution)/shard_map/ppermute | solution.py:81
  376.6 32.2 %collective-permute-start.48 = (bf16[2,512,256]{2,1,0:T(8,128)(2,1)S(1)}, bf16[2,512,256]{2,1,0:T(8,128)(2,1)S(1)}, u32[]{:S(2)}, u32[]{:S(2)}) collective-permute-start(bf16[2,512,256]{2,1,0:T(8,128)(2,1)S(1)} %broadcast_select_fusion.1), channel_id=1, source_target_pairs={{0,2},{1,3},{2,0},{3,1},{4,6},{5,7},{6,4},{7,5},{8,10},{9,11},{10,... | collective-permute-start | bytes 1572872 | tf_op jit(solution)/shard_map/ppermute | solution.py:81
  386.3 22.5 %collective-permute-start.49 = (bf16[2,512,256]{2,1,0:T(8,128)(2,1)S(1)}, bf16[2,512,256]{2,1,0:T(8,128)(2,1)S(1)}, u32[]{:S(2)}, u32[]{:S(2)}) collective-permute-start(bf16[2,512,256]{2,1,0:T(8,128)(2,1)S(1)} %broadcast_select_fusion.1), channel_id=1, source_target_pairs={{0,4},{1,5},{2,6},{3,7},{4,0},{5,1},{6,2},{7,3},{8,12},{9,13},{10,... | collective-permute-start | bytes 1572872 | tf_op jit(solution)/shard_map/ppermute | solution.py:81
  386.8 22.6 %collective-permute-start.50 = (bf16[2,512,256]{2,1,0:T(8,128)(2,1)S(1)}, bf16[2,512,256]{2,1,0:T(8,128)(2,1)S(1)}, u32[]{:S(2)}, u32[]{:S(2)}) collective-permute-start(bf16[2,512,256]{2,1,0:T(8,128)(2,1)S(1)} %collective-permute-done.46), channel_id=1, source_target_pairs={{0,4},{1,5},{2,6},{3,7},{4,0},{5,1},{6,2},{7,3},{8,12},{9,13},{10,... | collective-permute-start | bytes 1572872 | tf_op jit(solution)/shard_map/ppermute | solution.py:81
  388.4 31.6 %collective-permute-start.51 = (bf16[2,512,256]{2,1,0:T(8,128)(2,1)S(1)}, bf16[2,512,256]{2,1,0:T(8,128)(2,1)S(1)}, u32[]{:S(2)}, u32[]{:S(2)}) collective-permute-start(bf16[2,512,256]{2,1,0:T(8,128)(2,1)S(1)} %broadcast_select_fusion), channel_id=1, source_target_pairs={{0,2},{1,3},{2,0},{3,1},{4,6},{5,7},{6,4},{7,5},{8,10},{9,11},{10,... | collective-permute-start | bytes 1572872 | tf_op jit(solution)/shard_map/ppermute | solution.py:81
  408.8 29.3 %collective-permute-start.55 = (bf16[8,512,256]{2,1,0:T(8,128)(2,1)S(1)}, bf16[8,512,256]{2,1,0:T(8,128)(2,1)S(1)}, u32[]{:S(2)}, u32[]{:S(2)}) collective-permute-start(bf16[8,512,256]{2,1,0:T(8,128)(2,1)S(1)} %constant_dynamic-update-slice_fusion.4.refs_2_), channel_id=1, source_target_pairs={{0,1},{1,0},{2,3},{3,2},{4,5},{5,4},{6,7},{7,6},{8,9},{9,8},{10,11... | collective-permute-start | bytes 6291464 | tf_op jit(solution)/shard_map/ppermute | solution.py:81
  408.8 14.8 %collective-permute-start.52 = (bf16[2,512,256]{2,1,0:T(8,128)(2,1)S(1)}, bf16[2,512,256]{2,1,0:T(8,128)(2,1)S(1)}, u32[]{:S(2)}, u32[]{:S(2)}) collective-permute-start(bf16[2,512,256]{2,1,0:T(8,128)(2,1)S(1)} %broadcast_select_fusion), channel_id=1, source_target_pairs={{0,4},{1,5},{2,6},{3,7},{4,0},{5,1},{6,2},{7,3},{8,12},{9,13},{10,... | collective-permute-start | bytes 1572872 | tf_op jit(solution)/shard_map/ppermute | solution.py:81
  409.5 18.3 %collective-permute-start.53 = (bf16[2,512,256]{2,1,0:T(8,128)(2,1)S(1)}, bf16[2,512,256]{2,1,0:T(8,128)(2,1)S(1)}, u32[]{:S(2)}, u32[]{:S(2)}) collective-permute-start(bf16[2,512,256]{2,1,0:T(8,128)(2,1)S(1)} %collective-permute-done.49), channel_id=1, source_target_pairs={{0,2},{1,3},{2,0},{3,1},{4,6},{5,7},{6,4},{7,5},{8,10},{9,11},{10,... | collective-permute-start | bytes 1572872 | tf_op jit(solution)/shard_map/ppermute | solution.py:81
  410.8 27.3 %collective-permute-start.57 = (bf16[8,512,256]{2,1,0:T(8,128)(2,1)S(1)}, bf16[8,512,256]{2,1,0:T(8,128)(2,1)S(1)}, u32[]{:S(2)}, u32[]{:S(2)}) collective-permute-start(bf16[8,512,256]{2,1,0:T(8,128)(2,1)S(1)} %constant_dynamic-update-slice_fusion.8.refs_4_), channel_id=1, source_target_pairs={{0,1},{1,0},{2,3},{3,2},{4,5},{5,4},{6,7},{7,6},{8,9},{9,8},{10,11... | collective-permute-start | bytes 6291464 | tf_op jit(solution)/shard_map/ppermute | solution.py:81
  420.0 14.5 %collective-permute-start.54 = (bf16[2,512,256]{2,1,0:T(8,128)(2,1)S(1)}, bf16[2,512,256]{2,1,0:T(8,128)(2,1)S(1)}, u32[]{:S(2)}, u32[]{:S(2)}) collective-permute-start(bf16[2,512,256]{2,1,0:T(8,128)(2,1)S(1)} %collective-permute-done.51), channel_id=1, source_target_pairs={{0,4},{1,5},{2,6},{3,7},{4,0},{5,1},{6,2},{7,3},{8,12},{9,13},{10,... | collective-permute-start | bytes 1572872 | tf_op jit(solution)/shard_map/ppermute | solution.py:81
  423.6 14.5 %collective-permute-start.56 = (bf16[8,512,256]{2,1,0:T(8,128)(2,1)S(1)}, bf16[8,512,256]{2,1,0:T(8,128)(2,1)S(1)}, u32[]{:S(2)}, u32[]{:S(2)}) collective-permute-start(bf16[8,512,256]{2,1,0:T(8,128)(2,1)S(1)} %pad_maximum_fusion.refs_3_), channel_id=1, source_target_pairs={{0,1},{1,0},{2,3},{3,2},{4,5},{5,4},{6,7},{7,6},{8,9},{9,8},{10,11... | collective-permute-start | bytes 6291464 | tf_op jit(solution)/shard_map/ppermute | solution.py:81
  (53 other events, 396.1 us)
